TPU v7x, 32 devices: a whole 2x2x4 slice. The times are simulated.
32 devices in a mesh: section: 2 (over core), task: 4 (over y, x), fsdp: 4 (over z).
Axes of the slice: x: 2, y: 2, z: 4, core: 2. Of those that a mesh axis runs over, the one named last changes fastest.
Arguments:
- states: bfloat16 [4, 192, 2048], P('task', 'fsdp'), may hold values from -6 to 6
- task_weights: bfloat16 [4, 2, 2, 2048, 5120], P('task', 'section', None, None, 'fsdp'), may hold values from -0.125 to 0.125
- pad_mask: int32 [4, 192], P('task', 'fsdp'), may hold values 0 or 1
- direction: float32 [2, 2048, 2, 5120], P('section', ('task', 'fsdp')), may hold values from -0.125 to 0.125
- residual: float32 [2, 2048, 2, 5120], P('section', ('task', 'fsdp')), may hold values from -6 to 6
Outputs:
- residual_next: float32 [2, 2048, 2, 5120], P('section', ('task', 'fsdp'))
- direction_next: float32 [2, 2048, 2, 5120], P('section', ('task', 'fsdp'))
- step_size: float32 [], replicated
All inputs are finite; a program needn't handle non-finite values. No bound on the sum of `pad_mask` on one device may be relied on, other than what follows from the above.
Results may differ from a plain program's by a relative error of at most 0.0052.
Values may be sent and summed in bfloat16 or wider, within the bound.
No kernel may reach another device: no remote copies, remote signals or barrier semaphores. Data moves between devices by JAX's collectives and lax.ppermute only.
A program may use at most 192 MiB of HBM per device.

v0:
```python
import jax
import jax.numpy as jnp
from jax import lax
from jax.sharding import PartitionSpec as P

MICRO = 4


eps_norm = 1e-06


def from_behind(array, axis, by):
    count = lax.axis_size(axis)
    pairs = [(i, i + by) for i in range(count) if 0 <= i + by < count]
    return lax.ppermute(array, axis, pairs)


def normalize(token_rows):
    return token_rows * lax.rsqrt(
        jnp.mean(token_rows * token_rows, axis=-1, keepdims=True) + eps_norm
    )


def gelu_tanh(values):
    return jax.nn.gelu(values, approximate=True)


def across_hidden(left_side, right_side):
    return lax.dot_general(
        left_side, right_side, (((1,), (1,)), ((), ())), preferred_element_type=jnp.float32
    )


def across_tokens(left_side, right_side):
    return lax.dot_general(
        left_side, right_side, (((0,), (0,)), ((), ())), preferred_element_type=jnp.float32
    )


def put_slot(buffer, new_entry, index_at, active):
    previous = lax.dynamic_index_in_dim(buffer, index_at, 0, keepdims=False)
    return lax.dynamic_update_index_in_dim(
        buffer, jnp.where(active, new_entry, previous), index_at, 0
    )


def on_device(states, task_weights, pad_mask, direction, residual):
    segments = lax.axis_size("section")
    segment_id = lax.axis_index("section")
    is_first = segment_id == 0
    is_last = segment_id == segments - 1
    w_in = task_weights[0, 0, 0]
    w_out = task_weights[0, 0, 1]
    local_rows = states[0]
    keep_mask = pad_mask[0]
    model_width = local_rows.shape[1]
    block_rows = local_rows.shape[0] // MICRO
    hidden_dev = w_in.shape[1]
    joined = block_rows * lax.axis_size("fsdp")
    resid_local = residual[0]
    direc_local = direction[0]
    start_norm = lax.psum(jnp.sum(resid_local * resid_local), ("section", "task", "fsdp"))
    spread = lax.all_to_all(
        direc_local.astype(jnp.bfloat16), "fsdp", split_axis=2, concat_axis=0, tiled=True
    )
    steering = lax.all_gather(spread, "task", axis=0, tiled=True)
    steer_in = steering[:, 0, :]
    steer_out = steering[:, 1, :]
    store_x = jnp.zeros((MICRO, block_rows, model_width), jnp.bfloat16)
    store_n = jnp.zeros((MICRO, joined, model_width), jnp.bfloat16)
    store_h = jnp.zeros((MICRO, joined, hidden_dev), jnp.bfloat16)
    store_s = jnp.zeros((MICRO, joined, hidden_dev), jnp.float32)
    store_c = jnp.zeros((MICRO, block_rows, model_width), jnp.bfloat16)
    empty_rows = jnp.zeros((block_rows, model_width), jnp.bfloat16)
    incoming = (empty_rows, empty_rows)
    step_count = segments + MICRO - 1
    for moment in range(step_count):
        slot_raw = moment - segment_id
        active = (slot_raw >= 0) & (slot_raw < MICRO)
        slot_index = jnp.clip(slot_raw, 0, MICRO - 1)
        if moment < MICRO:
            fresh_rows = local_rows[moment * block_rows : (moment + 1) * block_rows]
        else:
            fresh_rows = empty_rows
        segment_in = jnp.where(is_first, fresh_rows, incoming[0])
        segment_dot = jnp.where(is_first, empty_rows, incoming[1])
        gathered, gathered_dot = (
            lax.all_gather(segment_in, "fsdp", axis=0, tiled=True),
            lax.all_gather(segment_dot, "fsdp", axis=0, tiled=True),
        )
        normed, normed_dot = jax.jvp(
            normalize, (gathered.astype(jnp.float32),), (gathered_dot.astype(jnp.float32),)
        )
        normed_b = normed.astype(jnp.bfloat16)
        normed_dot_b = normed_dot.astype(jnp.bfloat16)
        preact = jnp.dot(normed_b, w_in, preferred_element_type=jnp.float32)
        preact_dot = jnp.dot(normed_dot_b, w_in, preferred_element_type=jnp.float32) + jnp.dot(
            normed_b, steer_in, preferred_element_type=jnp.float32
        )
        hidden, slope_vals = jax.jvp(gelu_tanh, (preact,), (jnp.ones_like(preact),))
        hidden_b = hidden.astype(jnp.bfloat16)
        hidden_dot_b = (slope_vals * preact_dot).astype(jnp.bfloat16)
        part_out = across_hidden(hidden_b, w_out)
        part_dot = across_hidden(hidden_dot_b, w_out) + across_hidden(hidden_b, steer_out)
        mixed_out, mixed_dot = (
            lax.psum_scatter(part_out, "fsdp", scatter_dimension=0, tiled=True),
            lax.psum_scatter(part_dot, "fsdp", scatter_dimension=0, tiled=True),
        )
        segment_out = (segment_in.astype(jnp.float32) + mixed_out).astype(jnp.bfloat16)
        segment_out_dot = (segment_dot.astype(jnp.float32) + mixed_dot).astype(jnp.bfloat16)
        store_x = put_slot(store_x, segment_in, slot_index, active)
        store_n = put_slot(store_n, normed_b, slot_index, active)
        store_h = put_slot(store_h, hidden_b, slot_index, active)
        store_s = put_slot(store_s, slope_vals, slot_index, active)
        keep_rows = lax.dynamic_slice_in_dim(keep_mask, slot_index * block_rows, block_rows, 0)
        masked_top = segment_out_dot * keep_rows[:, None].astype(jnp.bfloat16)
        store_c = put_slot(store_c, masked_top, slot_index, active & is_last)
        if moment + 1 < step_count:
            incoming = from_behind((segment_out, segment_out_dot), "section", 1)
    store_u = jnp.zeros((MICRO, joined, model_width), jnp.bfloat16)
    store_a = jnp.zeros((MICRO, joined, hidden_dev), jnp.bfloat16)
    incoming_back = empty_rows
    for moment in range(step_count):
        slot_raw = moment - (segments - 1 - segment_id)
        active = (slot_raw >= 0) & (slot_raw < MICRO)
        slot_index = jnp.clip(slot_raw, 0, MICRO - 1)
        top_rows = lax.dynamic_index_in_dim(store_c, slot_index, 0, keepdims=False)
        cot_in = jnp.where(is_last, top_rows, incoming_back)
        cot_rows = lax.all_gather(cot_in, "fsdp", axis=0, tiled=True)
        slope_vals = lax.dynamic_index_in_dim(store_s, slot_index, 0, keepdims=False)
        hidden_bar = jnp.dot(cot_rows, w_out, preferred_element_type=jnp.float32)
        preact_bar = (hidden_bar * slope_vals).astype(jnp.bfloat16)
        normed_bar = lax.psum_scatter(
            across_hidden(preact_bar, w_in), "fsdp", scatter_dimension=0, tiled=True
        )
        segment_in = lax.dynamic_index_in_dim(store_x, slot_index, 0, keepdims=False)
        pullback = jax.vjp(normalize, segment_in.astype(jnp.float32))[1]
        cot_next = (cot_in.astype(jnp.float32) + pullback(normed_bar)[0]).astype(jnp.bfloat16)
        store_u = put_slot(store_u, cot_rows, slot_index, active)
        store_a = put_slot(store_a, preact_bar, slot_index, active)
        if moment + 1 < step_count:
            incoming_back = from_behind(cot_next, "section", -1)
    flat_n = store_n.reshape(MICRO * joined, model_width)
    flat_u = store_u.reshape(MICRO * joined, model_width)
    flat_a = store_a.reshape(MICRO * joined, hidden_dev)
    flat_h = store_h.reshape(MICRO * joined, hidden_dev)
    summed = lax.psum_scatter(
        jnp.stack([across_tokens(flat_n, flat_a), across_tokens(flat_u, flat_h)], axis=1),
        "task",
        scatter_dimension=0,
        tiled=True,
    )
    product = lax.all_to_all(summed, "fsdp", split_axis=0, concat_axis=2, tiled=True)
    curvature = lax.psum(jnp.sum(direc_local * product), ("section", "task", "fsdp"))
    step_size = start_norm / curvature
    resid_next = resid_local - step_size * product
    next_norm = lax.psum(jnp.sum(resid_next * resid_next), ("section", "task", "fsdp"))
    direc_next = resid_next + next_norm / start_norm * direc_local
    return (resid_next[None], direc_next[None], step_size)


def solution(mesh):
    placed = (
        P("task", "fsdp", None),
        P("task", "section", None, None, "fsdp"),
        P("task", "fsdp"),
        P("section", ("task", "fsdp"), None, None),
        P("section", ("task", "fsdp"), None, None),
    )
    return jax.shard_map(
        on_device,
        mesh=mesh,
        in_specs=placed,
        out_specs=(
            P("section", ("task", "fsdp"), None, None),
            P("section", ("task", "fsdp"), None, None),
            P(),
        ),
        check_vma=False,
    )
```

profile of v0, /device:TPU:0, one launch (start us, length us, event | category | flops | bytes accessed | tf_op | source)
XLA Modules:
  0.0 1301.8 jit_solution(14234534665451937717)
XLA Ops:
  18.7 22.2 %copy.56 = bf16[128,2,5120]{0,1,2:T(2,128)(2,1)S(1)} copy(bf16[128,2,5120]{0,2,1:T(8,128)(2,1)S(1)} %bitcast_convert_fusion) | data formatting | bytes 5242880 | tf_op jit(solution)/shard_map/convert_element_type | solution.py:64
  41.0 65.6 %all_to_all.36 = bf16[128,2,5120]{0,1,2:T(2,128)(2,1)S(1)} all-to-all(bf16[128,2,5120]{0,1,2:T(2,128)(2,1)S(1)} %copy.56), channel_id=1, replica_groups=mesh['section'=2,'task'=4,'fsdp'=4] {'fsdp'}, dimensions={2} | all-to-all | bytes 5242880 | tf_op jit(solution)/shard_map/all_to_all | solution.py:63
  113.3 15.1 %all-gather = bf16[1,48,2048]{2,0,1:T(2,128)(2,1)S(1)} all-gather(bf16[1,12,2048]{2,0,1:T(2,128)(2,1)S(1)} %get-tuple-element.67), channel_id=2, replica_groups=mesh['section'=2,'task'=4,'fsdp'=4] {'fsdp'}, dimensions={1}, use_global_device_ids=true | all-gather | bytes 245760 | tf_op jit(solution)/shard_map/all_gather | solution.py:88
  145.0 72.4 %all-gather.16.cloned.1.call-done = bf16[2048,2,1280]{2,0,1:T(8,128)(2,1)} async-done(((bf16[512,2,1280]{2,0,1:T(8,128)(2,1)}), bf16[2048,2,1280]{2,0,1:T(8,128)(2,1)}) %all-gather.16.cloned.1.call-update) | async-done | bytes 10485776 | tf_op jit(solution)/shard_map/all_gather | solution.py:66
  229.3 24.3 %fusion.310 = (f32[16,2048]{1,0:T(8,128)S(1)}, f32[16,2048]{1,0:T(8,128)S(1)}) fusion(f32[48,2048]{1,0:T(8,128)S(1)} %fusion.109, f32[48,2048]{1,0:T(8,128)S(1)} %copy-done.15), kind=kCustom, calls=%all-reduce-scatter.16 | all-reduce-scatter fusion | flops 262145 | bytes 1049088
  263.3 14.7 %all-gather.6 = bf16[4,12,2048]{2,1,0:T(8,128)(2,1)S(1)} all-gather(bf16[1,12,2048]{2,1,0:T(8,128)(2,1)S(1)} %fusion.244), channel_id=1, replica_groups=mesh['section'=2,'task'=4,'fsdp'=4] {'fsdp'}, dimensions={0}, use_global_device_ids=true | all-gather | bytes 245760 | tf_op jit(solution)/shard_map/all_gather | solution.py:89
  279.1 14.0 %all-gather.2 = bf16[4,12,2048]{2,1,0:T(8,128)(2,1)S(1)} all-gather(bf16[1,12,2048]{2,1,0:T(8,128)(2,1)S(1)} %bitcast.567), channel_id=1, replica_groups=mesh['section'=2,'task'=4,'fsdp'=4] {'fsdp'}, dimensions={0}, use_global_device_ids=true | all-gather | bytes 245760 | tf_op jit(solution)/shard_map/all_gather | solution.py:88
  317.0 18.1 %fusion.309 = (f32[16,2048]{1,0:T(8,128)S(1)}, f32[16,2048]{1,0:T(8,128)S(1)}) fusion(f32[48,2048]{1,0:T(8,128)S(1)} %fusion.110, f32[48,2048]{1,0:T(8,128)S(1)} %fusion.41), kind=kCustom, calls=%all-reduce-scatter.15 | all-reduce-scatter fusion | flops 262145 | bytes 1049088
  400.6 18.1 %fusion.308 = (f32[16,2048]{1,0:T(8,128)S(1)}, f32[16,2048]{1,0:T(8,128)S(1)}) fusion(f32[48,2048]{1,0:T(8,128)S(1)} %fusion.111, f32[48,2048]{1,0:T(8,128)S(1)} %fusion.39), kind=kCustom, calls=%all-reduce-scatter.14 | all-reduce-scatter fusion | flops 262145 | bytes 1049088
  444.6 14.5 %all-gather.4 = bf16[4,12,2048]{2,1,0:T(8,128)(2,1)} all-gather(bf16[1,12,2048]{2,1,0:T(8,128)(2,1)S(1)} %bitcast.566), channel_id=1, replica_groups=mesh['section'=2,'task'=4,'fsdp'=4] {'fsdp'}, dimensions={0}, use_global_device_ids=true | all-gather | bytes 245760 | tf_op jit(solution)/shard_map/all_gather | solution.py:88
  460.1 14.5 %all-gather.8 = bf16[4,12,2048]{2,1,0:T(8,128)(2,1)} all-gather(bf16[1,12,2048]{2,1,0:T(8,128)(2,1)S(1)} %fusion.246), channel_id=1, replica_groups=mesh['section'=2,'task'=4,'fsdp'=4] {'fsdp'}, dimensions={0}, use_global_device_ids=true | all-gather | bytes 245760 | tf_op jit(solution)/shard_map/all_gather | solution.py:89
  499.8 18.7 %fusion.307 = (f32[16,2048]{1,0:T(8,128)S(1)}, f32[16,2048]{1,0:T(8,128)S(1)}) fusion(f32[48,2048]{1,0:T(8,128)S(1)} %fusion.112, f32[48,2048]{1,0:T(8,128)S(1)} %fusion.37), kind=kCustom, calls=%all-reduce-scatter.13 | all-reduce-scatter fusion | flops 262145 | bytes 1049088
  528.6 14.1 %all-gather.5 = bf16[4,12,2048]{2,1,0:T(8,128)(2,1)S(1)} all-gather(bf16[1,12,2048]{2,1,0:T(8,128)(2,1)S(1)} %fusion.243), channel_id=1, replica_groups=mesh['section'=2,'task'=4,'fsdp'=4] {'fsdp'}, dimensions={0}, use_global_device_ids=true | all-gather | bytes 245760 | tf_op jit(solution)/shard_map/all_gather | solution.py:88
  576.2 17.4 %fusion.8 = f32[16,2048]{1,0:T(8,128)S(1)} fusion(f32[48,2048]{1,0:T(8,128)S(1)} %fusion.113), kind=kCustom, calls=%all-reduce-scatter.8 | all-reduce-scatter fusion | flops 131073 | bytes 524800
  599.3 14.2 %all-gather.1 = bf16[1,48,2048]{2,0,1:T(2,128)(2,1)S(1)} all-gather(bf16[1,12,2048]{2,0,1:T(2,128)(2,1)S(1)} %get-tuple-element.65), channel_id=3, replica_groups=mesh['section'=2,'task'=4,'fsdp'=4] {'fsdp'}, dimensions={1}, use_global_device_ids=true | all-gather | bytes 245760 | tf_op jit(solution)/shard_map/all_gather | solution.py:129
  621.3 16.0 %fusion.9 = f32[16,2048]{1,0:T(8,128)S(1)} fusion(f32[48,2048]{1,0:T(8,128)S(1)} %fusion.51), kind=kCustom, calls=%all-reduce-scatter.9 | all-reduce-scatter fusion | flops 131073 | bytes 524800
  672.0 18.2 %fusion.10 = f32[16,2048]{1,0:T(8,128)S(1)} fusion(f32[48,2048]{1,0:T(8,128)} %fusion.49), kind=kCustom, calls=%all-reduce-scatter.10 | all-reduce-scatter fusion | flops 131073 | bytes 524800
  723.1 18.1 %fusion.11 = f32[16,2048]{1,0:T(8,128)S(1)} fusion(f32[48,2048]{1,0:T(8,128)} %fusion.47), kind=kCustom, calls=%all-reduce-scatter.11 | all-reduce-scatter fusion | flops 131073 | bytes 524800
  774.1 18.2 %fusion.12 = f32[16,2048]{1,0:T(8,128)S(1)} fusion(f32[48,2048]{1,0:T(8,128)} %fusion.45), kind=kCustom, calls=%all-reduce-scatter.12 | all-reduce-scatter fusion | flops 131073 | bytes 524800
  801.5 14.1 %all-gather.13 = bf16[4,12,2048]{2,1,0:T(8,128)(2,1)S(1)} all-gather(bf16[1,12,2048]{2,1,0:T(8,128)(2,1)S(1)} %fusion.242), channel_id=1, replica_groups=mesh['section'=2,'task'=4,'fsdp'=4] {'fsdp'}, dimensions={0}, use_global_device_ids=true | all-gather | bytes 245760 | tf_op jit(solution)/shard_map/all_gather | solution.py:129
  830.0 188.3 %reduce-scatter.28.cloned.1.call-done = f32[512,2,1280]{2,0,1:T(8,128)} async-done(((f32[2048,2,1280]{2,0,1:T(8,128)}), f32[512,2,1280]{2,0,1:T(8,128)}) %reduce-scatter.28.cloned.1.call-update) | async-done | bytes 5242896 | tf_op jit(solution)/shard_map/reduce_scatter | solution.py:147
  1041.1 107.1 %all-to-all-done.1 = f32[512,2,1280]{2,1,0:T(2,128)} async-done(((f32[512,2,1280]{2,1,0:T(2,128)}), f32[512,2,1280]{2,1,0:T(2,128)}, u32[]{:S(2)}, u32[]{:S(2)}) %all-to-all-start.1) | async-done | bytes 5242912 | tf_op jit(solution)/shard_map/all_to_all | solution.py:153
  1166.9 37.3 %all-reduce.26 = (f32[]{:T(128)}, f32[]{:T(128)}) all-reduce(f32[]{:T(128)} %get-tuple-element.111, f32[]{:T(128)} %get-tuple-element.110), channel_id=1, replica_groups=mesh['section'=2,'task'=4,'fsdp'=4] {'section','task','fsdp'}, use_global_device_ids=true, to_apply=%region_1.0 | all-reduce | flops 2 | bytes 16 | tf_op jit(solution)/shard_map/psum | solution.py:62
  1221.8 42.6 %psum.23 = f32[]{:T(128)} all-reduce(f32[]{:T(128)} %fusion.16), channel_id=1, replica_groups=mesh['section'=2,'task'=4,'fsdp'=4] {'section','task','fsdp'}, use_global_device_ids=true, to_apply=%region_37.38 | all-reduce | flops 1 | bytes 8 | tf_op jit(solution)/shard_map/psum | solution.py:157
  (348 shorter events, 464.1 us)
Async XLA Ops:
  7.2 210.3 %all-gather.16.cloned.1.call-start = ((), (), s32[]{:S(2)}) async-start(), calls=%async_computation.3 | async-start | bytes 13107200 | tf_op jit(solution)/shard_map/all_gather | solution.py:66
  113.0 905.3 %reduce-scatter.28.cloned.1.call-start = ((), (), s32[]{:S(2)}) async-start(), calls=%async_computation.4 | async-start | bytes 26214400 | tf_op jit(solution)/shard_map/reduce_scatter | solution.py:147
  253.6 5.6 collective-permute-start.16
  257.3 4.4 collective-permute-start.12
  259.6 3.7 collective-permute-start.4
  262.0 16.1 %collective-permute-start = (bf16[12,2048]{1,0:T(8,128)(2,1)S(1)}, bf16[12,2048]{1,0:T(8,128)(2,1)S(1)}, u32[]{:S(2)}, u32[]{:S(2)}) collective-permute-start(bf16[12,2048]{1,0:T(8,128)(2,1)S(1)} %fusion.236), channel_id=1, source_target_pairs={{0,16},{1,17},{2,18},{3,19},{4,20},{5,21},{6,22},{7,23},{8,24},{9,... | collective-permute-start | bytes 147464 | tf_op jit(solution)/shard_map/ppermute | solution.py:15
  335.1 9.1 collective-permute-start.13
  338.3 7.4 collective-permute-start.17
  344.4 4.1 collective-permute-start.1
  346.6 15.9 %collective-permute-start.5 = (bf16[12,2048]{1,0:T(8,128)(2,1)}, bf16[12,2048]{1,0:T(8,128)(2,1)S(1)}, u32[]{:S(2)}, u32[]{:S(2)}) collective-permute-start(bf16[12,2048]{1,0:T(8,128)(2,1)} %get-tuple-element.60), channel_id=1, source_target_pairs={{0,16},{1,17},{2,18},{3,19},{4,20},{5,21},{6,22},{7,23},{8,24},{9,... | collective-permute-start | bytes 147464 | tf_op jit(solution)/shard_map/ppermute | solution.py:15
  418.7 12.6 collective-permute-start.14
  423.2 14.7 %collective-permute-start.18 = (f32[12,2048]{1,0:T(8,128)}, f32[12,2048]{1,0:T(8,128)}, u32[]{:S(2)}, u32[]{:S(2)}) collective-permute-start(f32[12,2048]{1,0:T(8,128)} %slice.53), channel_id=1, source_target_pairs={{0,1},{1,2},{2,3},{4,5},{5,6},{6,7},{8,9},{9,10},{10,11},{12,13},{... | collective-permute-start | bytes 294920
  436.0 7.1 collective-permute-start.2
  440.5 19.6 %collective-permute-start.6 = (bf16[12,2048]{1,0:T(8,128)(2,1)}, bf16[12,2048]{1,0:T(8,128)(2,1)}, u32[]{:S(2)}, u32[]{:S(2)}) collective-permute-start(bf16[12,2048]{1,0:T(8,128)(2,1)} %get-tuple-element.58), channel_id=1, source_target_pairs={{0,16},{1,17},{2,18},{3,19},{4,20},{5,21},{6,22},{7,23},{8,24},{9,... | collective-permute-start | bytes 147464 | tf_op jit(solution)/shard_map/ppermute | solution.py:15
  518.5 5.9 collective-permute-start.15
  520.0 6.1 collective-permute-start.19
  524.7 3.8 collective-permute-start.3
  527.2 15.5 %collective-permute-start.7 = (bf16[12,2048]{1,0:T(8,128)(2,1)S(1)}, bf16[12,2048]{1,0:T(8,128)(2,1)S(1)}, u32[]{:S(2)}, u32[]{:S(2)}) collective-permute-start(bf16[12,2048]{1,0:T(8,128)(2,1)S(1)} %get-tuple-element.56), channel_id=1, source_target_pairs={{0,16},{1,17},{2,18},{3,19},{4,20},{5,21},{6,22},{7,23},{8,24},{9,... | collective-permute-start | bytes 147464 | tf_op jit(solution)/shard_map/ppermute | solution.py:15
  593.7 4.6 collective-permute-start.20
  638.0 3.9 collective-permute-start.21
  690.2 3.8 collective-permute-start.22
  741.2 3.8 collective-permute-start.23
  792.3 3.8 collective-permute-start.24
  1027.2 121.0 %all-to-all-start.1 = ((f32[512,2,1280]{2,1,0:T(2,128)}), f32[512,2,1280]{2,1,0:T(2,128)}, u32[]{:S(2)}, u32[]{:S(2)}) async-start(f32[512,2,1280]{2,1,0:T(2,128)} %copy.61), calls=%async_computation.2 | async-start | bytes 10485760 | tf_op jit(solution)/shard_map/all_to_all | solution.py:153
  (52 other events, 993.1 us)
Sparse Core Ops, SparseCore 0:
  113.1 104.3 all-gather.15
  830.1 188.1 reduce-scatter.27
where the time goes:
time: 1310 us; the launch traced here: 1300 us
  blocking collectives  511 us (39%)
  waiting for transfers between devices  378 us (29%)
  matrix products  151 us (12%)
  local copies, waits for them, and re-layouts  130 us (10%)
  other arithmetic  60.1 us (5%)
  starting transfers between devices  51.4 us (4%)
  between operations  20.1 us (2%)
    reduce_scatter x1, waiting for transfers between devices, on_device(): lax.psum_scatter(jnp.stack([across_tokens(flat_n, flat_a), across_tokens(...  188 us
    unnamed x9, blocking collectives  167 us
    all_to_all x1, waiting for transfers between devices, on_device(): lax.all_to_all(summed, 'fsdp', split_axis=0, concat_axis=2, tiled=True)  107 us
    dot_general x18, matrix products, across_hidden(): lax.dot_general(left_side, right_side, (((1,), (1,)), ((), ())), preferre...  88.1 us
    all_gather x1, waiting for transfers between devices, on_device(): steering = lax.all_gather(spread, 'task', axis=0, tiled=True)  72.4 us
    all_gather x5, blocking collectives, on_device(): lax.all_gather(segment_in, 'fsdp', axis=0, tiled=True)  71.5 us
    all_gather x5, blocking collectives, on_device(): cot_rows = lax.all_gather(cot_in, 'fsdp', axis=0, tiled=True)  69.9 us
    all_to_all x1, blocking collectives, on_device(): lax.all_to_all(direc_local.astype(jnp.bfloat16), 'fsdp', split_axis=2, co...  65.6 us
  transfers between devices with their start and end apart: 28, of which 13 were waited for; matrix products, arithmetic and copies ran while one was open for 5% of the time, Pallas kernels for 0%

commit v1 on v0

v1 whole, which is shorter than its diff:
```python
import jax
import jax.numpy as jnp
from jax import lax
from jax.sharding import PartitionSpec as P

ALL = ("section", "task", "fsdp")
eps_norm = 1e-06


def normalize(token_rows):
    return token_rows * lax.rsqrt(
        jnp.mean(token_rows * token_rows, axis=-1, keepdims=True) + eps_norm
    )


def gelu_tanh(values):
    return jax.nn.gelu(values, approximate=True)


def across_hidden(left_side, right_side):
    return lax.dot_general(
        left_side, right_side, (((1,), (1,)), ((), ())), preferred_element_type=jnp.float32
    )


def across_tokens(left_side, right_side):
    return lax.dot_general(
        left_side, right_side, (((0,), (0,)), ((), ())), preferred_element_type=jnp.float32
    )


def dot(left_side, right_side):
    return jnp.dot(left_side, right_side, preferred_element_type=jnp.float32)


def send(value, route):
    sections, tasks, shards = (lax.axis_size(axis) for axis in ALL)
    pairs = []
    for s in range(sections):
        for t in range(tasks):
            for f in range(shards):
                target = route(s, t, f)
                if target is not None:
                    to_s, to_t, to_f = target
                    pairs.append(
                        ((s * tasks + t) * shards + f, (to_s * tasks + to_t) * shards + to_f)
                    )
    return lax.ppermute(value, ALL, pairs)


def between(start, end, k):
    return lambda s, t, f: (end, t, f ^ k) if s == start else None


def gather_rows(rows, start, end):
    parts = []
    for k in range(lax.axis_size("fsdp")):
        if k == 0 and start == end:
            parts.append(rows)
        else:
            parts.append(send(rows, between(start, end, k)))
    return jnp.concatenate(parts, axis=0)


def scatter_sum(partial, start, end):
    shards = lax.axis_size("fsdp")
    blocks = partial.reshape(shards, partial.shape[0] // shards, partial.shape[1])
    total = None
    for k in range(shards):
        if k == 0 and start == end:
            part = blocks[0]
        else:
            part = send(blocks[k].astype(jnp.bfloat16), between(start, end, k)).astype(jnp.float32)
        total = part if total is None else total + part
    return total


def task_partners(value_of):
    parts = [value_of(0)]
    for k in range(1, lax.axis_size("task")):
        parts.append(send(value_of(k), lambda s, t, f, k=k: (s, t ^ k, f)))
    return parts


def fsdp_partners(value_of):
    parts = [value_of(0)]
    for k in range(1, lax.axis_size("fsdp")):
        parts.append(send(value_of(k), lambda s, t, f, k=k: (s, t, f ^ k)))
    return parts


def in_order(parts, index, axis):
    stacked = jnp.stack(parts)
    return jnp.concatenate(
        [
            lax.dynamic_index_in_dim(stacked, index ^ j, 0, keepdims=False)
            for j in range(len(parts))
        ],
        axis=axis,
    )


def sum_everywhere(value):
    for axis in ALL:
        count = lax.axis_size(axis)
        parts = [value]
        for k in range(1, count):
            parts.append(lax.ppermute(value, axis, [(i, i ^ k) for i in range(count)]))
        while len(parts) > 1:
            parts = [parts[i] + parts[i + 1] for i in range(0, len(parts), 2)]
        value = parts[0]
    return value


def on_device(states, task_weights, pad_mask, direction, residual):
    sections = lax.axis_size("section")
    tasks = lax.axis_size("task")
    shards = lax.axis_size("fsdp")
    section_id = lax.axis_index("section")
    task_id = lax.axis_index("task")
    shard_id = lax.axis_index("fsdp")
    w_in = task_weights[0, 0, 0]
    w_out = task_weights[0, 0, 1]
    width, hidden = w_in.shape
    row_count = states.shape[1]
    joined = row_count * shards
    block = width // tasks
    piece = block // shards
    direc_local = direction[0]
    resid_local = residual[0]

    narrow = [direc_local[:, i, :].astype(jnp.bfloat16) for i in range(2)]

    def direction_for(k):
        at = (shard_id ^ k) * hidden
        return jnp.stack([lax.dynamic_slice_in_dim(part, at, hidden, 1) for part in narrow])

    steering = in_order(fsdp_partners(direction_for), shard_id, 1)
    steer_in, steer_out = steering[0], steering[1]

    own_rows = states[0]
    rows_all = gather_rows(own_rows, 0, 0)
    for layer in range(sections):
        normed = normalize(rows_all.astype(jnp.float32))
        normed_b = normed.astype(jnp.bfloat16)
        preact = dot(normed_b, w_in)
        acted, slope = jax.jvp(gelu_tanh, (preact,), (jnp.ones_like(preact),))
        acted_b = acted.astype(jnp.bfloat16)
        if layer + 1 < sections:
            mixed = scatter_sum(across_hidden(acted_b, w_out), layer, layer)
            after = (own_rows.astype(jnp.float32) + mixed).astype(jnp.bfloat16)
            arrived = gather_rows(after, layer, layer + 1)
            here = section_id == layer + 1
            rows_all = jnp.where(here, arrived, rows_all)
            own_rows = jnp.where(here, arrived[:row_count], own_rows)

    def features_for(array):
        return lambda k: lax.dynamic_slice_in_dim(array, (task_id ^ k) * block, block, 1)

    normed_tasks = jnp.concatenate(task_partners(features_for(normed_b)), axis=0)
    acted_tasks = jnp.concatenate(task_partners(lambda k: acted_b), axis=0)
    steered_parts = dot(normed_tasks, steer_in).reshape(tasks, joined, hidden)
    steered = task_partners(
        lambda k: steered_parts[k] if k == 0 else steered_parts[k].astype(jnp.bfloat16)
    )
    steered = sum(part.astype(jnp.float32) for part in steered)
    turned_parts = across_hidden(acted_tasks, steer_out).astype(jnp.bfloat16)
    turned_parts = turned_parts.reshape(tasks, joined, block)
    turned = in_order(task_partners(lambda k: turned_parts[k]), task_id, 1).astype(jnp.float32)

    own_dot = jnp.zeros((row_count, width), jnp.bfloat16)
    for layer in range(sections):
        if layer == 0:
            preact_dot = steered
        else:
            normed_dot = jax.jvp(
                normalize, (rows_all.astype(jnp.float32),), (dots_all.astype(jnp.float32),)
            )[1]
            preact_dot = dot(normed_dot.astype(jnp.bfloat16), w_in) + steered
        acted_dot_b = (slope * preact_dot).astype(jnp.bfloat16)
        mixed_dot = scatter_sum(across_hidden(acted_dot_b, w_out) + turned, layer, layer)
        after_dot = (own_dot.astype(jnp.float32) + mixed_dot).astype(jnp.bfloat16)
        if layer + 1 < sections:
            dots_all = gather_rows(after_dot, layer, layer + 1)
            own_dot = dots_all[:row_count]

    own_bar = after_dot * pad_mask[0][:, None].astype(jnp.bfloat16)
    for layer in reversed(range(sections)):
        if layer == sections - 1:
            bars_all = gather_rows(own_bar, layer, layer)
        else:
            arrived = gather_rows(own_bar, layer + 1, layer)
            here = section_id == layer
            bars_all = jnp.where(here, arrived, bars_all)
            own_bar = jnp.where(here, arrived[:row_count], own_bar)
        preact_bar = (dot(bars_all, w_out) * slope).astype(jnp.bfloat16)
        if layer > 0:
            normed_bar = scatter_sum(across_hidden(preact_bar, w_in), layer, layer)
            pullback = jax.vjp(normalize, own_rows.astype(jnp.float32))[1]
            own_bar = (own_bar.astype(jnp.float32) + pullback(normed_bar)[0]).astype(jnp.bfloat16)

    bars_tasks = jnp.concatenate(task_partners(features_for(bars_all)), axis=0)
    preact_bars_tasks = jnp.concatenate(task_partners(lambda k: preact_bar), axis=0)
    curved = [
        across_tokens(normed_tasks, preact_bars_tasks).astype(jnp.bfloat16),
        across_tokens(bars_tasks, acted_tasks).astype(jnp.bfloat16),
    ]

    def curved_for(k):
        at = (shard_id ^ k) * piece
        return jnp.stack([lax.dynamic_slice_in_dim(part, at, piece, 0) for part in curved])

    product = in_order(fsdp_partners(curved_for), shard_id, 2).astype(jnp.float32)
    product = jnp.transpose(product, (1, 0, 2))

    sums = sum_everywhere(
        jnp.stack(
            [
                jnp.sum(resid_local * resid_local),
                jnp.sum(direc_local * product),
                jnp.sum(resid_local * product),
                jnp.sum(product * product),
            ]
        )
    )
    start_norm, curvature, crossed, squared = sums[0], sums[1], sums[2], sums[3]
    step_size = start_norm / curvature
    next_norm = start_norm - 2.0 * step_size * crossed + step_size * step_size * squared
    resid_next = resid_local - step_size * product
    direc_next = resid_next + next_norm / start_norm * direc_local
    return (resid_next[None], direc_next[None], step_size)


def solution(mesh):
    placed = (
        P("task", "fsdp", None),
        P("task", "section", None, None, "fsdp"),
        P("task", "fsdp"),
        P("section", ("task", "fsdp"), None, None),
        P("section", ("task", "fsdp"), None, None),
    )
    return jax.shard_map(
        on_device,
        mesh=mesh,
        in_specs=placed,
        out_specs=(
            P("section", ("task", "fsdp"), None, None),
            P("section", ("task", "fsdp"), None, None),
            P(),
        ),
        check_vma=False,
    )
```

time: 1310 us -> 428 us (0.33)
  blocking collectives: 511 us -> 0 us
  waiting for transfers between devices: 378 us -> 202 us
  local copies, waits for them, and re-layouts: 130 us -> 23 us
  matrix products: 151 us -> 48.1 us
  starting transfers between devices: 51.4 us -> 110 us
  other arithmetic: 60.1 us -> 31.7 us
    all_gather x14 -> x0, blocking collectives: 198 us -> none  [the longest x5 71.5 us: on_device(): lax.all_gather(segment_in, 'fsdp', axis=0, tiled=True)]
    ppermute x12 -> x61, waiting for transfers between devices: 5.27 us -> 202 us  [the longest x54 195 us: send(): return lax.ppermute(value, ALL, pairs)]
    reduce_scatter x1 -> x0, waiting for transfers between devices: 188 us -> none  [on_device(): lax.psum_scatter(jnp.stack([across_tokens(flat_n, flat_a), across_tokens(...]
    unnamed x9 -> x0, blocking collectives: 167 us -> none
    all_to_all x1 -> x0, waiting for transfers between devices: 107 us -> none  [on_device(): lax.all_to_all(summed, 'fsdp', split_axis=0, concat_axis=2, tiled=True)]
    ppermute x12 -> x61, starting transfers between devices: 16.7 us -> 110 us  [the longest x54 91.9 us: send(): return lax.ppermute(value, ALL, pairs)]
    psum x2 -> x0, blocking collectives: 79.9 us -> none  [the longest x1 42.6 us: on_device(): lax.psum(jnp.sum(resid_next * resid_next), ('section', 'task', 'fsdp'))]
    all_gather x1 -> x0, waiting for transfers between devices: 72.4 us -> none  [on_device(): steering = lax.all_gather(spread, 'task', axis=0, tiled=True)]
  transfers between devices with their start and end apart: 28 -> 61, of which waited for: 13 -> 27; matrix products, arithmetic and copies ran while one was open for 5% -> 9% of each run, Pallas kernels for 0% -> 0%
where the time goes in v1:
time: 428 us; the launch traced here: 422 us
  waiting for transfers between devices  202 us (47%)
  starting transfers between devices  110 us (26%)
  matrix products  48.1 us (11%)
  other arithmetic  31.7 us (7%)
  local copies, waits for them, and re-layouts  23 us (5%)
  between operations  7.08 us (2%)
    ppermute x54, waiting for transfers between devices, send(): return lax.ppermute(value, ALL, pairs)  195 us
    ppermute x54, starting transfers between devices, send(): return lax.ppermute(value, ALL, pairs)  91.9 us
    dot_general x5, matrix products, across_hidden(): lax.dot_general(left_side, right_side, (((1,), (1,)), ((), ())), preferre...  33.9 us
    ppermute x7, starting transfers between devices, sum_everywhere(): parts.append(lax.ppermute(value, axis, [(i, i ^ k) for i in range(count)]))  18.4 us
    unnamed x63, local copies, waits for them, and re-layouts  18.2 us
    dot_general x3, matrix products, dot(): return jnp.dot(left_side, right_side, preferred_element_type=jnp.float32)  11.7 us
  transfers between devices with their start and end apart: 61, of which 27 were waited for; matrix products, arithmetic and copies ran while one was open for 9% of the time, Pallas kernels for 0%

profile of v1, /device:TPU:0, one launch (start us, length us, event | category | flops | bytes accessed | tf_op | source)
XLA Modules:
  0.0 422.2 jit_solution(13930090247643639637)
XLA Ops:
  0.6 7.0 %collective-permute-start.2 = (bf16[48,2048]{1,0:T(8,128)(2,1)}, bf16[48,2048]{1,0:T(8,128)(2,1)}, u32[]{:S(2)}, u32[]{:S(2)}) collective-permute-start(bf16[48,2048]{1,0:T(8,128)(2,1)} %bitcast.204), channel_id=1, source_target_pairs={{0,3},{1,2},{2,1},{3,0},{4,7},{5,6},{6,5},{7,4},{8,11},{9,10},{10,... | collective-permute-start | bytes 589832 | tf_op jit(solution)/shard_map/ppermute | solution.py:48
  22.8 8.9 %fusion.172 = (bf16[192,2048]{1,0:T(8,128)(2,1)}, f32[192,2048]{1,0:T(8,128)}) fusion(bf16[1,1,2,2048,1280]{4,3,2,1,0:T(8,128)(2,1)} %param.6, f32[192]{0:T(256)S(1)} %add_rsqrt_fusion, bf16[48,2048]{1,0:T(8,128)(2,1)} %collective-permute-done.2, bf16[48,2048]{1,0:T(8,128)(2,1)} %collective-permute-done.1, bf16[48,2048]{1,0:T(8,128)(2,1)} %collective-permute-done, ...), kind=kOutput, calls=%fused_computation.232 | convolution fusion | flops 2019803136 | bytes 13632256 | tf_op jit(solution)/shard_map/dot_general | solution.py:21
  34.9 5.7 %collective-permute-start.5 = (bf16[48,2048]{1,0:T(8,128)(2,1)S(1)}, bf16[48,2048]{1,0:T(8,128)(2,1)S(1)}, u32[]{:S(2)}, u32[]{:S(2)}) collective-permute-start(bf16[48,2048]{1,0:T(8,128)(2,1)S(1)} %get-tuple-element.72), channel_id=1, source_target_pairs={{0,3},{1,2},{2,1},{3,0},{4,7},{5,6},{6,5},{7,4},{8,11},{9,10},{10,... | collective-permute-start | bytes 589832 | tf_op jit(solution)/shard_map/ppermute | solution.py:48
  44.5 5.9 %collective-permute-done.4 = bf16[48,2048]{1,0:T(8,128)(2,1)S(1)} collective-permute-done((bf16[48,2048]{1,0:T(8,128)(2,1)S(1)}, bf16[48,2048]{1,0:T(8,128)(2,1)S(1)}, u32[]{:S(2)}, u32[]{:S(2)}) %collective-permute-start.4) | collective-permute-done | bytes 196640 | tf_op jit(solution)/shard_map/ppermute | solution.py:48
  62.1 4.7 %multiply_convert_fusion = (bf16[192,1280]{1,0:T(8,128)(2,1)S(1)}, f32[192,1280]{1,0:T(8,128)}) fusion(bf16[192,2048]{1,0:T(8,128)(2,1)S(1)} %fusion.78, bf16[1,1,2,2048,1280]{4,3,2,1,0:T(8,128)(2,1)} %param.6), kind=kOutput, calls=%fused_computation.108 | convolution fusion | flops 1008844800 | bytes 7503872 | tf_op jit(solution)/shard_map/dot_general | solution.py:33
  70.4 34.6 %collective-permute-done.14 = bf16[2,128,1280]{2,1,0:T(8,128)(2,1)S(1)} collective-permute-done((bf16[2,128,1280]{2,1,0:T(8,128)(2,1)S(1)}, bf16[2,128,1280]{2,1,0:T(8,128)(2,1)S(1)}, u32[]{:S(2)}, u32[]{:S(2)}) %collective-permute-start.14) | collective-permute-done | bytes 655392 | tf_op jit(solution)/shard_map/ppermute | solution.py:48
  132.8 21.9 %collective-permute-done.23 = bf16[192,512]{1,0:T(8,128)(2,1)} collective-permute-done((bf16[192,512]{1,0:T(8,128)(2,1)}, bf16[192,512]{1,0:T(8,128)(2,1)}, u32[]{:S(2)}, u32[]{:S(2)}) %collective-permute-start.23) | collective-permute-done | bytes 196640 | tf_op jit(solution)/shard_map/ppermute | solution.py:48
  156.0 5.5 %fusion.178 = (bf16[192,2048]{1,0:T(8,128)(2,1)S(1)}, f32[192,2048]{1,0:T(8,128)S(1)}) fusion(bf16[192,512]{1,0:T(8,128)(2,1)S(1)} %get-tuple-element.64, bf16[192,512]{1,0:T(8,128)(2,1)S(1)} %get-tuple-element.65, bf16[192,512]{1,0:T(8,128)(2,1)S(1)} %get-tuple-element.66, bf16[192,512]{1,0:T(8,128)(2,1)S(1)} %get-tuple-element.63, ...), kind=kOutput, calls=%fused_computation.234 | convolution fusion | flops 1016463360 | bytes 11829248 | tf_op jit(solution)/shard_map/dot_general | solution.py:21
  161.7 11.8 %collective-permute-start.25 = (bf16[48,2048]{1,0:T(8,128)(2,1)S(1)}, bf16[48,2048]{1,0:T(8,128)(2,1)S(1)}, u32[]{:S(2)}, u32[]{:S(2)}) collective-permute-start(bf16[48,2048]{1,0:T(8,128)(2,1)S(1)} %get-tuple-element.56), channel_id=1, source_target_pairs={{0,1},{1,0},{2,3},{3,2},{4,5},{5,4},{6,7},{7,6},{8,9},{9,8},{10,11... | collective-permute-start | bytes 589832 | tf_op jit(solution)/shard_map/ppermute | solution.py:48
  182.8 4.2 collective-permute-done.26
  196.6 9.7 %fusion.179 = (bf16[192,2048]{1,0:T(8,128)(2,1)S(1)}, f32[192,2048]{1,0:T(8,128)}) fusion(bf16[192,512]{1,0:T(8,128)(2,1)S(1)} %get-tuple-element.64, bf16[192,512]{1,0:T(8,128)(2,1)S(1)} %copy-done.4, bf16[192,512]{1,0:T(8,128)(2,1)S(1)} %copy-done.6, bf16[192,512]{1,0:T(8,128)(2,1)S(1)} %get-tuple-element.63, bf16[1,1,2,2048,1280]{4,3,2,1,0:T(8,128)(2,1)} %param.6, ...), kind=kOutput, calls=%fused_computation.235 | convolution fusion | flops 2028453888 | bytes 18646528 | tf_op jit(solution)/shard_map/dot_general | solution.py:21
  211.7 8.5 %fusion.184 = (bf16[192,2048]{1,0:T(8,128)(2,1)S(1)}, f32[192,2048]{1,0:T(8,128)}) fusion(bf16[1,1,2,2048,1280]{4,3,2,1,0:T(8,128)(2,1)} %param.6, bf16[48,2048]{1,0:T(8,128)(2,1)S(1)} %collective-permute-done.37, bf16[48,2048]{1,0:T(8,128)(2,1)S(1)} %collective-permute-done.36, bf16[48,2048]{1,0:T(8,128)(2,1)S(1)} %collective-permute-done.35, ...), kind=kOutput, calls=%fused_computation.236 | convolution fusion | flops 2021228544 | bytes 14614528 | tf_op jit(solution)/shard_map/dot_general | solution.py:21
  230.3 42.6 %collective-permute-done.44 = bf16[48,2048]{1,0:T(8,128)(2,1)S(1)} collective-permute-done((bf16[48,2048]{1,0:T(8,128)(2,1)S(1)}, bf16[48,2048]{1,0:T(8,128)(2,1)S(1)}, u32[]{:S(2)}, u32[]{:S(2)}) %collective-permute-start.44) | collective-permute-done | bytes 196640 | tf_op jit(solution)/shard_map/ppermute | solution.py:48
  272.9 4.1 collective-permute-done.43
  281.1 4.0 fusion.56
  288.6 8.9 %collective-permute-done.49 = bf16[192,512]{1,0:T(8,128)(2,1)S(1)} collective-permute-done((bf16[192,512]{1,0:T(8,128)(2,1)S(1)}, bf16[192,512]{1,0:T(8,128)(2,1)S(1)}, u32[]{:S(2)}, u32[]{:S(2)}) %collective-permute-start.49) | collective-permute-done | bytes 196640 | tf_op jit(solution)/shard_map/ppermute | solution.py:48
  300.1 7.8 %collective-permute-done.46 = bf16[192,1280]{1,0:T(8,128)(2,1)S(1)} collective-permute-done((bf16[192,1280]{1,0:T(8,128)(2,1)S(1)}, bf16[192,1280]{1,0:T(8,128)(2,1)S(1)}, u32[]{:S(2)}, u32[]{:S(2)}) %collective-permute-start.46) | collective-permute-done | bytes 491552 | tf_op jit(solution)/shard_map/ppermute | solution.py:48
  314.1 23.9 %collective-permute-done.51 = bf16[2,128,1280]{2,1,0:T(8,128)(2,1)S(1)} collective-permute-done((bf16[2,128,1280]{2,1,0:T(8,128)(2,1)S(1)}, bf16[2,128,1280]{2,1,0:T(8,128)(2,1)S(1)}, u32[]{:S(2)}, u32[]{:S(2)}) %collective-permute-start.51) | collective-permute-done | bytes 655392 | tf_op jit(solution)/shard_map/ppermute | solution.py:48
  338.1 19.5 %collective-permute-done.52 = bf16[2,128,1280]{2,1,0:T(8,128)(2,1)S(1)} collective-permute-done((bf16[2,128,1280]{2,1,0:T(8,128)(2,1)S(1)}, bf16[2,128,1280]{2,1,0:T(8,128)(2,1)S(1)}, u32[]{:S(2)}, u32[]{:S(2)}) %collective-permute-start.52) | collective-permute-done | bytes 655392 | tf_op jit(solution)/shard_map/ppermute | solution.py:48
  359.1 5.2 %fusion.24 = (f32[]{:T(128)}, f32[]{:T(128)}, f32[]{:T(128)}, f32[]{:T(128)}) fusion(f32[1,128,2,5120]{3,2,1,0:T(2,128)S(1)} %bitcast.202, bf16[2,128,1280]{2,1,0:T(8,128)(2,1)S(1)} %get-tuple-element.18, bf16[2,128,1280]{2,1,0:T(8,128)(2,1)S(1)} %get-tuple-element.19, bf16[2,128,1280]{2,1,0:T(8,128)(2,1)S(1)} %get-tuple-element.20, ...), kind=kLoop, calls=%fused_computation.31 | loop fusion | flops 20971516 | bytes 13107216 | tf_op jit(solution)/shard_map/reduce_sum | solution.py:219
  378.8 12.9 %collective-permute-start.59 = (f32[4]{0:T(128)S(1)}, f32[4]{0:T(128)S(1)}, u32[]{:S(2)}, u32[]{:S(2)}) collective-permute-start(f32[4]{0:T(128)S(1)} %add_add_fusion.2), channel_id=1, source_target_pairs={{0,2},{1,3},{2,0},{3,1},{4,6},{5,7},{6,4},{7,5},{8,10},{9,11},{10,... | collective-permute-start | bytes 56 | tf_op jit(solution)/shard_map/ppermute | solution.py:108
  399.6 8.2 %fusion.23 = (f32[1,128,2,5120]{3,1,2,0:T(8,128)S(1)}, f32[1,128,2,5120]{3,1,2,0:T(8,128)S(1)}) fusion(f32[1,128,2,5120]{3,2,1,0:T(2,128)} %param.8, f32[1,128,2,5120]{3,2,1,0:T(2,128)} %param.9, f32[]{:T(128)S(6)} %div.44, f32[]{:T(128)} %div.43, bf16[2,128,1280]{2,1,0:T(8,128)(2,1)S(1)} %get-tuple-element.18, ...), kind=kLoop, calls=%fused_computation.29 | loop fusion | flops 15728640 | bytes 23592968 | tf_op jit(solution)/shard_map/broadcast_in_dim | solution.py:231
  407.9 6.4 %copy.15 = f32[1,128,2,5120]{3,2,1,0:T(2,128)} copy(f32[1,128,2,5120]{3,1,2,0:T(8,128)S(1)} %get-tuple-element.15) | data formatting | bytes 10485760
  414.3 6.4 %copy.14 = f32[1,128,2,5120]{3,2,1,0:T(2,128)} copy(f32[1,128,2,5120]{3,1,2,0:T(8,128)S(1)} %get-tuple-element.16) | data formatting | bytes 10485760
  (222 shorter events, 137.0 us)
Async XLA Ops:
  0.6 20.2 %collective-permute-start.2 = (bf16[48,2048]{1,0:T(8,128)(2,1)}, bf16[48,2048]{1,0:T(8,128)(2,1)}, u32[]{:S(2)}, u32[]{:S(2)}) collective-permute-start(bf16[48,2048]{1,0:T(8,128)(2,1)} %bitcast.204), channel_id=1, source_target_pairs={{0,3},{1,2},{2,1},{3,0},{4,7},{5,6},{6,5},{7,4},{8,11},{9,10},{10,... | collective-permute-start | bytes 589832 | tf_op jit(solution)/shard_map/ppermute | solution.py:48
  18.2 51.6 %collective-permute-start.13 = (bf16[2,128,1280]{2,1,0:T(8,128)(2,1)}, bf16[2,128,1280]{2,1,0:T(8,128)(2,1)S(1)}, u32[]{:S(2)}, u32[]{:S(2)}) collective-permute-start(bf16[2,128,1280]{2,1,0:T(8,128)(2,1)} %pad_maximum_fusion.11), channel_id=1, source_target_pairs={{0,1},{1,0},{2,3},{3,2},{4,5},{5,4},{6,7},{7,6},{8,9},{9,8},{10,11... | collective-permute-start | bytes 1966088 | tf_op jit(solution)/shard_map/ppermute | solution.py:48
  57.0 48.0 %collective-permute-start.14 = (bf16[2,128,1280]{2,1,0:T(8,128)(2,1)S(1)}, bf16[2,128,1280]{2,1,0:T(8,128)(2,1)S(1)}, u32[]{:S(2)}, u32[]{:S(2)}) collective-permute-start(bf16[2,128,1280]{2,1,0:T(8,128)(2,1)S(1)} %pad_maximum_fusion.12), channel_id=1, source_target_pairs={{0,2},{1,3},{2,0},{3,1},{4,6},{5,7},{6,4},{7,5},{8,10},{9,11},{10,... | collective-permute-start | bytes 1966088 | tf_op jit(solution)/shard_map/ppermute | solution.py:48
  58.1 49.3 %collective-permute-start.15 = (bf16[2,128,1280]{2,1,0:T(8,128)(2,1)S(1)}, bf16[2,128,1280]{2,1,0:T(8,128)(2,1)S(1)}, u32[]{:S(2)}, u32[]{:S(2)}) collective-permute-start(bf16[2,128,1280]{2,1,0:T(8,128)(2,1)S(1)} %pad_maximum_fusion.13), channel_id=1, source_target_pairs={{0,3},{1,2},{2,1},{3,0},{4,7},{5,6},{6,5},{7,4},{8,11},{9,10},{10,... | collective-permute-start | bytes 1966088 | tf_op jit(solution)/shard_map/ppermute | solution.py:48
  66.8 53.8 %collective-permute-start.21 = (bf16[192,1280]{1,0:T(8,128)(2,1)S(1)}, bf16[192,1280]{1,0:T(8,128)(2,1)S(1)}, u32[]{:S(2)}, u32[]{:S(2)}) collective-permute-start(bf16[192,1280]{1,0:T(8,128)(2,1)S(1)} %get-tuple-element.82), channel_id=1, source_target_pairs={{0,12},{1,13},{2,14},{3,15},{4,8},{5,9},{6,10},{7,11},{8,4},{9,5},... | collective-permute-start | bytes 1474568 | tf_op jit(solution)/shard_map/ppermute | solution.py:48
  69.2 51.4 %collective-permute-start.20 = (bf16[192,1280]{1,0:T(8,128)(2,1)S(1)}, bf16[192,1280]{1,0:T(8,128)(2,1)S(1)}, u32[]{:S(2)}, u32[]{:S(2)}) collective-permute-start(bf16[192,1280]{1,0:T(8,128)(2,1)S(1)} %get-tuple-element.82), channel_id=1, source_target_pairs={{0,8},{1,9},{2,10},{3,11},{4,12},{5,13},{6,14},{7,15},{8,0},{9,1},... | collective-permute-start | bytes 1474568 | tf_op jit(solution)/shard_map/ppermute | solution.py:48
  69.8 50.8 %collective-permute-start.19 = (bf16[192,1280]{1,0:T(8,128)(2,1)S(1)}, bf16[192,1280]{1,0:T(8,128)(2,1)S(1)}, u32[]{:S(2)}, u32[]{:S(2)}) collective-permute-start(bf16[192,1280]{1,0:T(8,128)(2,1)S(1)} %get-tuple-element.82), channel_id=1, source_target_pairs={{0,4},{1,5},{2,6},{3,7},{4,0},{5,1},{6,2},{7,3},{8,12},{9,13},{10,... | collective-permute-start | bytes 1474568 | tf_op jit(solution)/shard_map/ppermute | solution.py:48
  125.2 30.8 %collective-permute-start.16 = (bf16[192,1280]{1,0:T(8,128)(2,1)S(1)}, bf16[192,1280]{1,0:T(8,128)(2,1)}, u32[]{:S(2)}, u32[]{:S(2)}) collective-permute-start(bf16[192,1280]{1,0:T(8,128)(2,1)S(1)} %get-tuple-element.27), channel_id=1, source_target_pairs={{0,4},{1,5},{2,6},{3,7},{4,0},{5,1},{6,2},{7,3},{8,12},{9,13},{10,... | collective-permute-start | bytes 1474568 | tf_op jit(solution)/shard_map/ppermute | solution.py:48
  125.8 30.2 %collective-permute-start.18 = (bf16[192,1280]{1,0:T(8,128)(2,1)S(1)}, bf16[192,1280]{1,0:T(8,128)(2,1)}, u32[]{:S(2)}, u32[]{:S(2)}) collective-permute-start(bf16[192,1280]{1,0:T(8,128)(2,1)S(1)} %get-tuple-element.28), channel_id=1, source_target_pairs={{0,12},{1,13},{2,14},{3,15},{4,8},{5,9},{6,10},{7,11},{8,4},{9,5},... | collective-permute-start | bytes 1474568 | tf_op jit(solution)/shard_map/ppermute | solution.py:48
  127.2 28.8 %collective-permute-start.17 = (bf16[192,1280]{1,0:T(8,128)(2,1)S(1)}, bf16[192,1280]{1,0:T(8,128)(2,1)}, u32[]{:S(2)}, u32[]{:S(2)}) collective-permute-start(bf16[192,1280]{1,0:T(8,128)(2,1)S(1)} %get-tuple-element.29), channel_id=1, source_target_pairs={{0,8},{1,9},{2,10},{3,11},{4,12},{5,13},{6,14},{7,15},{8,0},{9,1},... | collective-permute-start | bytes 1474568 | tf_op jit(solution)/shard_map/ppermute | solution.py:48
  128.7 26.1 %collective-permute-start.23 = (bf16[192,512]{1,0:T(8,128)(2,1)}, bf16[192,512]{1,0:T(8,128)(2,1)}, u32[]{:S(2)}, u32[]{:S(2)}) collective-permute-start(bf16[192,512]{1,0:T(8,128)(2,1)} %get-tuple-element.69), channel_id=1, source_target_pairs={{0,8},{1,9},{2,10},{3,11},{4,12},{5,13},{6,14},{7,15},{8,0},{9,1},... | collective-permute-start | bytes 589832 | tf_op jit(solution)/shard_map/ppermute | solution.py:48
  131.4 23.4 %collective-permute-start.22 = (bf16[192,512]{1,0:T(8,128)(2,1)S(1)}, bf16[192,512]{1,0:T(8,128)(2,1)}, u32[]{:S(2)}, u32[]{:S(2)}) collective-permute-start(bf16[192,512]{1,0:T(8,128)(2,1)S(1)} %get-tuple-element.70), channel_id=1, source_target_pairs={{0,4},{1,5},{2,6},{3,7},{4,0},{5,1},{6,2},{7,3},{8,12},{9,13},{10,... | collective-permute-start | bytes 589832 | tf_op jit(solution)/shard_map/ppermute | solution.py:48
  161.7 17.5 %collective-permute-start.25 = (bf16[48,2048]{1,0:T(8,128)(2,1)S(1)}, bf16[48,2048]{1,0:T(8,128)(2,1)S(1)}, u32[]{:S(2)}, u32[]{:S(2)}) collective-permute-start(bf16[48,2048]{1,0:T(8,128)(2,1)S(1)} %get-tuple-element.56), channel_id=1, source_target_pairs={{0,1},{1,0},{2,3},{3,2},{4,5},{5,4},{6,7},{7,6},{8,9},{9,8},{10,11... | collective-permute-start | bytes 589832 | tf_op jit(solution)/shard_map/ppermute | solution.py:48
  224.8 48.0 %collective-permute-start.44 = (bf16[48,2048]{1,0:T(8,128)(2,1)S(1)}, bf16[48,2048]{1,0:T(8,128)(2,1)S(1)}, u32[]{:S(2)}, u32[]{:S(2)}) collective-permute-start(bf16[48,2048]{1,0:T(8,128)(2,1)S(1)} %fusion.131), channel_id=1, source_target_pairs={{16,3},{17,2},{18,1},{19,0},{20,7},{21,6},{22,5},{23,4},{24,11},{2... | collective-permute-start | bytes 589832 | tf_op jit(solution)/shard_map/ppermute | solution.py:48
  226.1 50.9 %collective-permute-start.43 = (bf16[48,2048]{1,0:T(8,128)(2,1)S(1)}, bf16[48,2048]{1,0:T(8,128)(2,1)S(1)}, u32[]{:S(2)}, u32[]{:S(2)}) collective-permute-start(bf16[48,2048]{1,0:T(8,128)(2,1)S(1)} %fusion.131), channel_id=1, source_target_pairs={{16,2},{17,3},{18,0},{19,1},{20,6},{21,7},{22,4},{23,5},{24,10},{2... | collective-permute-start | bytes 589832 | tf_op jit(solution)/shard_map/ppermute | solution.py:48
  227.4 49.6 %collective-permute-start.42 = (bf16[48,2048]{1,0:T(8,128)(2,1)S(1)}, bf16[48,2048]{1,0:T(8,128)(2,1)S(1)}, u32[]{:S(2)}, u32[]{:S(2)}) collective-permute-start(bf16[48,2048]{1,0:T(8,128)(2,1)S(1)} %fusion.131), channel_id=1, source_target_pairs={{16,1},{17,0},{18,3},{19,2},{20,5},{21,4},{22,7},{23,6},{24,9},{25... | collective-permute-start | bytes 589832 | tf_op jit(solution)/shard_map/ppermute | solution.py:48
  228.7 48.3 %collective-permute-start.41 = (bf16[48,2048]{1,0:T(8,128)(2,1)S(1)}, bf16[48,2048]{1,0:T(8,128)(2,1)S(1)}, u32[]{:S(2)}, u32[]{:S(2)}) collective-permute-start(bf16[48,2048]{1,0:T(8,128)(2,1)S(1)} %fusion.131), channel_id=1, source_target_pairs={{16,0},{17,1},{18,2},{19,3},{20,4},{21,5},{22,6},{23,7},{24,8},{25... | collective-permute-start | bytes 589832 | tf_op jit(solution)/shard_map/ppermute | solution.py:48
  278.3 19.1 %collective-permute-start.49 = (bf16[192,512]{1,0:T(8,128)(2,1)S(1)}, bf16[192,512]{1,0:T(8,128)(2,1)S(1)}, u32[]{:S(2)}, u32[]{:S(2)}) collective-permute-start(bf16[192,512]{1,0:T(8,128)(2,1)S(1)} %get-tuple-element.48), channel_id=1, source_target_pairs={{0,8},{1,9},{2,10},{3,11},{4,12},{5,13},{6,14},{7,15},{8,0},{9,1},... | collective-permute-start | bytes 589832 | tf_op jit(solution)/shard_map/ppermute | solution.py:48
  279.7 17.7 %collective-permute-start.48 = (bf16[192,512]{1,0:T(8,128)(2,1)S(1)}, bf16[192,512]{1,0:T(8,128)(2,1)S(1)}, u32[]{:S(2)}, u32[]{:S(2)}) collective-permute-start(bf16[192,512]{1,0:T(8,128)(2,1)S(1)} %get-tuple-element.49), channel_id=1, source_target_pairs={{0,4},{1,5},{2,6},{3,7},{4,0},{5,1},{6,2},{7,3},{8,12},{9,13},{10,... | collective-permute-start | bytes 589832 | tf_op jit(solution)/shard_map/ppermute | solution.py:48
  285.9 22.0 %collective-permute-start.46 = (bf16[192,1280]{1,0:T(8,128)(2,1)S(1)}, bf16[192,1280]{1,0:T(8,128)(2,1)S(1)}, u32[]{:S(2)}, u32[]{:S(2)}) collective-permute-start(bf16[192,1280]{1,0:T(8,128)(2,1)S(1)} %fusion.56), channel_id=1, source_target_pairs={{0,8},{1,9},{2,10},{3,11},{4,12},{5,13},{6,14},{7,15},{8,0},{9,1},... | collective-permute-start | bytes 1474568 | tf_op jit(solution)/shard_map/ppermute | solution.py:48
  287.3 20.6 %collective-permute-start.45 = (bf16[192,1280]{1,0:T(8,128)(2,1)S(1)}, bf16[192,1280]{1,0:T(8,128)(2,1)S(1)}, u32[]{:S(2)}, u32[]{:S(2)}) collective-permute-start(bf16[192,1280]{1,0:T(8,128)(2,1)S(1)} %fusion.56), channel_id=1, source_target_pairs={{0,4},{1,5},{2,6},{3,7},{4,0},{5,1},{6,2},{7,3},{8,12},{9,13},{10,... | collective-permute-start | bytes 1474568 | tf_op jit(solution)/shard_map/ppermute | solution.py:48
  309.4 28.7 %collective-permute-start.51 = (bf16[2,128,1280]{2,1,0:T(8,128)(2,1)S(1)}, bf16[2,128,1280]{2,1,0:T(8,128)(2,1)S(1)}, u32[]{:S(2)}, u32[]{:S(2)}) collective-permute-start(bf16[2,128,1280]{2,1,0:T(8,128)(2,1)S(1)} %pad_maximum_fusion.14), channel_id=1, source_target_pairs={{0,1},{1,0},{2,3},{3,2},{4,5},{5,4},{6,7},{7,6},{8,9},{9,8},{10,11... | collective-permute-start | bytes 1966088 | tf_op jit(solution)/shard_map/ppermute | solution.py:48
  310.8 46.7 %collective-permute-start.52 = (bf16[2,128,1280]{2,1,0:T(8,128)(2,1)S(1)}, bf16[2,128,1280]{2,1,0:T(8,128)(2,1)S(1)}, u32[]{:S(2)}, u32[]{:S(2)}) collective-permute-start(bf16[2,128,1280]{2,1,0:T(8,128)(2,1)S(1)} %pad_maximum_fusion.15), channel_id=1, source_target_pairs={{0,2},{1,3},{2,0},{3,1},{4,6},{5,7},{6,4},{7,5},{8,10},{9,11},{10,... | collective-permute-start | bytes 1966088 | tf_op jit(solution)/shard_map/ppermute | solution.py:48
  312.0 45.6 %collective-permute-start.53 = (bf16[2,128,1280]{2,1,0:T(8,128)(2,1)S(1)}, bf16[2,128,1280]{2,1,0:T(8,128)(2,1)S(1)}, u32[]{:S(2)}, u32[]{:S(2)}) collective-permute-start(bf16[2,128,1280]{2,1,0:T(8,128)(2,1)S(1)} %pad_maximum_fusion.16), channel_id=1, source_target_pairs={{0,3},{1,2},{2,1},{3,0},{4,7},{5,6},{6,5},{7,4},{8,11},{9,10},{10,... | collective-permute-start | bytes 1966088 | tf_op jit(solution)/shard_map/ppermute | solution.py:48
  (67 other events, 710.6 us)

commit v2 on v1

--- a/solution.py
+++ b/solution.py
@@ -87,6 +87,10 @@
     for k in range(1, lax.axis_size("fsdp")):
         parts.append(send(value_of(k), lambda s, t, f, k=k: (s, t, f ^ k)))
     return parts
+
+
+def tie(value, other):
+    return lax.optimization_barrier((value, other))
 
 
 def in_order(parts, index, axis):
@@ -135,11 +139,10 @@
         at = (shard_id ^ k) * hidden
         return jnp.stack([lax.dynamic_slice_in_dim(part, at, hidden, 1) for part in narrow])
 
-    steering = in_order(fsdp_partners(direction_for), shard_id, 1)
-    steer_in, steer_out = steering[0], steering[1]
-
-    own_rows = states[0]
-    rows_all = gather_rows(own_rows, 0, 0)
+    pieces = fsdp_partners(direction_for)
+
+    own_inputs = [states[0]]
+    rows_all = gather_rows(states[0], 0, 0)
     for layer in range(sections):
         normed = normalize(rows_all.astype(jnp.float32))
         normed_b = normed.astype(jnp.bfloat16)
@@ -147,12 +150,19 @@
         acted, slope = jax.jvp(gelu_tanh, (preact,), (jnp.ones_like(preact),))
         acted_b = acted.astype(jnp.bfloat16)
         if layer + 1 < sections:
-            mixed = scatter_sum(across_hidden(acted_b, w_out), layer, layer)
-            after = (own_rows.astype(jnp.float32) + mixed).astype(jnp.bfloat16)
-            arrived = gather_rows(after, layer, layer + 1)
-            here = section_id == layer + 1
-            rows_all = jnp.where(here, arrived, rows_all)
-            own_rows = jnp.where(here, arrived[:row_count], own_rows)
+            mixed = across_hidden(acted_b, w_out)
+            if layer == 0:
+                mixed, pieces[1] = tie(mixed, pieces[1])
+            mixed = scatter_sum(mixed, layer, 0)
+            own_rows = (own_inputs[layer].astype(jnp.float32) + mixed).astype(jnp.bfloat16)
+            if layer == 0:
+                own_rows, pieces[2] = tie(own_rows, pieces[2])
+            own_inputs.append(own_rows)
+            arrived = gather_rows(own_rows, 0, layer + 1)
+            rows_all = jnp.where(section_id == layer + 1, arrived, rows_all)
+
+    steering = in_order(pieces, shard_id, 1)
+    steer_in, steer_out = steering[0], steering[1]
 
     def features_for(array):
         return lambda k: lax.dynamic_slice_in_dim(array, (task_id ^ k) * block, block, 1)
@@ -173,45 +183,39 @@
         if layer == 0:
             preact_dot = steered
         else:
+            dots_all = gather_rows(own_dot, 0, layer)
             normed_dot = jax.jvp(
                 normalize, (rows_all.astype(jnp.float32),), (dots_all.astype(jnp.float32),)
             )[1]
             preact_dot = dot(normed_dot.astype(jnp.bfloat16), w_in) + steered
         acted_dot_b = (slope * preact_dot).astype(jnp.bfloat16)
-        mixed_dot = scatter_sum(across_hidden(acted_dot_b, w_out) + turned, layer, layer)
-        after_dot = (own_dot.astype(jnp.float32) + mixed_dot).astype(jnp.bfloat16)
-        if layer + 1 < sections:
-            dots_all = gather_rows(after_dot, layer, layer + 1)
-            own_dot = dots_all[:row_count]
-
-    own_bar = after_dot * pad_mask[0][:, None].astype(jnp.bfloat16)
+        mixed_dot = scatter_sum(across_hidden(acted_dot_b, w_out) + turned, layer, 0)
+        own_dot = (own_dot.astype(jnp.float32) + mixed_dot).astype(jnp.bfloat16)
+
+    own_bar = own_dot * pad_mask[0][:, None].astype(jnp.bfloat16)
+    bars_all = jnp.zeros((joined, width), jnp.bfloat16)
     for layer in reversed(range(sections)):
-        if layer == sections - 1:
-            bars_all = gather_rows(own_bar, layer, layer)
-        else:
-            arrived = gather_rows(own_bar, layer + 1, layer)
-            here = section_id == layer
-            bars_all = jnp.where(here, arrived, bars_all)
-            own_bar = jnp.where(here, arrived[:row_count], own_bar)
+        arrived = gather_rows(own_bar, 0, layer)
+        bars_all = jnp.where(section_id == layer, arrived, bars_all)
         preact_bar = (dot(bars_all, w_out) * slope).astype(jnp.bfloat16)
         if layer > 0:
-            normed_bar = scatter_sum(across_hidden(preact_bar, w_in), layer, layer)
-            pullback = jax.vjp(normalize, own_rows.astype(jnp.float32))[1]
+            normed_bar = scatter_sum(across_hidden(preact_bar, w_in), layer, 0)
+            pullback = jax.vjp(normalize, own_inputs[layer].astype(jnp.float32))[1]
             own_bar = (own_bar.astype(jnp.float32) + pullback(normed_bar)[0]).astype(jnp.bfloat16)
 
+    def to_owners(curved):
+        curved = curved.astype(jnp.bfloat16).reshape(shards, piece, hidden)
+
+        def curved_for(k):
+            return lax.dynamic_index_in_dim(curved, shard_id ^ k, 0, keepdims=False)
+
+        return in_order(fsdp_partners(curved_for), shard_id, 1)
+
     bars_tasks = jnp.concatenate(task_partners(features_for(bars_all)), axis=0)
+    curved_out = to_owners(across_tokens(bars_tasks, acted_tasks))
     preact_bars_tasks = jnp.concatenate(task_partners(lambda k: preact_bar), axis=0)
-    curved = [
-        across_tokens(normed_tasks, preact_bars_tasks).astype(jnp.bfloat16),
-        across_tokens(bars_tasks, acted_tasks).astype(jnp.bfloat16),
-    ]
-
-    def curved_for(k):
-        at = (shard_id ^ k) * piece
-        return jnp.stack([lax.dynamic_slice_in_dim(part, at, piece, 0) for part in curved])
-
-    product = in_order(fsdp_partners(curved_for), shard_id, 2).astype(jnp.float32)
-    product = jnp.transpose(product, (1, 0, 2))
+    curved_in = to_owners(across_tokens(normed_tasks, preact_bars_tasks))
+    product = jnp.stack([curved_in, curved_out], axis=1).astype(jnp.float32)
 
     sums = sum_everywhere(
         jnp.stack(

time: 428 us -> 384 us (0.90)
  waiting for transfers between devices: 202 us -> 165 us
  matrix products: 48.1 us -> 41.4 us
  starting transfers between devices: 110 us -> 115 us
    ppermute x54 -> x59, waiting for transfers between devices: 195 us -> 159 us  [send(): return lax.ppermute(value, ALL, pairs)]
    ppermute x54 -> x59, starting transfers between devices: 91.9 us -> 107 us  [send(): return lax.ppermute(value, ALL, pairs)]
    ppermute x7, starting transfers between devices: 18.4 us -> 7.89 us  [sum_everywhere(): parts.append(lax.ppermute(value, axis, [(i, i ^ k) for i in range(count)]))]
    broadcast_in_dim x1 -> x0, other arithmetic: 8.23 us -> none  [on_device(): return (resid_next[None], direc_next[None], step_size)]
    add x0 -> x1, other arithmetic: none -> 8.23 us  [on_device(): direc_next = resid_next + next_norm / start_norm * direc_local]
    unnamed x63 -> x67, local copies, waits for them, and re-layouts: 18.2 us -> 18.3 us
  transfers between devices with their start and end apart: 61 -> 66, of which waited for: 27 -> 31; matrix products, arithmetic and copies ran while one was open for 9% -> 9% of each run, Pallas kernels for 0% -> 0%
where the time goes in v2:
time: 384 us; the launch traced here: 378 us
  waiting for transfers between devices  165 us (43%)
  starting transfers between devices  115 us (30%)
  matrix products  41.4 us (11%)
  other arithmetic  28.4 us (7%)
  local copies, waits for them, and re-layouts  21.3 us (6%)
  between operations  7.31 us (2%)
    ppermute x59, waiting for transfers between devices, send(): return lax.ppermute(value, ALL, pairs)  159 us
    ppermute x59, starting transfers between devices, send(): return lax.ppermute(value, ALL, pairs)  107 us
    dot_general x5, matrix products, across_hidden(): lax.dot_general(left_side, right_side, (((1,), (1,)), ((), ())), preferre...  29.7 us
    unnamed x67, local copies, waits for them, and re-layouts  18.3 us
    dot_general x3, matrix products, dot(): return jnp.dot(left_side, right_side, preferred_element_type=jnp.float32)  9.31 us
    add x1, other arithmetic, on_device(): direc_next = resid_next + next_norm / start_norm * direc_local  8.23 us
    ppermute x7, starting transfers between devices, sum_everywhere(): parts.append(lax.ppermute(value, axis, [(i, i ^ k) for i in range(count)]))  7.89 us
  transfers between devices with their start and end apart: 66, of which 31 were waited for; matrix products, arithmetic and copies ran while one was open for 9% of the time, Pallas kernels for 0%

profile of v2, /device:TPU:0, one launch (start us, length us, event | category | flops | bytes accessed | tf_op | source)
XLA Modules:
  0.0 378.2 jit_solution(6353108278800979761)
XLA Ops:
  0.6 7.0 %collective-permute-start.2 = (bf16[48,2048]{1,0:T(8,128)(2,1)}, bf16[48,2048]{1,0:T(8,128)(2,1)S(1)}, u32[]{:S(2)}, u32[]{:S(2)}) collective-permute-start(bf16[48,2048]{1,0:T(8,128)(2,1)} %bitcast.178), channel_id=1, source_target_pairs={{0,3},{1,2},{2,1},{3,0},{4,7},{5,6},{6,5},{7,4},{8,11},{9,10},{10,... | collective-permute-start | bytes 589832 | tf_op jit(solution)/shard_map/ppermute | solution.py:48
  24.3 5.8 %collective-permute-done = bf16[48,2048]{1,0:T(8,128)(2,1)} collective-permute-done((bf16[48,2048]{1,0:T(8,128)(2,1)}, bf16[48,2048]{1,0:T(8,128)(2,1)}, u32[]{:S(2)}, u32[]{:S(2)}) %collective-permute-start) | collective-permute-done | bytes 196640 | tf_op jit(solution)/shard_map/ppermute | solution.py:48
  31.5 7.4 %fusion.11 = f32[192,2048]{1,0:T(8,128)S(1)} fusion(bf16[1,1,2,2048,1280]{4,3,2,1,0:T(8,128)(2,1)} %param.6, f32[192]{0:T(256)S(1)} %add_rsqrt_fusion, bf16[48,2048]{1,0:T(8,128)(2,1)S(1)} %collective-permute-done.2, bf16[48,2048]{1,0:T(8,128)(2,1)} %collective-permute-done.1, bf16[48,2048]{1,0:T(8,128)(2,1)} %collective-permute-done, ...), kind=kOutput, calls=%fused_computation.14 | convolution fusion | flops 2019409920 | bytes 12845824 | tf_op jit(solution)/shard_map/dot_general | solution.py:21
  38.9 6.0 %collective-permute-done.3 = bf16[2,128,1280]{2,1,0:T(8,128)(2,1)} collective-permute-done((bf16[2,128,1280]{2,1,0:T(8,128)(2,1)}, bf16[2,128,1280]{2,1,0:T(8,128)(2,1)}, u32[]{:S(2)}, u32[]{:S(2)}) %collective-permute-start.3) | collective-permute-done | bytes 655392 | tf_op jit(solution)/shard_map/ppermute | solution.py:48
  47.2 6.8 %collective-permute-start.6 = (bf16[48,2048]{1,0:T(8,128)(2,1)S(1)}, bf16[48,2048]{1,0:T(8,128)(2,1)S(1)}, u32[]{:S(2)}, u32[]{:S(2)}) collective-permute-start(bf16[48,2048]{1,0:T(8,128)(2,1)S(1)} %get-tuple-element.89), channel_id=1, source_target_pairs={{0,3},{1,2},{2,1},{3,0},{4,7},{5,6},{6,5},{7,4},{8,11},{9,10},{10,... | collective-permute-start | bytes 589832 | tf_op jit(solution)/shard_map/ppermute | solution.py:48
  56.5 8.7 %collective-permute-done.4 = bf16[48,2048]{1,0:T(8,128)(2,1)S(1)} collective-permute-done((bf16[48,2048]{1,0:T(8,128)(2,1)S(1)}, bf16[48,2048]{1,0:T(8,128)(2,1)S(1)}, u32[]{:S(2)}, u32[]{:S(2)}) %collective-permute-start.4) | collective-permute-done | bytes 196640 | tf_op jit(solution)/shard_map/ppermute | solution.py:48
  65.2 16.8 %collective-permute-done.5 = bf16[48,2048]{1,0:T(8,128)(2,1)S(1)} collective-permute-done((bf16[48,2048]{1,0:T(8,128)(2,1)S(1)}, bf16[48,2048]{1,0:T(8,128)(2,1)S(1)}, u32[]{:S(2)}, u32[]{:S(2)}) %collective-permute-start.5) | collective-permute-done | bytes 196640 | tf_op jit(solution)/shard_map/ppermute | solution.py:48
  102.1 24.2 %collective-permute-done.13 = bf16[192,512]{1,0:T(8,128)(2,1)S(1)} collective-permute-done((bf16[192,512]{1,0:T(8,128)(2,1)S(1)}, bf16[192,512]{1,0:T(8,128)(2,1)S(1)}, u32[]{:S(2)}, u32[]{:S(2)}) %collective-permute-start.13) | collective-permute-done | bytes 196640 | tf_op jit(solution)/shard_map/ppermute | solution.py:48
  141.3 22.9 %collective-permute-done.23 = bf16[192,512]{1,0:T(8,128)(2,1)} collective-permute-done((bf16[192,512]{1,0:T(8,128)(2,1)S(1)}, bf16[192,512]{1,0:T(8,128)(2,1)}, u32[]{:S(2)}, u32[]{:S(2)}) %collective-permute-start.23) | collective-permute-done | bytes 196640 | tf_op jit(solution)/shard_map/ppermute | solution.py:48
  165.9 5.5 %fusion.171 = (bf16[192,2048]{1,0:T(8,128)(2,1)S(1)}, f32[192,2048]{1,0:T(8,128)S(1)}) fusion(bf16[192,512]{1,0:T(8,128)(2,1)S(1)} %get-tuple-element.81, bf16[192,512]{1,0:T(8,128)(2,1)S(1)} %get-tuple-element.82, bf16[192,512]{1,0:T(8,128)(2,1)S(1)} %get-tuple-element.83, bf16[192,512]{1,0:T(8,128)(2,1)S(1)} %get-tuple-element.80, ...), kind=kOutput, calls=%fused_computation.228 | convolution fusion | flops 1016463360 | bytes 11829248 | tf_op jit(solution)/shard_map/dot_general | solution.py:21
  198.5 8.4 %fusion.55 = bf16[192,2048]{1,0:T(8,128)(2,1)S(1)} fusion(bf16[1,1,2,2048,1280]{4,3,2,1,0:T(8,128)(2,1)} %param.6, bf16[192,2048]{1,0:T(8,128)(2,1)S(1)} %get-tuple-element.23, f32[192]{0:T(256)S(1)} %multiply_multiply_fusion.3, f32[192]{0:T(256)S(1)} %fusion.144, bf16[48,2048]{1,0:T(8,128)(2,1)S(1)} %collective-permute-done.31, ...), kind=kOutput, calls=%fused_computation.55 | convolution fusion | flops 2028453888 | bytes 17073664 | tf_op jit(solution)/shard_map/dot_general | solution.py:21
  212.4 5.0 %collective-permute-done.35 = bf16[48,2048]{1,0:T(8,128)(2,1)S(1)} collective-permute-done((bf16[48,2048]{1,0:T(8,128)(2,1)S(1)}, bf16[48,2048]{1,0:T(8,128)(2,1)S(1)}, u32[]{:S(2)}, u32[]{:S(2)}) %collective-permute-start.35) | collective-permute-done | bytes 196640 | tf_op jit(solution)/shard_map/ppermute | solution.py:48
  217.4 5.3 %collective-permute-done.34 = bf16[48,2048]{1,0:T(8,128)(2,1)S(1)} collective-permute-done((bf16[48,2048]{1,0:T(8,128)(2,1)S(1)}, bf16[48,2048]{1,0:T(8,128)(2,1)S(1)}, u32[]{:S(2)}, u32[]{:S(2)}) %collective-permute-start.34) | collective-permute-done | bytes 196640 | tf_op jit(solution)/shard_map/ppermute | solution.py:48
  231.6 7.1 %fusion.52 = bf16[192,2048]{1,0:T(8,128)(2,1)S(1)} fusion(bf16[1,1,2,2048,1280]{4,3,2,1,0:T(8,128)(2,1)} %param.6, bf16[48,2048]{1,0:T(8,128)(2,1)S(1)} %collective-permute-done.39, bf16[48,2048]{1,0:T(8,128)(2,1)S(1)} %collective-permute-done.38, bf16[48,2048]{1,0:T(8,128)(2,1)S(1)} %collective-permute-done.37, ...), kind=kOutput, calls=%fused_computation.54 | convolution fusion | flops 2021621760 | bytes 13041665 | tf_op jit(solution)/shard_map/dot_general | solution.py:21
  244.0 5.7 %collective-permute-done.43 = bf16[48,2048]{1,0:T(8,128)(2,1)S(1)} collective-permute-done((bf16[48,2048]{1,0:T(8,128)(2,1)S(1)}, bf16[48,2048]{1,0:T(8,128)(2,1)S(1)}, u32[]{:S(2)}, u32[]{:S(2)}) %collective-permute-start.43) | collective-permute-done | bytes 196640 | tf_op jit(solution)/shard_map/ppermute | solution.py:48
  249.7 5.7 %collective-permute-done.42 = bf16[48,2048]{1,0:T(8,128)(2,1)S(1)} collective-permute-done((bf16[48,2048]{1,0:T(8,128)(2,1)S(1)}, bf16[48,2048]{1,0:T(8,128)(2,1)S(1)}, u32[]{:S(2)}, u32[]{:S(2)}) %collective-permute-start.42) | collective-permute-done | bytes 196640 | tf_op jit(solution)/shard_map/ppermute | solution.py:48
  269.5 5.6 %collective-permute-done.44 = bf16[48,2048]{1,0:T(8,128)(2,1)S(1)} collective-permute-done((bf16[48,2048]{1,0:T(8,128)(2,1)S(1)}, bf16[48,2048]{1,0:T(8,128)(2,1)S(1)}, u32[]{:S(2)}, u32[]{:S(2)}) %collective-permute-start.44) | collective-permute-done | bytes 196640 | tf_op jit(solution)/shard_map/ppermute | solution.py:48
  293.2 5.2 %collective-permute-done.48 = bf16[192,1280]{1,0:T(8,128)(2,1)S(1)} collective-permute-done((bf16[192,1280]{1,0:T(8,128)(2,1)S(1)}, bf16[192,1280]{1,0:T(8,128)(2,1)S(1)}, u32[]{:S(2)}, u32[]{:S(2)}) %collective-permute-start.48) | collective-permute-done | bytes 491552 | tf_op jit(solution)/shard_map/ppermute | solution.py:48
  300.6 9.2 %collective-permute-start.50 = (bf16[128,1280]{1,0:T(8,128)(2,1)S(1)}, bf16[128,1280]{1,0:T(8,128)(2,1)S(1)}, u32[]{:S(2)}, u32[]{:S(2)}) collective-permute-start(bf16[128,1280]{1,0:T(8,128)(2,1)S(1)} %get-tuple-element.44), channel_id=1, source_target_pairs={{0,1},{1,0},{2,3},{3,2},{4,5},{5,4},{6,7},{7,6},{8,9},{9,8},{10,11... | collective-permute-start | bytes 983048 | tf_op jit(solution)/shard_map/ppermute | solution.py:48
  309.8 9.1 %collective-permute-done.57 = bf16[128,1280]{1,0:T(8,128)(2,1)S(1)} collective-permute-done((bf16[128,1280]{1,0:T(8,128)(2,1)S(1)}, bf16[128,1280]{1,0:T(8,128)(2,1)S(1)}, u32[]{:S(2)}, u32[]{:S(2)}) %collective-permute-start.57) | collective-permute-done | bytes 327712 | tf_op jit(solution)/shard_map/ppermute | solution.py:48
  319.5 6.8 %collective-permute-done.51 = bf16[128,1280]{1,0:T(8,128)(2,1)S(1)} collective-permute-done((bf16[128,1280]{1,0:T(8,128)(2,1)S(1)}, bf16[128,1280]{1,0:T(8,128)(2,1)S(1)}, u32[]{:S(2)}, u32[]{:S(2)}) %collective-permute-start.51) | collective-permute-done | bytes 327712 | tf_op jit(solution)/shard_map/ppermute | solution.py:48
  355.6 8.2 %multiply_add_fusion = (f32[1,128,2,5120]{3,1,2,0:T(8,128)S(1)}, f32[1,128,2,5120]{3,1,2,0:T(8,128)S(1)}) fusion(f32[1,128,2,5120]{3,2,1,0:T(2,128)} %param.8, f32[]{:T(128)S(6)} %div.44, bf16[1,128,1,5120]{3,1,2,0:T(8,128)(2,1)S(1)} %get-tuple-element.35, bf16[1,128,1,5120]{3,1,2,0:T(8,128)(2,1)S(1)} %get-tuple-element.33, f32[]{:T(128)} %div.43, ...), kind=kLoop, calls=%fused_computation.27 | loop fusion | flops 7864320 | bytes 23592968 | tf_op jit(solution)/shard_map/add | solution.py:234
  363.9 6.4 %copy.16 = f32[1,128,2,5120]{3,2,1,0:T(2,128)} copy(f32[1,128,2,5120]{3,1,2,0:T(8,128)S(1)} %get-tuple-element.20) | data formatting | bytes 10485760
  370.3 6.4 %copy.15 = f32[1,128,2,5120]{3,2,1,0:T(2,128)} copy(f32[1,128,2,5120]{3,1,2,0:T(8,128)S(1)} %get-tuple-element.21) | data formatting | bytes 10485760
  (238 shorter events, 165.7 us)
Async XLA Ops:
  0.6 23.7 %collective-permute-start.2 = (bf16[48,2048]{1,0:T(8,128)(2,1)}, bf16[48,2048]{1,0:T(8,128)(2,1)S(1)}, u32[]{:S(2)}, u32[]{:S(2)}) collective-permute-start(bf16[48,2048]{1,0:T(8,128)(2,1)} %bitcast.178), channel_id=1, source_target_pairs={{0,3},{1,2},{2,1},{3,0},{4,7},{5,6},{6,5},{7,4},{8,11},{9,10},{10,... | collective-permute-start | bytes 589832 | tf_op jit(solution)/shard_map/ppermute | solution.py:48
  7.6 16.7 %collective-permute-start.1 = (bf16[48,2048]{1,0:T(8,128)(2,1)}, bf16[48,2048]{1,0:T(8,128)(2,1)}, u32[]{:S(2)}, u32[]{:S(2)}) collective-permute-start(bf16[48,2048]{1,0:T(8,128)(2,1)} %bitcast.179), channel_id=1, source_target_pairs={{0,2},{1,3},{2,0},{3,1},{4,6},{5,7},{6,4},{7,5},{8,10},{9,11},{10,... | collective-permute-start | bytes 589832 | tf_op jit(solution)/shard_map/ppermute | solution.py:48
  9.5 20.7 %collective-permute-start = (bf16[48,2048]{1,0:T(8,128)(2,1)}, bf16[48,2048]{1,0:T(8,128)(2,1)}, u32[]{:S(2)}, u32[]{:S(2)}) collective-permute-start(bf16[48,2048]{1,0:T(8,128)(2,1)} %bitcast.180), channel_id=1, source_target_pairs={{0,1},{1,0},{2,3},{3,2},{4,5},{5,4},{6,7},{7,6},{8,9},{9,8},{10,11... | collective-permute-start | bytes 589832 | tf_op jit(solution)/shard_map/ppermute | solution.py:48
  18.2 26.7 %collective-permute-start.3 = (bf16[2,128,1280]{2,1,0:T(8,128)(2,1)}, bf16[2,128,1280]{2,1,0:T(8,128)(2,1)}, u32[]{:S(2)}, u32[]{:S(2)}) collective-permute-start(bf16[2,128,1280]{2,1,0:T(8,128)(2,1)} %pad_maximum_fusion.13), channel_id=1, source_target_pairs={{0,1},{1,0},{2,3},{3,2},{4,5},{5,4},{6,7},{7,6},{8,9},{9,8},{10,11... | collective-permute-start | bytes 1966088 | tf_op jit(solution)/shard_map/ppermute | solution.py:48
  20.5 61.7 %collective-permute-start.7 = (bf16[2,128,1280]{2,1,0:T(8,128)(2,1)}, bf16[2,128,1280]{2,1,0:T(8,128)(2,1)}, u32[]{:S(2)}, u32[]{:S(2)}) collective-permute-start(bf16[2,128,1280]{2,1,0:T(8,128)(2,1)} %pad_maximum_fusion.14), channel_id=1, source_target_pairs={{0,2},{1,3},{2,0},{3,1},{4,6},{5,7},{6,4},{7,5},{8,10},{9,11},{10,... | collective-permute-start | bytes 1966088 | tf_op jit(solution)/shard_map/ppermute | solution.py:48
  24.3 63.3 %collective-permute-start.15 = (bf16[2,128,1280]{2,1,0:T(8,128)(2,1)}, bf16[2,128,1280]{2,1,0:T(8,128)(2,1)S(1)}, u32[]{:S(2)}, u32[]{:S(2)}) collective-permute-start(bf16[2,128,1280]{2,1,0:T(8,128)(2,1)} %pad_maximum_fusion.15), channel_id=1, source_target_pairs={{0,3},{1,2},{2,1},{3,0},{4,7},{5,6},{6,5},{7,4},{8,11},{9,10},{10,... | collective-permute-start | bytes 1966088 | tf_op jit(solution)/shard_map/ppermute | solution.py:48
  45.0 20.2 %collective-permute-start.4 = (bf16[48,2048]{1,0:T(8,128)(2,1)S(1)}, bf16[48,2048]{1,0:T(8,128)(2,1)S(1)}, u32[]{:S(2)}, u32[]{:S(2)}) collective-permute-start(bf16[48,2048]{1,0:T(8,128)(2,1)S(1)} %get-tuple-element.88), channel_id=1, source_target_pairs={{0,1},{1,0},{2,3},{3,2},{4,5},{5,4},{6,7},{7,6},{8,9},{9,8},{10,11... | collective-permute-start | bytes 589832 | tf_op jit(solution)/shard_map/ppermute | solution.py:48
  47.2 18.0 %collective-permute-start.6 = (bf16[48,2048]{1,0:T(8,128)(2,1)S(1)}, bf16[48,2048]{1,0:T(8,128)(2,1)S(1)}, u32[]{:S(2)}, u32[]{:S(2)}) collective-permute-start(bf16[48,2048]{1,0:T(8,128)(2,1)S(1)} %get-tuple-element.89), channel_id=1, source_target_pairs={{0,3},{1,2},{2,1},{3,0},{4,7},{5,6},{6,5},{7,4},{8,11},{9,10},{10,... | collective-permute-start | bytes 589832 | tf_op jit(solution)/shard_map/ppermute | solution.py:48
  54.0 28.1 %collective-permute-start.5 = (bf16[48,2048]{1,0:T(8,128)(2,1)S(1)}, bf16[48,2048]{1,0:T(8,128)(2,1)S(1)}, u32[]{:S(2)}, u32[]{:S(2)}) collective-permute-start(bf16[48,2048]{1,0:T(8,128)(2,1)S(1)} %get-tuple-element.90), channel_id=1, source_target_pairs={{0,2},{1,3},{2,0},{3,1},{4,6},{5,7},{6,4},{7,5},{8,10},{9,11},{10,... | collective-permute-start | bytes 589832 | tf_op jit(solution)/shard_map/ppermute | solution.py:48
  97.3 32.1 %collective-permute-start.21 = (bf16[192,1280]{1,0:T(8,128)(2,1)S(1)}, bf16[192,1280]{1,0:T(8,128)(2,1)S(1)}, u32[]{:S(2)}, u32[]{:S(2)}) collective-permute-start(bf16[192,1280]{1,0:T(8,128)(2,1)S(1)} %get-tuple-element.97), channel_id=1, source_target_pairs={{0,12},{1,13},{2,14},{3,15},{4,8},{5,9},{6,10},{7,11},{8,4},{9,5},... | collective-permute-start | bytes 1474568 | tf_op jit(solution)/shard_map/ppermute | solution.py:48
  97.8 31.7 %collective-permute-start.20 = (bf16[192,1280]{1,0:T(8,128)(2,1)S(1)}, bf16[192,1280]{1,0:T(8,128)(2,1)S(1)}, u32[]{:S(2)}, u32[]{:S(2)}) collective-permute-start(bf16[192,1280]{1,0:T(8,128)(2,1)S(1)} %get-tuple-element.97), channel_id=1, source_target_pairs={{0,8},{1,9},{2,10},{3,11},{4,12},{5,13},{6,14},{7,15},{8,0},{9,1},... | collective-permute-start | bytes 1474568 | tf_op jit(solution)/shard_map/ppermute | solution.py:48
  99.3 30.2 %collective-permute-start.19 = (bf16[192,1280]{1,0:T(8,128)(2,1)S(1)}, bf16[192,1280]{1,0:T(8,128)(2,1)S(1)}, u32[]{:S(2)}, u32[]{:S(2)}) collective-permute-start(bf16[192,1280]{1,0:T(8,128)(2,1)S(1)} %get-tuple-element.97), channel_id=1, source_target_pairs={{0,4},{1,5},{2,6},{3,7},{4,0},{5,1},{6,2},{7,3},{8,12},{9,13},{10,... | collective-permute-start | bytes 1474568 | tf_op jit(solution)/shard_map/ppermute | solution.py:48
  100.8 25.5 %collective-permute-start.13 = (bf16[192,512]{1,0:T(8,128)(2,1)S(1)}, bf16[192,512]{1,0:T(8,128)(2,1)S(1)}, u32[]{:S(2)}, u32[]{:S(2)}) collective-permute-start(bf16[192,512]{1,0:T(8,128)(2,1)S(1)} %get-tuple-element.78), channel_id=1, source_target_pairs={{0,8},{1,9},{2,10},{3,11},{4,12},{5,13},{6,14},{7,15},{8,0},{9,1},... | collective-permute-start | bytes 589832 | tf_op jit(solution)/shard_map/ppermute | solution.py:48
  101.3 25.0 %collective-permute-start.12 = (bf16[192,512]{1,0:T(8,128)(2,1)S(1)}, bf16[192,512]{1,0:T(8,128)(2,1)S(1)}, u32[]{:S(2)}, u32[]{:S(2)}) collective-permute-start(bf16[192,512]{1,0:T(8,128)(2,1)S(1)} %get-tuple-element.79), channel_id=1, source_target_pairs={{0,4},{1,5},{2,6},{3,7},{4,0},{5,1},{6,2},{7,3},{8,12},{9,13},{10,... | collective-permute-start | bytes 589832 | tf_op jit(solution)/shard_map/ppermute | solution.py:48
  133.7 32.1 %collective-permute-start.16 = (bf16[192,1280]{1,0:T(8,128)(2,1)S(1)}, bf16[192,1280]{1,0:T(8,128)(2,1)}, u32[]{:S(2)}, u32[]{:S(2)}) collective-permute-start(bf16[192,1280]{1,0:T(8,128)(2,1)S(1)} %get-tuple-element.30), channel_id=1, source_target_pairs={{0,4},{1,5},{2,6},{3,7},{4,0},{5,1},{6,2},{7,3},{8,12},{9,13},{10,... | collective-permute-start | bytes 1474568 | tf_op jit(solution)/shard_map/ppermute | solution.py:48
  134.3 31.5 %collective-permute-start.18 = (bf16[192,1280]{1,0:T(8,128)(2,1)S(1)}, bf16[192,1280]{1,0:T(8,128)(2,1)}, u32[]{:S(2)}, u32[]{:S(2)}) collective-permute-start(bf16[192,1280]{1,0:T(8,128)(2,1)S(1)} %get-tuple-element.31), channel_id=1, source_target_pairs={{0,12},{1,13},{2,14},{3,15},{4,8},{5,9},{6,10},{7,11},{8,4},{9,5},... | collective-permute-start | bytes 1474568 | tf_op jit(solution)/shard_map/ppermute | solution.py:48
  135.7 30.1 %collective-permute-start.17 = (bf16[192,1280]{1,0:T(8,128)(2,1)S(1)}, bf16[192,1280]{1,0:T(8,128)(2,1)}, u32[]{:S(2)}, u32[]{:S(2)}) collective-permute-start(bf16[192,1280]{1,0:T(8,128)(2,1)S(1)} %get-tuple-element.32), channel_id=1, source_target_pairs={{0,8},{1,9},{2,10},{3,11},{4,12},{5,13},{6,14},{7,15},{8,0},{9,1},... | collective-permute-start | bytes 1474568 | tf_op jit(solution)/shard_map/ppermute | solution.py:48
  137.3 26.9 %collective-permute-start.23 = (bf16[192,512]{1,0:T(8,128)(2,1)S(1)}, bf16[192,512]{1,0:T(8,128)(2,1)}, u32[]{:S(2)}, u32[]{:S(2)}) collective-permute-start(bf16[192,512]{1,0:T(8,128)(2,1)S(1)} %get-tuple-element.86), channel_id=1, source_target_pairs={{0,8},{1,9},{2,10},{3,11},{4,12},{5,13},{6,14},{7,15},{8,0},{9,1},... | collective-permute-start | bytes 589832 | tf_op jit(solution)/shard_map/ppermute | solution.py:48
  139.5 24.9 %collective-permute-start.22 = (bf16[192,512]{1,0:T(8,128)(2,1)S(1)}, bf16[192,512]{1,0:T(8,128)(2,1)}, u32[]{:S(2)}, u32[]{:S(2)}) collective-permute-start(bf16[192,512]{1,0:T(8,128)(2,1)S(1)} %get-tuple-element.87), channel_id=1, source_target_pairs={{0,4},{1,5},{2,6},{3,7},{4,0},{5,1},{6,2},{7,3},{8,12},{9,13},{10,... | collective-permute-start | bytes 589832 | tf_op jit(solution)/shard_map/ppermute | solution.py:48
  288.3 30.6 %collective-permute-start.57 = (bf16[128,1280]{1,0:T(8,128)(2,1)S(1)}, bf16[128,1280]{1,0:T(8,128)(2,1)S(1)}, u32[]{:S(2)}, u32[]{:S(2)}) collective-permute-start(bf16[128,1280]{1,0:T(8,128)(2,1)S(1)} %get-tuple-element.51), channel_id=1, source_target_pairs={{0,2},{1,3},{2,0},{3,1},{4,6},{5,7},{6,4},{7,5},{8,10},{9,11},{10,... | collective-permute-start | bytes 983048 | tf_op jit(solution)/shard_map/ppermute | solution.py:48
  293.2 25.8 %collective-permute-start.56 = (bf16[128,1280]{1,0:T(8,128)(2,1)S(1)}, bf16[128,1280]{1,0:T(8,128)(2,1)S(1)}, u32[]{:S(2)}, u32[]{:S(2)}) collective-permute-start(bf16[128,1280]{1,0:T(8,128)(2,1)S(1)} %get-tuple-element.52), channel_id=1, source_target_pairs={{0,1},{1,0},{2,3},{3,2},{4,5},{5,4},{6,7},{7,6},{8,9},{9,8},{10,11... | collective-permute-start | bytes 983048 | tf_op jit(solution)/shard_map/ppermute | solution.py:48
  299.7 19.8 %collective-permute-start.52 = (bf16[128,1280]{1,0:T(8,128)(2,1)S(1)}, bf16[128,1280]{1,0:T(8,128)(2,1)S(1)}, u32[]{:S(2)}, u32[]{:S(2)}) collective-permute-start(bf16[128,1280]{1,0:T(8,128)(2,1)S(1)} %get-tuple-element.42), channel_id=1, source_target_pairs={{0,3},{1,2},{2,1},{3,0},{4,7},{5,6},{6,5},{7,4},{8,11},{9,10},{10,... | collective-permute-start | bytes 983048 | tf_op jit(solution)/shard_map/ppermute | solution.py:48
  299.8 26.4 %collective-permute-start.51 = (bf16[128,1280]{1,0:T(8,128)(2,1)S(1)}, bf16[128,1280]{1,0:T(8,128)(2,1)S(1)}, u32[]{:S(2)}, u32[]{:S(2)}) collective-permute-start(bf16[128,1280]{1,0:T(8,128)(2,1)S(1)} %get-tuple-element.43), channel_id=1, source_target_pairs={{0,2},{1,3},{2,0},{3,1},{4,6},{5,7},{6,4},{7,5},{8,10},{9,11},{10,... | collective-permute-start | bytes 983048 | tf_op jit(solution)/shard_map/ppermute | solution.py:48
  300.6 25.6 %collective-permute-start.50 = (bf16[128,1280]{1,0:T(8,128)(2,1)S(1)}, bf16[128,1280]{1,0:T(8,128)(2,1)S(1)}, u32[]{:S(2)}, u32[]{:S(2)}) collective-permute-start(bf16[128,1280]{1,0:T(8,128)(2,1)S(1)} %get-tuple-element.44), channel_id=1, source_target_pairs={{0,1},{1,0},{2,3},{3,2},{4,5},{5,4},{6,7},{7,6},{8,9},{9,8},{10,11... | collective-permute-start | bytes 983048 | tf_op jit(solution)/shard_map/ppermute | solution.py:48
  (74 other events, 663.9 us)

commit v3 on v2

--- a/solution.py
+++ b/solution.py
@@ -1,6 +1,9 @@
 import jax
 import jax.numpy as jnp
 from jax import lax
+from jax.experimental import pallas as pl
+from jax.experimental.pallas import tpu as pltpu
+from jax.experimental.layout import Layout, with_layout_constraint
 from jax.sharding import PartitionSpec as P
 
 ALL = ("section", "task", "fsdp")
@@ -114,6 +117,35 @@
             parts = [parts[i] + parts[i + 1] for i in range(0, len(parts), 2)]
         value = parts[0]
     return value
+
+
+def update_kernel(scalars, in_ref, out_ref, resid_ref, direc_ref, resid_next, direc_next):
+    for i, product in ((0, in_ref), (1, out_ref)):
+        fresh = resid_ref[:, i, :] - scalars[0] * product[...].astype(jnp.float32)
+        resid_next[:, i, :] = fresh
+        direc_next[:, i, :] = fresh + scalars[1] * direc_ref[:, i, :]
+
+
+def update(scalars, curved_in, curved_out, resid, direc, columns):
+    rows, pair, total = resid.shape
+    native = pl.BlockSpec((rows, pair, columns), lambda i: (0, 0, i))
+    flat = pl.BlockSpec((rows, columns), lambda i: (0, i))
+    return pl.pallas_call(
+        update_kernel,
+        grid=(total // columns,),
+        in_specs=[pl.BlockSpec(memory_space=pltpu.SMEM), flat, flat, native, native],
+        out_specs=[native, native],
+        out_shape=[jax.ShapeDtypeStruct(resid.shape, jnp.float32)] * 2,
+        compiler_params=pltpu.CompilerParams(vmem_limit_bytes=32 * 1024 * 1024),
+        cost_estimate=pl.CostEstimate(
+            flops=4 * resid.size, bytes_accessed=20 * resid.size, transcendentals=0
+        ),
+    )(scalars, curved_in, curved_out, resid, direc)
+
+
+def apart(array):
+    turned = with_layout_constraint(jnp.transpose(array, (1, 0, 2)), Layout((0, 1, 2)))
+    return lax.optimization_barrier(turned)
 
 
 def on_device(states, task_weights, pad_mask, direction, residual):
@@ -133,7 +165,9 @@
     direc_local = direction[0]
     resid_local = residual[0]
 
-    narrow = [direc_local[:, i, :].astype(jnp.bfloat16) for i in range(2)]
+    direc_apart = apart(direc_local)
+    resid_apart = apart(resid_local)
+    narrow = [direc_apart[i].astype(jnp.bfloat16) for i in range(2)]
 
     def direction_for(k):
         at = (shard_id ^ k) * hidden
@@ -159,6 +193,8 @@
                 own_rows, pieces[2] = tie(own_rows, pieces[2])
             own_inputs.append(own_rows)
             arrived = gather_rows(own_rows, 0, layer + 1)
+            if layer == 0:
+                arrived, (pieces[3], resid_apart) = tie(arrived, (pieces[3], resid_apart))
             rows_all = jnp.where(section_id == layer + 1, arrived, rows_all)
 
     steering = in_order(pieces, shard_id, 1)
@@ -167,7 +203,9 @@
     def features_for(array):
         return lambda k: lax.dynamic_slice_in_dim(array, (task_id ^ k) * block, block, 1)
 
-    normed_tasks = jnp.concatenate(task_partners(features_for(normed_b)), axis=0)
+    normed_parts = task_partners(features_for(normed_b))
+    acted_b, normed_parts = tie(acted_b, normed_parts)
+    normed_tasks = jnp.concatenate(normed_parts, axis=0)
     acted_tasks = jnp.concatenate(task_partners(lambda k: acted_b), axis=0)
     steered_parts = dot(normed_tasks, steer_in).reshape(tasks, joined, hidden)
     steered = task_partners(
@@ -215,23 +253,29 @@
     curved_out = to_owners(across_tokens(bars_tasks, acted_tasks))
     preact_bars_tasks = jnp.concatenate(task_partners(lambda k: preact_bar), axis=0)
     curved_in = to_owners(across_tokens(normed_tasks, preact_bars_tasks))
-    product = jnp.stack([curved_in, curved_out], axis=1).astype(jnp.float32)
+    products = [curved.astype(jnp.float32) for curved in (curved_in, curved_out)]
 
     sums = sum_everywhere(
         jnp.stack(
             [
-                jnp.sum(resid_local * resid_local),
-                jnp.sum(direc_local * product),
-                jnp.sum(resid_local * product),
-                jnp.sum(product * product),
+                jnp.sum(resid_apart * resid_apart),
+                sum(jnp.sum(direc_apart[i] * products[i]) for i in range(2)),
+                sum(jnp.sum(resid_apart[i] * products[i]) for i in range(2)),
+                sum(jnp.sum(products[i] * products[i]) for i in range(2)),
             ]
         )
     )
     start_norm, curvature, crossed, squared = sums[0], sums[1], sums[2], sums[3]
     step_size = start_norm / curvature
     next_norm = start_norm - 2.0 * step_size * crossed + step_size * step_size * squared
-    resid_next = resid_local - step_size * product
-    direc_next = resid_next + next_norm / start_norm * direc_local
+    resid_next, direc_next = update(
+        jnp.stack([step_size, next_norm / start_norm]),
+        curved_in,
+        curved_out,
+        resid_local,
+        direc_local,
+        hidden,
+    )
     return (resid_next[None], direc_next[None], step_size)
 
 

time: 384 us -> 373 us (0.971); the launches traced: 378 us -> 372 us
  waiting for transfers between devices: 165 us -> 137 us
  starting transfers between devices: 115 us -> 128 us
  other arithmetic: 28.4 us -> 20 us
  Pallas kernels: 0 us -> 7.69 us
    ppermute x59, waiting for transfers between devices: 159 us -> 131 us  [send(): return lax.ppermute(value, ALL, pairs)]
    ppermute x59, starting transfers between devices: 107 us -> 121 us  [send(): return lax.ppermute(value, ALL, pairs)]
    transpose x0 -> x2, local copies, waits for them, and re-layouts: none -> 10.7 us  [apart(): jnp.transpose(array, (1, 0, 2))]
    unnamed x67 -> x60, local copies, waits for them, and re-layouts: 18.3 us -> 8.07 us
    add x1 -> x0, other arithmetic: 8.23 us -> none  [on_device(): direc_next = resid_next + next_norm / start_norm * direc_local]
    pallas_call x0 -> x1, Pallas kernels: none -> 7.69 us  [update(): pl.pallas_call(update_kernel, grid=(total // columns,), in_specs=[pl.Bloc...]
  transfers between devices with their start and end apart: 66 -> 66, of which waited for: 31 -> 35; matrix products, arithmetic and copies ran while one was open for 9% -> 12% of each run, Pallas kernels for 0% -> 0%
where the time goes in v3:
time: 373 us; the launch traced here: 372 us
  waiting for transfers between devices  137 us (37%)
  starting transfers between devices  128 us (34%)
  matrix products  44.5 us (12%)
  local copies, waits for them, and re-layouts  23.6 us (6%)
  other arithmetic  20 us (5%)
  between operations  10.6 us (3%)
  Pallas kernels  7.69 us (2%)
    ppermute x59, waiting for transfers between devices, send(): return lax.ppermute(value, ALL, pairs)  131 us
    ppermute x59, starting transfers between devices, send(): return lax.ppermute(value, ALL, pairs)  121 us
    dot_general x5, matrix products, across_hidden(): lax.dot_general(left_side, right_side, (((1,), (1,)), ((), ())), preferre...  30.4 us
    dot_general x3, matrix products, dot(): return jnp.dot(left_side, right_side, preferred_element_type=jnp.float32)  11.7 us
    transpose x2, local copies, waits for them, and re-layouts, apart(): jnp.transpose(array, (1, 0, 2))  10.7 us
    unnamed x60, local copies, waits for them, and re-layouts  8.07 us
    pallas_call x1, Pallas kernels, update(): pl.pallas_call(update_kernel, grid=(total // columns,), in_specs=[pl.Bloc...  7.69 us
  transfers between devices with their start and end apart: 66, of which 35 were waited for; matrix products, arithmetic and copies ran while one was open for 12% of the time, Pallas kernels for 0%

profile of v3, /device:TPU:0, one launch (start us, length us, event | category | flops | bytes accessed | tf_op | source)
XLA Modules:
  0.0 371.7 jit_solution(2320868134012570155)
XLA Ops:
  0.6 7.0 %collective-permute-start.2 = (bf16[48,2048]{1,0:T(8,128)(2,1)}, bf16[48,2048]{1,0:T(8,128)(2,1)S(1)}, u32[]{:S(2)}, u32[]{:S(2)}) collective-permute-start(bf16[48,2048]{1,0:T(8,128)(2,1)} %bitcast.194), channel_id=1, source_target_pairs={{0,3},{1,2},{2,1},{3,0},{4,7},{5,6},{6,5},{7,4},{8,11},{9,10},{10,... | collective-permute-start | bytes 589832 | tf_op jit(solution)/shard_map/ppermute | solution.py:51
  12.0 4.2 %copy.8 = f32[2,128,5120]{2,1,0:T(8,128)S(1)} copy(f32[2,128,5120]{2,0,1:T(2,128)} %bitcast.188) | data formatting | bytes 10485760 | tf_op jit(solution)/shard_map/transpose | solution.py:147
  29.8 7.4 %fusion.8 = f32[192,2048]{1,0:T(8,128)S(1)} fusion(bf16[1,1,2,2048,1280]{4,3,2,1,0:T(8,128)(2,1)} %param.6, f32[192]{0:T(256)S(1)} %add_rsqrt_fusion, bf16[48,2048]{1,0:T(8,128)(2,1)S(1)} %collective-permute-done.2, bf16[48,2048]{1,0:T(8,128)(2,1)} %collective-permute-done.1, bf16[48,2048]{1,0:T(8,128)(2,1)} %collective-permute-done, ...), kind=kOutput, calls=%fused_computation.8 | convolution fusion | flops 2019409920 | bytes 12845824 | tf_op jit(solution)/shard_map/dot_general | solution.py:24
  37.2 9.7 %collective-permute-done.3 = bf16[2,128,1280]{2,1,0:T(8,128)(2,1)} collective-permute-done((bf16[2,128,1280]{2,1,0:T(8,128)(2,1)}, bf16[2,128,1280]{2,1,0:T(8,128)(2,1)}, u32[]{:S(2)}, u32[]{:S(2)}) %collective-permute-start.3) | collective-permute-done | bytes 655392 | tf_op jit(solution)/shard_map/ppermute | solution.py:51
  52.7 5.3 %collective-permute-start.4 = (bf16[48,2048]{1,0:T(8,128)(2,1)}, bf16[48,2048]{1,0:T(8,128)(2,1)}, u32[]{:S(2)}, u32[]{:S(2)}) collective-permute-start(bf16[48,2048]{1,0:T(8,128)(2,1)} %get-tuple-element.105), channel_id=1, source_target_pairs={{0,1},{1,0},{2,3},{3,2},{4,5},{5,4},{6,7},{7,6},{8,9},{9,8},{10,11... | collective-permute-start | bytes 589832 | tf_op jit(solution)/shard_map/ppermute | solution.py:51
  59.8 6.5 %copy.9 = f32[2,128,5120]{2,1,0:T(8,128)} copy(f32[2,128,5120]{2,0,1:T(2,128)} %bitcast.186) | data formatting | bytes 10485760 | tf_op jit(solution)/shard_map/transpose | solution.py:147
  66.4 12.7 %collective-permute-done.5 = bf16[48,2048]{1,0:T(8,128)(2,1)} collective-permute-done((bf16[48,2048]{1,0:T(8,128)(2,1)}, bf16[48,2048]{1,0:T(8,128)(2,1)}, u32[]{:S(2)}, u32[]{:S(2)}) %collective-permute-start.5) | collective-permute-done | bytes 196640 | tf_op jit(solution)/shard_map/ppermute | solution.py:51
  90.7 4.7 %multiply_convert_fusion.1 = (bf16[192,1280]{1,0:T(8,128)(2,1)S(1)}, f32[192,1280]{1,0:T(8,128)}) fusion(bf16[192,2048]{1,0:T(8,128)(2,1)S(1)} %fusion.84, bf16[1,1,2,2048,1280]{4,3,2,1,0:T(8,128)(2,1)} %param.6), kind=kOutput, calls=%fused_computation.114 | convolution fusion | flops 1008844800 | bytes 7503872 | tf_op jit(solution)/shard_map/dot_general | solution.py:36
  111.8 4.2 %collective-permute-done.19 = bf16[192,1280]{1,0:T(8,128)(2,1)S(1)} collective-permute-done((bf16[192,1280]{1,0:T(8,128)(2,1)S(1)}, bf16[192,1280]{1,0:T(8,128)(2,1)S(1)}, u32[]{:S(2)}, u32[]{:S(2)}) %collective-permute-start.19) | collective-permute-done | bytes 491552 | tf_op jit(solution)/shard_map/ppermute | solution.py:51
  119.4 8.3 %collective-permute-done.21 = bf16[192,1280]{1,0:T(8,128)(2,1)S(1)} collective-permute-done((bf16[192,1280]{1,0:T(8,128)(2,1)S(1)}, bf16[192,1280]{1,0:T(8,128)(2,1)S(1)}, u32[]{:S(2)}, u32[]{:S(2)}) %collective-permute-start.21) | collective-permute-done | bytes 491552 | tf_op jit(solution)/shard_map/ppermute | solution.py:51
  137.9 26.0 %collective-permute-done.23 = bf16[192,512]{1,0:T(8,128)(2,1)} collective-permute-done((bf16[192,512]{1,0:T(8,128)(2,1)}, bf16[192,512]{1,0:T(8,128)(2,1)}, u32[]{:S(2)}, u32[]{:S(2)}) %collective-permute-start.23) | collective-permute-done | bytes 196640 | tf_op jit(solution)/shard_map/ppermute | solution.py:51
  165.3 5.6 %fusion.168 = (bf16[192,2048]{1,0:T(8,128)(2,1)S(1)}, f32[192,2048]{1,0:T(8,128)S(1)}) fusion(bf16[192,512]{1,0:T(8,128)(2,1)S(1)} %get-tuple-element.94, bf16[192,512]{1,0:T(8,128)(2,1)S(1)} %get-tuple-element.95, bf16[192,512]{1,0:T(8,128)(2,1)S(1)} %get-tuple-element.96, bf16[192,512]{1,0:T(8,128)(2,1)S(1)} %get-tuple-element.93, ...), kind=kOutput, calls=%fused_computation.234 | convolution fusion | flops 1016463360 | bytes 11829248 | tf_op jit(solution)/shard_map/dot_general | solution.py:24
  173.6 10.6 %collective-permute-start.26 = (bf16[48,2048]{1,0:T(8,128)(2,1)S(1)}, bf16[48,2048]{1,0:T(8,128)(2,1)S(1)}, u32[]{:S(2)}, u32[]{:S(2)}) collective-permute-start(bf16[48,2048]{1,0:T(8,128)(2,1)S(1)} %get-tuple-element.92), channel_id=1, source_target_pairs={{0,2},{1,3},{2,0},{3,1},{4,6},{5,7},{6,4},{7,5},{8,10},{9,11},{10,... | collective-permute-start | bytes 589832 | tf_op jit(solution)/shard_map/ppermute | solution.py:51
  201.9 8.7 %fusion.57 = bf16[192,2048]{1,0:T(8,128)(2,1)S(1)} fusion(bf16[1,1,2,2048,1280]{4,3,2,1,0:T(8,128)(2,1)} %param.6, bf16[192,2048]{1,0:T(8,128)(2,1)S(1)} %get-tuple-element.44, f32[192]{0:T(256)S(1)} %multiply_multiply_fusion.3, f32[192]{0:T(256)S(1)} %fusion.144, bf16[48,2048]{1,0:T(8,128)(2,1)} %copy-done.14, bf16[48,2048]{1,0:T(8,128)(2,1)} %copy-done.15, ...), kind=kOutput, calls=%fused_computation.58 | convolution fusion | flops 2028453888 | bytes 17073664 | tf_op jit(solution)/shard_map/dot_general | solution.py:24
  219.7 5.6 %collective-permute-done.34 = bf16[48,2048]{1,0:T(8,128)(2,1)S(1)} collective-permute-done((bf16[48,2048]{1,0:T(8,128)(2,1)S(1)}, bf16[48,2048]{1,0:T(8,128)(2,1)S(1)}, u32[]{:S(2)}, u32[]{:S(2)}) %collective-permute-start.34) | collective-permute-done | bytes 196640 | tf_op jit(solution)/shard_map/ppermute | solution.py:51
  234.2 7.4 %fusion.54 = bf16[192,2048]{1,0:T(8,128)(2,1)S(1)} fusion(bf16[1,1,2,2048,1280]{4,3,2,1,0:T(8,128)(2,1)} %param.6, bf16[48,2048]{1,0:T(8,128)(2,1)S(1)} %collective-permute-done.39, bf16[48,2048]{1,0:T(8,128)(2,1)S(1)} %collective-permute-done.38, bf16[48,2048]{1,0:T(8,128)(2,1)S(1)} %collective-permute-done.37, ...), kind=kOutput, calls=%fused_computation.57 | convolution fusion | flops 2021621760 | bytes 13041665 | tf_op jit(solution)/shard_map/dot_general | solution.py:24
  246.9 4.4 %collective-permute-done.43 = bf16[48,2048]{1,0:T(8,128)(2,1)S(1)} collective-permute-done((bf16[48,2048]{1,0:T(8,128)(2,1)S(1)}, bf16[48,2048]{1,0:T(8,128)(2,1)S(1)}, u32[]{:S(2)}, u32[]{:S(2)}) %collective-permute-start.43) | collective-permute-done | bytes 196640 | tf_op jit(solution)/shard_map/ppermute | solution.py:51
  251.3 5.7 %collective-permute-done.42 = bf16[48,2048]{1,0:T(8,128)(2,1)S(1)} collective-permute-done((bf16[48,2048]{1,0:T(8,128)(2,1)S(1)}, bf16[48,2048]{1,0:T(8,128)(2,1)S(1)}, u32[]{:S(2)}, u32[]{:S(2)}) %collective-permute-start.42) | collective-permute-done | bytes 196640 | tf_op jit(solution)/shard_map/ppermute | solution.py:51
  262.6 5.0 %collective-permute-start.44 = (bf16[48,2048]{1,0:T(8,128)(2,1)S(1)}, bf16[48,2048]{1,0:T(8,128)(2,1)S(1)}, u32[]{:S(2)}, u32[]{:S(2)}) collective-permute-start(bf16[48,2048]{1,0:T(8,128)(2,1)S(1)} %fusion.137), channel_id=1, source_target_pairs={{0,1},{1,0},{2,3},{3,2},{4,5},{5,4},{6,7},{7,6},{8,9},{9,8},{10,11... | collective-permute-start | bytes 589832 | tf_op jit(solution)/shard_map/ppermute | solution.py:51
  267.6 4.5 %multiply_reduce_fusion = f32[]{:T(128)} fusion(f32[2,128,5120]{2,1,0:T(8,128)} %copy.9), kind=kLoop, calls=%fused_computation.18 | loop fusion | flops 2621439 | bytes 5242884 | tf_op jit(solution)/shard_map/reduce_sum | solution.py:261
  301.4 12.4 %collective-permute-start.50 = (bf16[128,1280]{1,0:T(8,128)(2,1)S(1)}, bf16[128,1280]{1,0:T(8,128)(2,1)S(1)}, u32[]{:S(2)}, u32[]{:S(2)}) collective-permute-start(bf16[128,1280]{1,0:T(8,128)(2,1)S(1)} %get-tuple-element.69), channel_id=1, source_target_pairs={{0,1},{1,0},{2,3},{3,2},{4,5},{5,4},{6,7},{7,6},{8,9},{9,8},{10,11... | collective-permute-start | bytes 983048 | tf_op jit(solution)/shard_map/ppermute | solution.py:51
  313.8 10.9 %collective-permute-done.57 = bf16[128,1280]{1,0:T(8,128)(2,1)S(1)} collective-permute-done((bf16[128,1280]{1,0:T(8,128)(2,1)S(1)}, bf16[128,1280]{1,0:T(8,128)(2,1)S(1)}, u32[]{:S(2)}, u32[]{:S(2)}) %collective-permute-start.57) | collective-permute-done | bytes 327712 | tf_op jit(solution)/shard_map/ppermute | solution.py:51
  325.0 7.4 %collective-permute-done.51 = bf16[128,1280]{1,0:T(8,128)(2,1)S(1)} collective-permute-done((bf16[128,1280]{1,0:T(8,128)(2,1)S(1)}, bf16[128,1280]{1,0:T(8,128)(2,1)S(1)}, u32[]{:S(2)}, u32[]{:S(2)}) %collective-permute-start.51) | collective-permute-done | bytes 327712 | tf_op jit(solution)/shard_map/ppermute | solution.py:51
  362.9 7.7 %shard_map.76 = (f32[128,2,5120]{2,1,0:T(2,128)}, f32[128,2,5120]{2,1,0:T(2,128)}) custom-call(f32[2]{0:T(128)S(1)} %pad_maximum_fusion.17.scalars, bf16[128,5120]{1,0:T(8,128)(2,1)S(1)} %get-tuple-element.41.in_ref, bf16[128,5120]{1,0:T(8,128)(2,1)S(1)} %get-tuple-element.42.out_ref, f32[128,2,5120]{2,1,0:T(2,128)S(1)} %bitcast.187, ...), custom_call_target="tpu_custom_call" | custom-call | flops 5242880 | bytes 26214400 | tf_op jit(solution)/shard_map/pallas_call | solution.py:133
  (235 shorter events, 169.2 us)
Async XLA Ops:
  0.6 25.6 %collective-permute-start.2 = (bf16[48,2048]{1,0:T(8,128)(2,1)}, bf16[48,2048]{1,0:T(8,128)(2,1)S(1)}, u32[]{:S(2)}, u32[]{:S(2)}) collective-permute-start(bf16[48,2048]{1,0:T(8,128)(2,1)} %bitcast.194), channel_id=1, source_target_pairs={{0,3},{1,2},{2,1},{3,0},{4,7},{5,6},{6,5},{7,4},{8,11},{9,10},{10,... | collective-permute-start | bytes 589832 | tf_op jit(solution)/shard_map/ppermute | solution.py:51
  7.6 18.6 %collective-permute-start.1 = (bf16[48,2048]{1,0:T(8,128)(2,1)}, bf16[48,2048]{1,0:T(8,128)(2,1)}, u32[]{:S(2)}, u32[]{:S(2)}) collective-permute-start(bf16[48,2048]{1,0:T(8,128)(2,1)} %bitcast.195), channel_id=1, source_target_pairs={{0,2},{1,3},{2,0},{3,1},{4,6},{5,7},{6,4},{7,5},{8,10},{9,11},{10,... | collective-permute-start | bytes 589832 | tf_op jit(solution)/shard_map/ppermute | solution.py:51
  9.5 18.9 %collective-permute-start = (bf16[48,2048]{1,0:T(8,128)(2,1)}, bf16[48,2048]{1,0:T(8,128)(2,1)}, u32[]{:S(2)}, u32[]{:S(2)}) collective-permute-start(bf16[48,2048]{1,0:T(8,128)(2,1)} %bitcast.196), channel_id=1, source_target_pairs={{0,1},{1,0},{2,3},{3,2},{4,5},{5,4},{6,7},{7,6},{8,9},{9,8},{10,11... | collective-permute-start | bytes 589832 | tf_op jit(solution)/shard_map/ppermute | solution.py:51
  20.9 26.0 %collective-permute-start.3 = (bf16[2,128,1280]{2,1,0:T(8,128)(2,1)}, bf16[2,128,1280]{2,1,0:T(8,128)(2,1)}, u32[]{:S(2)}, u32[]{:S(2)}) collective-permute-start(bf16[2,128,1280]{2,1,0:T(8,128)(2,1)} %pad_maximum_fusion.11), channel_id=1, source_target_pairs={{0,1},{1,0},{2,3},{3,2},{4,5},{5,4},{6,7},{7,6},{8,9},{9,8},{10,11... | collective-permute-start | bytes 1966088 | tf_op jit(solution)/shard_map/ppermute | solution.py:51
  23.3 57.0 %collective-permute-start.7 = (bf16[2,128,1280]{2,1,0:T(8,128)(2,1)}, bf16[2,128,1280]{2,1,0:T(8,128)(2,1)}, u32[]{:S(2)}, u32[]{:S(2)}) collective-permute-start(bf16[2,128,1280]{2,1,0:T(8,128)(2,1)} %pad_maximum_fusion.12), channel_id=1, source_target_pairs={{0,2},{1,3},{2,0},{3,1},{4,6},{5,7},{6,4},{7,5},{8,10},{9,11},{10,... | collective-permute-start | bytes 1966088 | tf_op jit(solution)/shard_map/ppermute | solution.py:51
  47.9 18.5 %collective-permute-start.6 = (bf16[48,2048]{1,0:T(8,128)(2,1)}, bf16[48,2048]{1,0:T(8,128)(2,1)}, u32[]{:S(2)}, u32[]{:S(2)}) collective-permute-start(bf16[48,2048]{1,0:T(8,128)(2,1)} %get-tuple-element.106), channel_id=1, source_target_pairs={{0,3},{1,2},{2,1},{3,0},{4,7},{5,6},{6,5},{7,4},{8,11},{9,10},{10,... | collective-permute-start | bytes 589832 | tf_op jit(solution)/shard_map/ppermute | solution.py:51
  50.7 28.4 %collective-permute-start.5 = (bf16[48,2048]{1,0:T(8,128)(2,1)}, bf16[48,2048]{1,0:T(8,128)(2,1)}, u32[]{:S(2)}, u32[]{:S(2)}) collective-permute-start(bf16[48,2048]{1,0:T(8,128)(2,1)} %get-tuple-element.107), channel_id=1, source_target_pairs={{0,2},{1,3},{2,0},{3,1},{4,6},{5,7},{6,4},{7,5},{8,10},{9,11},{10,... | collective-permute-start | bytes 589832 | tf_op jit(solution)/shard_map/ppermute | solution.py:51
  52.7 26.3 %collective-permute-start.4 = (bf16[48,2048]{1,0:T(8,128)(2,1)}, bf16[48,2048]{1,0:T(8,128)(2,1)}, u32[]{:S(2)}, u32[]{:S(2)}) collective-permute-start(bf16[48,2048]{1,0:T(8,128)(2,1)} %get-tuple-element.105), channel_id=1, source_target_pairs={{0,1},{1,0},{2,3},{3,2},{4,5},{5,4},{6,7},{7,6},{8,9},{9,8},{10,11... | collective-permute-start | bytes 589832 | tf_op jit(solution)/shard_map/ppermute | solution.py:51
  58.9 30.2 %collective-permute-start.12 = (bf16[2,128,1280]{2,1,0:T(8,128)(2,1)}, bf16[2,128,1280]{2,1,0:T(8,128)(2,1)S(1)}, u32[]{:S(2)}, u32[]{:S(2)}) collective-permute-start(bf16[2,128,1280]{2,1,0:T(8,128)(2,1)} %pad_maximum_fusion.13), channel_id=1, source_target_pairs={{0,3},{1,2},{2,1},{3,0},{4,7},{5,6},{6,5},{7,4},{8,11},{9,10},{10,... | collective-permute-start | bytes 1966088 | tf_op jit(solution)/shard_map/ppermute | solution.py:51
  106.8 20.9 %collective-permute-start.21 = (bf16[192,1280]{1,0:T(8,128)(2,1)S(1)}, bf16[192,1280]{1,0:T(8,128)(2,1)S(1)}, u32[]{:S(2)}, u32[]{:S(2)}) collective-permute-start(bf16[192,1280]{1,0:T(8,128)(2,1)S(1)} %get-tuple-element.28), channel_id=1, source_target_pairs={{0,12},{1,13},{2,14},{3,15},{4,8},{5,9},{6,10},{7,11},{8,4},{9,5},... | collective-permute-start | bytes 1474568 | tf_op jit(solution)/shard_map/ppermute | solution.py:51
  130.0 35.3 %collective-permute-start.18 = (bf16[192,1280]{1,0:T(8,128)(2,1)S(1)}, bf16[192,1280]{1,0:T(8,128)(2,1)}, u32[]{:S(2)}, u32[]{:S(2)}) collective-permute-start(bf16[192,1280]{1,0:T(8,128)(2,1)S(1)} %get-tuple-element.52), channel_id=1, source_target_pairs={{0,12},{1,13},{2,14},{3,15},{4,8},{5,9},{6,10},{7,11},{8,4},{9,5},... | collective-permute-start | bytes 1474568 | tf_op jit(solution)/shard_map/ppermute | solution.py:51
  133.0 32.3 %collective-permute-start.17 = (bf16[192,1280]{1,0:T(8,128)(2,1)S(1)}, bf16[192,1280]{1,0:T(8,128)(2,1)}, u32[]{:S(2)}, u32[]{:S(2)}) collective-permute-start(bf16[192,1280]{1,0:T(8,128)(2,1)S(1)} %get-tuple-element.53), channel_id=1, source_target_pairs={{0,8},{1,9},{2,10},{3,11},{4,12},{5,13},{6,14},{7,15},{8,0},{9,1},... | collective-permute-start | bytes 1474568 | tf_op jit(solution)/shard_map/ppermute | solution.py:51
  133.0 32.3 %collective-permute-start.16 = (bf16[192,1280]{1,0:T(8,128)(2,1)S(1)}, bf16[192,1280]{1,0:T(8,128)(2,1)}, u32[]{:S(2)}, u32[]{:S(2)}) collective-permute-start(bf16[192,1280]{1,0:T(8,128)(2,1)S(1)} %get-tuple-element.51), channel_id=1, source_target_pairs={{0,4},{1,5},{2,6},{3,7},{4,0},{5,1},{6,2},{7,3},{8,12},{9,13},{10,... | collective-permute-start | bytes 1474568 | tf_op jit(solution)/shard_map/ppermute | solution.py:51
  134.3 29.5 %collective-permute-start.23 = (bf16[192,512]{1,0:T(8,128)(2,1)}, bf16[192,512]{1,0:T(8,128)(2,1)}, u32[]{:S(2)}, u32[]{:S(2)}) collective-permute-start(bf16[192,512]{1,0:T(8,128)(2,1)} %get-tuple-element.99), channel_id=1, source_target_pairs={{0,8},{1,9},{2,10},{3,11},{4,12},{5,13},{6,14},{7,15},{8,0},{9,1},... | collective-permute-start | bytes 589832 | tf_op jit(solution)/shard_map/ppermute | solution.py:51
  136.6 27.3 %collective-permute-start.22 = (bf16[192,512]{1,0:T(8,128)(2,1)}, bf16[192,512]{1,0:T(8,128)(2,1)}, u32[]{:S(2)}, u32[]{:S(2)}) collective-permute-start(bf16[192,512]{1,0:T(8,128)(2,1)} %get-tuple-element.100), channel_id=1, source_target_pairs={{0,4},{1,5},{2,6},{3,7},{4,0},{5,1},{6,2},{7,3},{8,12},{9,13},{10,... | collective-permute-start | bytes 589832 | tf_op jit(solution)/shard_map/ppermute | solution.py:51
  171.1 15.1 %collective-permute-start.27 = (bf16[48,2048]{1,0:T(8,128)(2,1)S(1)}, bf16[48,2048]{1,0:T(8,128)(2,1)S(1)}, u32[]{:S(2)}, u32[]{:S(2)}) collective-permute-start(bf16[48,2048]{1,0:T(8,128)(2,1)S(1)} %get-tuple-element.91), channel_id=1, source_target_pairs={{0,3},{1,2},{2,1},{3,0},{4,7},{5,6},{6,5},{7,4},{8,11},{9,10},{10,... | collective-permute-start | bytes 589832 | tf_op jit(solution)/shard_map/ppermute | solution.py:51
  173.6 16.6 %collective-permute-start.26 = (bf16[48,2048]{1,0:T(8,128)(2,1)S(1)}, bf16[48,2048]{1,0:T(8,128)(2,1)S(1)}, u32[]{:S(2)}, u32[]{:S(2)}) collective-permute-start(bf16[48,2048]{1,0:T(8,128)(2,1)S(1)} %get-tuple-element.92), channel_id=1, source_target_pairs={{0,2},{1,3},{2,0},{3,1},{4,6},{5,7},{6,4},{7,5},{8,10},{9,11},{10,... | collective-permute-start | bytes 589832 | tf_op jit(solution)/shard_map/ppermute | solution.py:51
  257.4 14.6 %collective-permute-start.46 = (bf16[48,2048]{1,0:T(8,128)(2,1)S(1)}, bf16[48,2048]{1,0:T(8,128)(2,1)S(1)}, u32[]{:S(2)}, u32[]{:S(2)}) collective-permute-start(bf16[48,2048]{1,0:T(8,128)(2,1)S(1)} %fusion.137), channel_id=1, source_target_pairs={{0,3},{1,2},{2,1},{3,0},{4,7},{5,6},{6,5},{7,4},{8,11},{9,10},{10,... | collective-permute-start | bytes 589832 | tf_op jit(solution)/shard_map/ppermute | solution.py:51
  286.2 15.2 %collective-permute-start.58 = (bf16[128,1280]{1,0:T(8,128)(2,1)S(1)}, bf16[128,1280]{1,0:T(8,128)(2,1)S(1)}, u32[]{:S(2)}, u32[]{:S(2)}) collective-permute-start(bf16[128,1280]{1,0:T(8,128)(2,1)S(1)} %get-tuple-element.59), channel_id=1, source_target_pairs={{0,3},{1,2},{2,1},{3,0},{4,7},{5,6},{6,5},{7,4},{8,11},{9,10},{10,... | collective-permute-start | bytes 983048 | tf_op jit(solution)/shard_map/ppermute | solution.py:51
  288.2 36.5 %collective-permute-start.57 = (bf16[128,1280]{1,0:T(8,128)(2,1)S(1)}, bf16[128,1280]{1,0:T(8,128)(2,1)S(1)}, u32[]{:S(2)}, u32[]{:S(2)}) collective-permute-start(bf16[128,1280]{1,0:T(8,128)(2,1)S(1)} %get-tuple-element.60), channel_id=1, source_target_pairs={{0,2},{1,3},{2,0},{3,1},{4,6},{5,7},{6,4},{7,5},{8,10},{9,11},{10,... | collective-permute-start | bytes 983048 | tf_op jit(solution)/shard_map/ppermute | solution.py:51
  290.9 33.8 %collective-permute-start.56 = (bf16[128,1280]{1,0:T(8,128)(2,1)S(1)}, bf16[128,1280]{1,0:T(8,128)(2,1)S(1)}, u32[]{:S(2)}, u32[]{:S(2)}) collective-permute-start(bf16[128,1280]{1,0:T(8,128)(2,1)S(1)} %get-tuple-element.61), channel_id=1, source_target_pairs={{0,1},{1,0},{2,3},{3,2},{4,5},{5,4},{6,7},{7,6},{8,9},{9,8},{10,11... | collective-permute-start | bytes 983048 | tf_op jit(solution)/shard_map/ppermute | solution.py:51
  297.5 27.5 %collective-permute-start.52 = (bf16[128,1280]{1,0:T(8,128)(2,1)S(1)}, bf16[128,1280]{1,0:T(8,128)(2,1)S(1)}, u32[]{:S(2)}, u32[]{:S(2)}) collective-permute-start(bf16[128,1280]{1,0:T(8,128)(2,1)S(1)} %get-tuple-element.67), channel_id=1, source_target_pairs={{0,3},{1,2},{2,1},{3,0},{4,7},{5,6},{6,5},{7,4},{8,11},{9,10},{10,... | collective-permute-start | bytes 983048 | tf_op jit(solution)/shard_map/ppermute | solution.py:51
  299.4 33.0 %collective-permute-start.51 = (bf16[128,1280]{1,0:T(8,128)(2,1)S(1)}, bf16[128,1280]{1,0:T(8,128)(2,1)S(1)}, u32[]{:S(2)}, u32[]{:S(2)}) collective-permute-start(bf16[128,1280]{1,0:T(8,128)(2,1)S(1)} %get-tuple-element.68), channel_id=1, source_target_pairs={{0,2},{1,3},{2,0},{3,1},{4,6},{5,7},{6,4},{7,5},{8,10},{9,11},{10,... | collective-permute-start | bytes 983048 | tf_op jit(solution)/shard_map/ppermute | solution.py:51
  301.4 31.0 %collective-permute-start.50 = (bf16[128,1280]{1,0:T(8,128)(2,1)S(1)}, bf16[128,1280]{1,0:T(8,128)(2,1)S(1)}, u32[]{:S(2)}, u32[]{:S(2)}) collective-permute-start(bf16[128,1280]{1,0:T(8,128)(2,1)S(1)} %get-tuple-element.69), channel_id=1, source_target_pairs={{0,1},{1,0},{2,3},{3,2},{4,5},{5,4},{6,7},{7,6},{8,9},{9,8},{10,11... | collective-permute-start | bytes 983048 | tf_op jit(solution)/shard_map/ppermute | solution.py:51
  (69 other events, 676.6 us)

commit v4 on v3

--- a/solution.py
+++ b/solution.py
@@ -78,10 +78,13 @@
     return total
 
 
-def task_partners(value_of):
+def task_partners(value_of, section=None):
+    def route(k):
+        return lambda s, t, f: (s, t ^ k, f) if section in (None, s) else None
+
     parts = [value_of(0)]
     for k in range(1, lax.axis_size("task")):
-        parts.append(send(value_of(k), lambda s, t, f, k=k: (s, t ^ k, f)))
+        parts.append(send(value_of(k), route(k)))
     return parts
 
 
@@ -175,7 +178,11 @@
 
     pieces = fsdp_partners(direction_for)
 
+    def features_for(array):
+        return lambda k: lax.dynamic_slice_in_dim(array, (task_id ^ k) * block, block, 1)
+
     own_inputs = [states[0]]
+    early = []
     rows_all = gather_rows(states[0], 0, 0)
     for layer in range(sections):
         normed = normalize(rows_all.astype(jnp.float32))
@@ -184,29 +191,38 @@
         acted, slope = jax.jvp(gelu_tanh, (preact,), (jnp.ones_like(preact),))
         acted_b = acted.astype(jnp.bfloat16)
         if layer + 1 < sections:
+            early.append(
+                task_partners(
+                    lambda k: jnp.concatenate([features_for(normed_b)(k), acted_b], axis=1), layer
+                )
+            )
             mixed = across_hidden(acted_b, w_out)
             if layer == 0:
                 mixed, pieces[1] = tie(mixed, pieces[1])
             mixed = scatter_sum(mixed, layer, 0)
             own_rows = (own_inputs[layer].astype(jnp.float32) + mixed).astype(jnp.bfloat16)
             if layer == 0:
-                own_rows, pieces[2] = tie(own_rows, pieces[2])
+                own_rows, (pieces[2], resid_apart) = tie(own_rows, (pieces[2], resid_apart))
+            own_rows, early[layer] = tie(own_rows, early[layer])
             own_inputs.append(own_rows)
             arrived = gather_rows(own_rows, 0, layer + 1)
             if layer == 0:
-                arrived, (pieces[3], resid_apart) = tie(arrived, (pieces[3], resid_apart))
+                arrived, pieces[3] = tie(arrived, pieces[3])
             rows_all = jnp.where(section_id == layer + 1, arrived, rows_all)
 
     steering = in_order(pieces, shard_id, 1)
     steer_in, steer_out = steering[0], steering[1]
 
-    def features_for(array):
-        return lambda k: lax.dynamic_slice_in_dim(array, (task_id ^ k) * block, block, 1)
-
-    normed_parts = task_partners(features_for(normed_b))
+    normed_parts = task_partners(features_for(normed_b), sections - 1)
     acted_b, normed_parts = tie(acted_b, normed_parts)
+    acted_parts = task_partners(lambda k: acted_b, sections - 1)
+    for layer in range(sections - 1):
+        for k in range(1, tasks):
+            here = section_id == layer
+            normed_parts[k] = jnp.where(here, early[layer][k][:, :block], normed_parts[k])
+            acted_parts[k] = jnp.where(here, early[layer][k][:, block:], acted_parts[k])
     normed_tasks = jnp.concatenate(normed_parts, axis=0)
-    acted_tasks = jnp.concatenate(task_partners(lambda k: acted_b), axis=0)
+    acted_tasks = jnp.concatenate(acted_parts, axis=0)
     steered_parts = dot(normed_tasks, steer_in).reshape(tasks, joined, hidden)
     steered = task_partners(
         lambda k: steered_parts[k] if k == 0 else steered_parts[k].astype(jnp.bfloat16)

time: 373 us -> 360 us (0.965)
  waiting for transfers between devices: 137 us -> 111 us
  starting transfers between devices: 128 us -> 147 us
  other arithmetic: 20 us -> 15.4 us
    ppermute x59 -> x62, waiting for transfers between devices: 131 us -> 105 us  [send(): return lax.ppermute(value, ALL, pairs)]
    ppermute x59 -> x62, starting transfers between devices: 121 us -> 140 us  [send(): return lax.ppermute(value, ALL, pairs)]
    dot_general x3 -> x4, matrix products: 11.7 us -> 13 us  [dot(): return jnp.dot(left_side, right_side, preferred_element_type=jnp.float32)]
    unnamed x60 -> x72, local copies, waits for them, and re-layouts: 8.07 us -> 8.58 us
  transfers between devices with their start and end apart: 66 -> 69, of which waited for: 35 -> 30; matrix products, arithmetic and copies ran while one was open for 12% -> 11% of each run, Pallas kernels for 0% -> 0%
where the time goes in v4:
time: 360 us; the launch traced here: 358 us
  starting transfers between devices  147 us (41%)
  waiting for transfers between devices  111 us (31%)
  matrix products  42.8 us (12%)
  local copies, waits for them, and re-layouts  24 us (7%)
  other arithmetic  15.4 us (4%)
  between operations  10.7 us (3%)
  Pallas kernels  7.69 us (2%)
    ppermute x62, starting transfers between devices, send(): return lax.ppermute(value, ALL, pairs)  140 us
    ppermute x62, waiting for transfers between devices, send(): return lax.ppermute(value, ALL, pairs)  105 us
    dot_general x5, matrix products, across_hidden(): lax.dot_general(left_side, right_side, (((1,), (1,)), ((), ())), preferre...  27.4 us
    dot_general x4, matrix products, dot(): return jnp.dot(left_side, right_side, preferred_element_type=jnp.float32)  13 us
    transpose x2, local copies, waits for them, and re-layouts, apart(): jnp.transpose(array, (1, 0, 2))  10.7 us
    unnamed x72, local copies, waits for them, and re-layouts  8.58 us
    pallas_call x1, Pallas kernels, update(): pl.pallas_call(update_kernel, grid=(total // columns,), in_specs=[pl.Bloc...  7.69 us
  transfers between devices with their start and end apart: 69, of which 30 were waited for; matrix products, arithmetic and copies ran while one was open for 11% of the time, Pallas kernels for 0%

profile of v4, /device:TPU:0, one launch (start us, length us, event | category | flops | bytes accessed | tf_op | source)
XLA Modules:
  0.0 358.2 jit_solution(12756842989438359197)
XLA Ops:
  0.6 7.0 %collective-permute-start.2 = (bf16[48,2048]{1,0:T(8,128)(2,1)}, bf16[48,2048]{1,0:T(8,128)(2,1)S(1)}, u32[]{:S(2)}, u32[]{:S(2)}) collective-permute-start(bf16[48,2048]{1,0:T(8,128)(2,1)} %bitcast.190), channel_id=1, source_target_pairs={{0,3},{1,2},{2,1},{3,0},{4,7},{5,6},{6,5},{7,4},{8,11},{9,10},{10,... | collective-permute-start | bytes 589832 | tf_op jit(solution)/shard_map/ppermute | solution.py:51
  25.4 6.6 %copy.9 = f32[2,128,5120]{2,1,0:T(8,128)} copy(f32[2,128,5120]{2,0,1:T(2,128)} %bitcast.182) | data formatting | bytes 10485760 | tf_op jit(solution)/shard_map/transpose | solution.py:150
  36.3 4.5 %fusion.8 = f32[192,2048]{1,0:T(8,128)S(1)} fusion(bf16[192,1280]{1,0:T(8,128)(2,1)S(1)} %fusion.106, bf16[1,1,2,2048,1280]{4,3,2,1,0:T(8,128)(2,1)} %param.6), kind=kOutput, calls=%fused_computation.8 | convolution fusion | flops 1006632960 | bytes 7307264 | tf_op jit(solution)/shard_map/dot_general | solution.py:24
  40.8 5.3 %collective-permute-done.3 = bf16[2,128,1280]{2,1,0:T(8,128)(2,1)S(1)} collective-permute-done((bf16[2,128,1280]{2,1,0:T(8,128)(2,1)S(1)}, bf16[2,128,1280]{2,1,0:T(8,128)(2,1)S(1)}, u32[]{:S(2)}, u32[]{:S(2)}) %collective-permute-start.3) | collective-permute-done | bytes 655392 | tf_op jit(solution)/shard_map/ppermute | solution.py:51
  46.9 5.7 %collective-permute-start.6 = (bf16[48,2048]{1,0:T(8,128)(2,1)S(1)}, bf16[48,2048]{1,0:T(8,128)(2,1)S(1)}, u32[]{:S(2)}, u32[]{:S(2)}) collective-permute-start(bf16[48,2048]{1,0:T(8,128)(2,1)S(1)} %get-tuple-element.117), channel_id=1, source_target_pairs={{0,3},{1,2},{2,1},{3,0},{4,7},{5,6},{6,5},{7,4},{8,11},{9,10},{10,... | collective-permute-start | bytes 589832 | tf_op jit(solution)/shard_map/ppermute | solution.py:51
  64.1 7.8 %collective-permute-done.5 = bf16[48,2048]{1,0:T(8,128)(2,1)S(1)} collective-permute-done((bf16[48,2048]{1,0:T(8,128)(2,1)S(1)}, bf16[48,2048]{1,0:T(8,128)(2,1)S(1)}, u32[]{:S(2)}, u32[]{:S(2)}) %collective-permute-start.5) | collective-permute-done | bytes 196640 | tf_op jit(solution)/shard_map/ppermute | solution.py:51
  74.6 4.8 %collective-permute-done.4 = bf16[48,2048]{1,0:T(8,128)(2,1)S(1)} collective-permute-done((bf16[48,2048]{1,0:T(8,128)(2,1)S(1)}, bf16[48,2048]{1,0:T(8,128)(2,1)S(1)}, u32[]{:S(2)}, u32[]{:S(2)}) %collective-permute-start.4) | collective-permute-done | bytes 196640 | tf_op jit(solution)/shard_map/ppermute | solution.py:51
  87.9 4.8 %collective-permute-done.14 = bf16[48,2048]{1,0:T(8,128)(2,1)S(1)} collective-permute-done((bf16[48,2048]{1,0:T(8,128)(2,1)S(1)}, bf16[48,2048]{1,0:T(8,128)(2,1)S(1)}, u32[]{:S(2)}, u32[]{:S(2)}) %collective-permute-start.14) | collective-permute-done | bytes 196640 | tf_op jit(solution)/shard_map/ppermute | solution.py:51
  119.9 20.0 %collective-permute-done.26 = bf16[192,512]{1,0:T(8,128)(2,1)} collective-permute-done((bf16[192,512]{1,0:T(8,128)(2,1)}, bf16[192,512]{1,0:T(8,128)(2,1)}, u32[]{:S(2)}, u32[]{:S(2)}) %collective-permute-start.26) | collective-permute-done | bytes 196640 | tf_op jit(solution)/shard_map/ppermute | solution.py:51
  141.3 5.6 %fusion.156 = (bf16[192,2048]{1,0:T(8,128)(2,1)S(1)}, f32[192,2048]{1,0:T(8,128)S(1)}) fusion(bf16[192,512]{1,0:T(8,128)(2,1)S(1)} %get-tuple-element.102, bf16[192,512]{1,0:T(8,128)(2,1)S(1)} %get-tuple-element.103, bf16[192,512]{1,0:T(8,128)(2,1)S(1)} %get-tuple-element.104, bf16[192,512]{1,0:T(8,128)(2,1)S(1)} %get-tuple-element.101, ...), kind=kOutput, calls=%fused_computation.233 | convolution fusion | flops 1016463360 | bytes 11829248 | tf_op jit(solution)/shard_map/dot_general | solution.py:24
  147.0 4.4 %collective-permute-start.30 = (bf16[48,2048]{1,0:T(8,128)(2,1)S(1)}, bf16[48,2048]{1,0:T(8,128)(2,1)S(1)}, u32[]{:S(2)}, u32[]{:S(2)}) collective-permute-start(bf16[48,2048]{1,0:T(8,128)(2,1)S(1)} %get-tuple-element.99), channel_id=1, source_target_pairs={{0,3},{1,2},{2,1},{3,0},{4,7},{5,6},{6,5},{7,4},{8,11},{9,10},{10,... | collective-permute-start | bytes 589832 | tf_op jit(solution)/shard_map/ppermute | solution.py:51
  151.4 11.5 %collective-permute-start.29 = (bf16[48,2048]{1,0:T(8,128)(2,1)S(1)}, bf16[48,2048]{1,0:T(8,128)(2,1)S(1)}, u32[]{:S(2)}, u32[]{:S(2)}) collective-permute-start(bf16[48,2048]{1,0:T(8,128)(2,1)S(1)} %get-tuple-element.100), channel_id=1, source_target_pairs={{0,2},{1,3},{2,0},{3,1},{4,6},{5,7},{6,4},{7,5},{8,10},{9,11},{10,... | collective-permute-start | bytes 589832 | tf_op jit(solution)/shard_map/ppermute | solution.py:51
  171.1 7.6 %collective-permute-start.34 = (bf16[48,2048]{1,0:T(8,128)(2,1)S(1)}, bf16[48,2048]{1,0:T(8,128)(2,1)S(1)}, u32[]{:S(2)}, u32[]{:S(2)}) collective-permute-start(bf16[48,2048]{1,0:T(8,128)(2,1)S(1)} %fusion.130), channel_id=1, source_target_pairs={{0,19},{1,18},{2,17},{3,16},{4,23},{5,22},{6,21},{7,20},{8,27},{9,... | collective-permute-start | bytes 589832 | tf_op jit(solution)/shard_map/ppermute | solution.py:51
  187.2 8.8 %fusion.57 = bf16[192,2048]{1,0:T(8,128)(2,1)S(1)} fusion(bf16[1,1,2,2048,1280]{4,3,2,1,0:T(8,128)(2,1)} %param.6, bf16[192,2048]{1,0:T(8,128)(2,1)S(1)} %get-tuple-element.52, f32[192]{0:T(256)S(1)} %multiply_multiply_fusion.3, f32[192]{0:T(256)S(1)} %fusion.134, bf16[48,2048]{1,0:T(8,128)(2,1)} %copy-done.20, bf16[48,2048]{1,0:T(8,128)(2,1)} %copy-done.21, ...), kind=kOutput, calls=%fused_computation.58 | convolution fusion | flops 2028453888 | bytes 17073664 | tf_op jit(solution)/shard_map/dot_general | solution.py:24
  201.3 5.1 %collective-permute-done.38 = bf16[48,2048]{1,0:T(8,128)(2,1)S(1)} collective-permute-done((bf16[48,2048]{1,0:T(8,128)(2,1)S(1)}, bf16[48,2048]{1,0:T(8,128)(2,1)S(1)}, u32[]{:S(2)}, u32[]{:S(2)}) %collective-permute-start.38) | collective-permute-done | bytes 196640 | tf_op jit(solution)/shard_map/ppermute | solution.py:51
  206.4 5.7 %collective-permute-done.37 = bf16[48,2048]{1,0:T(8,128)(2,1)S(1)} collective-permute-done((bf16[48,2048]{1,0:T(8,128)(2,1)S(1)}, bf16[48,2048]{1,0:T(8,128)(2,1)S(1)}, u32[]{:S(2)}, u32[]{:S(2)}) %collective-permute-start.37) | collective-permute-done | bytes 196640 | tf_op jit(solution)/shard_map/ppermute | solution.py:51
  221.0 7.4 %fusion.54 = bf16[192,2048]{1,0:T(8,128)(2,1)S(1)} fusion(bf16[1,1,2,2048,1280]{4,3,2,1,0:T(8,128)(2,1)} %param.6, bf16[48,2048]{1,0:T(8,128)(2,1)S(1)} %collective-permute-done.42, bf16[48,2048]{1,0:T(8,128)(2,1)S(1)} %collective-permute-done.41, bf16[48,2048]{1,0:T(8,128)(2,1)S(1)} %collective-permute-done.40, ...), kind=kOutput, calls=%fused_computation.57 | convolution fusion | flops 2021621760 | bytes 13041665 | tf_op jit(solution)/shard_map/dot_general | solution.py:24
  238.0 5.7 %collective-permute-done.45 = bf16[48,2048]{1,0:T(8,128)(2,1)S(1)} collective-permute-done((bf16[48,2048]{1,0:T(8,128)(2,1)S(1)}, bf16[48,2048]{1,0:T(8,128)(2,1)S(1)}, u32[]{:S(2)}, u32[]{:S(2)}) %collective-permute-start.45) | collective-permute-done | bytes 196640 | tf_op jit(solution)/shard_map/ppermute | solution.py:51
  249.7 4.6 %collective-permute-start.47 = (bf16[48,2048]{1,0:T(8,128)(2,1)S(1)}, bf16[48,2048]{1,0:T(8,128)(2,1)S(1)}, u32[]{:S(2)}, u32[]{:S(2)}) collective-permute-start(bf16[48,2048]{1,0:T(8,128)(2,1)S(1)} %fusion.127), channel_id=1, source_target_pairs={{0,1},{1,0},{2,3},{3,2},{4,5},{5,4},{6,7},{7,6},{8,9},{9,8},{10,11... | collective-permute-start | bytes 589832 | tf_op jit(solution)/shard_map/ppermute | solution.py:51
  254.3 4.5 %multiply_reduce_fusion = f32[]{:T(128)} fusion(f32[2,128,5120]{2,1,0:T(8,128)} %copy.9), kind=kLoop, calls=%fused_computation.18 | loop fusion | flops 2621439 | bytes 5242884 | tf_op jit(solution)/shard_map/reduce_sum | solution.py:277
  288.6 11.3 %collective-permute-start.53 = (bf16[128,1280]{1,0:T(8,128)(2,1)S(1)}, bf16[128,1280]{1,0:T(8,128)(2,1)S(1)}, u32[]{:S(2)}, u32[]{:S(2)}) collective-permute-start(bf16[128,1280]{1,0:T(8,128)(2,1)S(1)} %get-tuple-element.77), channel_id=1, source_target_pairs={{0,1},{1,0},{2,3},{3,2},{4,5},{5,4},{6,7},{7,6},{8,9},{9,8},{10,11... | collective-permute-start | bytes 983048 | tf_op jit(solution)/shard_map/ppermute | solution.py:51
  299.9 11.7 %collective-permute-done.60 = bf16[128,1280]{1,0:T(8,128)(2,1)S(1)} collective-permute-done((bf16[128,1280]{1,0:T(8,128)(2,1)S(1)}, bf16[128,1280]{1,0:T(8,128)(2,1)S(1)}, u32[]{:S(2)}, u32[]{:S(2)}) %collective-permute-start.60) | collective-permute-done | bytes 327712 | tf_op jit(solution)/shard_map/ppermute | solution.py:51
  311.9 7.5 %collective-permute-done.54 = bf16[128,1280]{1,0:T(8,128)(2,1)S(1)} collective-permute-done((bf16[128,1280]{1,0:T(8,128)(2,1)S(1)}, bf16[128,1280]{1,0:T(8,128)(2,1)S(1)}, u32[]{:S(2)}, u32[]{:S(2)}) %collective-permute-start.54) | collective-permute-done | bytes 327712 | tf_op jit(solution)/shard_map/ppermute | solution.py:51
  349.4 7.7 %shard_map.76 = (f32[128,2,5120]{2,1,0:T(2,128)}, f32[128,2,5120]{2,1,0:T(2,128)}) custom-call(f32[2]{0:T(128)S(1)} %pad_maximum_fusion.26.scalars, bf16[128,5120]{1,0:T(8,128)(2,1)S(1)} %get-tuple-element.49.in_ref, bf16[128,5120]{1,0:T(8,128)(2,1)S(1)} %get-tuple-element.50.out_ref, f32[128,2,5120]{2,1,0:T(2,128)S(1)} %bitcast.183, ...), custom_call_target="tpu_custom_call" | custom-call | flops 5242880 | bytes 26214400 | tf_op jit(solution)/shard_map/pallas_call | solution.py:136
  (262 shorter events, 172.0 us)
Async XLA Ops:
  0.6 31.3 %collective-permute-start.2 = (bf16[48,2048]{1,0:T(8,128)(2,1)}, bf16[48,2048]{1,0:T(8,128)(2,1)S(1)}, u32[]{:S(2)}, u32[]{:S(2)}) collective-permute-start(bf16[48,2048]{1,0:T(8,128)(2,1)} %bitcast.190), channel_id=1, source_target_pairs={{0,3},{1,2},{2,1},{3,0},{4,7},{5,6},{6,5},{7,4},{8,11},{9,10},{10,... | collective-permute-start | bytes 589832 | tf_op jit(solution)/shard_map/ppermute | solution.py:51
  7.6 24.4 %collective-permute-start.1 = (bf16[48,2048]{1,0:T(8,128)(2,1)}, bf16[48,2048]{1,0:T(8,128)(2,1)S(1)}, u32[]{:S(2)}, u32[]{:S(2)}) collective-permute-start(bf16[48,2048]{1,0:T(8,128)(2,1)} %bitcast.191), channel_id=1, source_target_pairs={{0,2},{1,3},{2,0},{3,1},{4,6},{5,7},{6,4},{7,5},{8,10},{9,11},{10,... | collective-permute-start | bytes 589832 | tf_op jit(solution)/shard_map/ppermute | solution.py:51
  9.5 22.4 %collective-permute-start = (bf16[48,2048]{1,0:T(8,128)(2,1)}, bf16[48,2048]{1,0:T(8,128)(2,1)S(1)}, u32[]{:S(2)}, u32[]{:S(2)}) collective-permute-start(bf16[48,2048]{1,0:T(8,128)(2,1)} %bitcast.192), channel_id=1, source_target_pairs={{0,1},{1,0},{2,3},{3,2},{4,5},{5,4},{6,7},{7,6},{8,9},{9,8},{10,11... | collective-permute-start | bytes 589832 | tf_op jit(solution)/shard_map/ppermute | solution.py:51
  20.1 26.0 %collective-permute-start.3 = (bf16[2,128,1280]{2,1,0:T(8,128)(2,1)S(1)}, bf16[2,128,1280]{2,1,0:T(8,128)(2,1)S(1)}, u32[]{:S(2)}, u32[]{:S(2)}) collective-permute-start(bf16[2,128,1280]{2,1,0:T(8,128)(2,1)S(1)} %pad_maximum_fusion.16), channel_id=1, source_target_pairs={{0,1},{1,0},{2,3},{3,2},{4,5},{5,4},{6,7},{7,6},{8,9},{9,8},{10,11... | collective-permute-start | bytes 1966088 | tf_op jit(solution)/shard_map/ppermute | solution.py:51
  22.5 60.0 %collective-permute-start.7 = (bf16[2,128,1280]{2,1,0:T(8,128)(2,1)}, bf16[2,128,1280]{2,1,0:T(8,128)(2,1)}, u32[]{:S(2)}, u32[]{:S(2)}) collective-permute-start(bf16[2,128,1280]{2,1,0:T(8,128)(2,1)} %pad_maximum_fusion.17), channel_id=1, source_target_pairs={{0,2},{1,3},{2,0},{3,1},{4,6},{5,7},{6,4},{7,5},{8,10},{9,11},{10,... | collective-permute-start | bytes 1966088 | tf_op jit(solution)/shard_map/ppermute | solution.py:51
  46.9 14.8 %collective-permute-start.6 = (bf16[48,2048]{1,0:T(8,128)(2,1)S(1)}, bf16[48,2048]{1,0:T(8,128)(2,1)S(1)}, u32[]{:S(2)}, u32[]{:S(2)}) collective-permute-start(bf16[48,2048]{1,0:T(8,128)(2,1)S(1)} %get-tuple-element.117), channel_id=1, source_target_pairs={{0,3},{1,2},{2,1},{3,0},{4,7},{5,6},{6,5},{7,4},{8,11},{9,10},{10,... | collective-permute-start | bytes 589832 | tf_op jit(solution)/shard_map/ppermute | solution.py:51
  52.6 19.3 %collective-permute-start.5 = (bf16[48,2048]{1,0:T(8,128)(2,1)S(1)}, bf16[48,2048]{1,0:T(8,128)(2,1)S(1)}, u32[]{:S(2)}, u32[]{:S(2)}) collective-permute-start(bf16[48,2048]{1,0:T(8,128)(2,1)S(1)} %get-tuple-element.118), channel_id=1, source_target_pairs={{0,2},{1,3},{2,0},{3,1},{4,6},{5,7},{6,4},{7,5},{8,10},{9,11},{10,... | collective-permute-start | bytes 589832 | tf_op jit(solution)/shard_map/ppermute | solution.py:51
  54.7 27.8 %collective-permute-start.8 = (bf16[192,1792]{1,0:T(8,128)(2,1)S(1)}, bf16[192,1792]{1,0:T(8,128)(2,1)S(1)}, u32[]{:S(2)}, u32[]{:S(2)}) collective-permute-start(bf16[192,1792]{1,0:T(8,128)(2,1)S(1)} %get-tuple-element.121), channel_id=1, source_target_pairs={{0,4},{1,5},{2,6},{3,7},{4,0},{5,1},{6,2},{7,3},{8,12},{9,13},{10,... | collective-permute-start | bytes 2064392 | tf_op jit(solution)/shard_map/ppermute | solution.py:51
  58.2 24.3 %collective-permute-start.9 = (bf16[192,1792]{1,0:T(8,128)(2,1)S(1)}, bf16[192,1792]{1,0:T(8,128)(2,1)S(1)}, u32[]{:S(2)}, u32[]{:S(2)}) collective-permute-start(bf16[192,1792]{1,0:T(8,128)(2,1)S(1)} %get-tuple-element.120), channel_id=1, source_target_pairs={{0,8},{1,9},{2,10},{3,11},{4,12},{5,13},{6,14},{7,15},{8,0},{9,1},... | collective-permute-start | bytes 2064392 | tf_op jit(solution)/shard_map/ppermute | solution.py:51
  61.7 20.9 %collective-permute-start.10 = (bf16[192,1792]{1,0:T(8,128)(2,1)S(1)}, bf16[192,1792]{1,0:T(8,128)(2,1)S(1)}, u32[]{:S(2)}, u32[]{:S(2)}) collective-permute-start(bf16[192,1792]{1,0:T(8,128)(2,1)S(1)} %get-tuple-element.119), channel_id=1, source_target_pairs={{0,12},{1,13},{2,14},{3,15},{4,8},{5,9},{6,10},{7,11},{8,4},{9,5},... | collective-permute-start | bytes 2064392 | tf_op jit(solution)/shard_map/ppermute | solution.py:51
  79.4 17.5 %collective-permute-start.15 = (bf16[2,128,1280]{2,1,0:T(8,128)(2,1)S(1)}, bf16[2,128,1280]{2,1,0:T(8,128)(2,1)S(1)}, u32[]{:S(2)}, u32[]{:S(2)}) collective-permute-start(bf16[2,128,1280]{2,1,0:T(8,128)(2,1)S(1)} %pad_maximum_fusion.18), channel_id=1, source_target_pairs={{0,3},{1,2},{2,1},{3,0},{4,7},{5,6},{6,5},{7,4},{8,11},{9,10},{10,... | collective-permute-start | bytes 1966088 | tf_op jit(solution)/shard_map/ppermute | solution.py:51
  115.0 26.2 %collective-permute-start.21 = (bf16[192,1280]{1,0:T(8,128)(2,1)}, bf16[192,1280]{1,0:T(8,128)(2,1)}, u32[]{:S(2)}, u32[]{:S(2)}) collective-permute-start(bf16[192,1280]{1,0:T(8,128)(2,1)} %get-tuple-element.60), channel_id=1, source_target_pairs={{0,12},{1,13},{2,14},{3,15},{4,8},{5,9},{6,10},{7,11},{8,4},{9,5},... | collective-permute-start | bytes 1474568 | tf_op jit(solution)/shard_map/ppermute | solution.py:51
  115.5 25.8 %collective-permute-start.20 = (bf16[192,1280]{1,0:T(8,128)(2,1)S(1)}, bf16[192,1280]{1,0:T(8,128)(2,1)}, u32[]{:S(2)}, u32[]{:S(2)}) collective-permute-start(bf16[192,1280]{1,0:T(8,128)(2,1)S(1)} %get-tuple-element.61), channel_id=1, source_target_pairs={{0,8},{1,9},{2,10},{3,11},{4,12},{5,13},{6,14},{7,15},{8,0},{9,1},... | collective-permute-start | bytes 1474568 | tf_op jit(solution)/shard_map/ppermute | solution.py:51
  117.0 24.2 %collective-permute-start.19 = (bf16[192,1280]{1,0:T(8,128)(2,1)S(1)}, bf16[192,1280]{1,0:T(8,128)(2,1)}, u32[]{:S(2)}, u32[]{:S(2)}) collective-permute-start(bf16[192,1280]{1,0:T(8,128)(2,1)S(1)} %get-tuple-element.59), channel_id=1, source_target_pairs={{0,4},{1,5},{2,6},{3,7},{4,0},{5,1},{6,2},{7,3},{8,12},{9,13},{10,... | collective-permute-start | bytes 1474568 | tf_op jit(solution)/shard_map/ppermute | solution.py:51
  118.5 21.4 %collective-permute-start.26 = (bf16[192,512]{1,0:T(8,128)(2,1)}, bf16[192,512]{1,0:T(8,128)(2,1)}, u32[]{:S(2)}, u32[]{:S(2)}) collective-permute-start(bf16[192,512]{1,0:T(8,128)(2,1)} %get-tuple-element.107), channel_id=1, source_target_pairs={{0,8},{1,9},{2,10},{3,11},{4,12},{5,13},{6,14},{7,15},{8,0},{9,1},... | collective-permute-start | bytes 589832 | tf_op jit(solution)/shard_map/ppermute | solution.py:51
  119.0 20.9 %collective-permute-start.25 = (bf16[192,512]{1,0:T(8,128)(2,1)S(1)}, bf16[192,512]{1,0:T(8,128)(2,1)}, u32[]{:S(2)}, u32[]{:S(2)}) collective-permute-start(bf16[192,512]{1,0:T(8,128)(2,1)S(1)} %get-tuple-element.108), channel_id=1, source_target_pairs={{0,4},{1,5},{2,6},{3,7},{4,0},{5,1},{6,2},{7,3},{8,12},{9,13},{10,... | collective-permute-start | bytes 589832 | tf_op jit(solution)/shard_map/ppermute | solution.py:51
  147.0 17.9 %collective-permute-start.30 = (bf16[48,2048]{1,0:T(8,128)(2,1)S(1)}, bf16[48,2048]{1,0:T(8,128)(2,1)S(1)}, u32[]{:S(2)}, u32[]{:S(2)}) collective-permute-start(bf16[48,2048]{1,0:T(8,128)(2,1)S(1)} %get-tuple-element.99), channel_id=1, source_target_pairs={{0,3},{1,2},{2,1},{3,0},{4,7},{5,6},{6,5},{7,4},{8,11},{9,10},{10,... | collective-permute-start | bytes 589832 | tf_op jit(solution)/shard_map/ppermute | solution.py:51
  151.4 17.5 %collective-permute-start.29 = (bf16[48,2048]{1,0:T(8,128)(2,1)S(1)}, bf16[48,2048]{1,0:T(8,128)(2,1)S(1)}, u32[]{:S(2)}, u32[]{:S(2)}) collective-permute-start(bf16[48,2048]{1,0:T(8,128)(2,1)S(1)} %get-tuple-element.100), channel_id=1, source_target_pairs={{0,2},{1,3},{2,0},{3,1},{4,6},{5,7},{6,4},{7,5},{8,10},{9,11},{10,... | collective-permute-start | bytes 589832 | tf_op jit(solution)/shard_map/ppermute | solution.py:51
  273.3 15.2 %collective-permute-start.61 = (bf16[128,1280]{1,0:T(8,128)(2,1)S(1)}, bf16[128,1280]{1,0:T(8,128)(2,1)S(1)}, u32[]{:S(2)}, u32[]{:S(2)}) collective-permute-start(bf16[128,1280]{1,0:T(8,128)(2,1)S(1)} %get-tuple-element.67), channel_id=1, source_target_pairs={{0,3},{1,2},{2,1},{3,0},{4,7},{5,6},{6,5},{7,4},{8,11},{9,10},{10,... | collective-permute-start | bytes 983048 | tf_op jit(solution)/shard_map/ppermute | solution.py:51
  275.2 36.4 %collective-permute-start.60 = (bf16[128,1280]{1,0:T(8,128)(2,1)S(1)}, bf16[128,1280]{1,0:T(8,128)(2,1)S(1)}, u32[]{:S(2)}, u32[]{:S(2)}) collective-permute-start(bf16[128,1280]{1,0:T(8,128)(2,1)S(1)} %get-tuple-element.68), channel_id=1, source_target_pairs={{0,2},{1,3},{2,0},{3,1},{4,6},{5,7},{6,4},{7,5},{8,10},{9,11},{10,... | collective-permute-start | bytes 983048 | tf_op jit(solution)/shard_map/ppermute | solution.py:51
  277.7 33.8 %collective-permute-start.59 = (bf16[128,1280]{1,0:T(8,128)(2,1)S(1)}, bf16[128,1280]{1,0:T(8,128)(2,1)S(1)}, u32[]{:S(2)}, u32[]{:S(2)}) collective-permute-start(bf16[128,1280]{1,0:T(8,128)(2,1)S(1)} %get-tuple-element.69), channel_id=1, source_target_pairs={{0,1},{1,0},{2,3},{3,2},{4,5},{5,4},{6,7},{7,6},{8,9},{9,8},{10,11... | collective-permute-start | bytes 983048 | tf_op jit(solution)/shard_map/ppermute | solution.py:51
  284.3 27.6 %collective-permute-start.55 = (bf16[128,1280]{1,0:T(8,128)(2,1)S(1)}, bf16[128,1280]{1,0:T(8,128)(2,1)S(1)}, u32[]{:S(2)}, u32[]{:S(2)}) collective-permute-start(bf16[128,1280]{1,0:T(8,128)(2,1)S(1)} %get-tuple-element.75), channel_id=1, source_target_pairs={{0,3},{1,2},{2,1},{3,0},{4,7},{5,6},{6,5},{7,4},{8,11},{9,10},{10,... | collective-permute-start | bytes 983048 | tf_op jit(solution)/shard_map/ppermute | solution.py:51
  286.2 33.2 %collective-permute-start.54 = (bf16[128,1280]{1,0:T(8,128)(2,1)S(1)}, bf16[128,1280]{1,0:T(8,128)(2,1)S(1)}, u32[]{:S(2)}, u32[]{:S(2)}) collective-permute-start(bf16[128,1280]{1,0:T(8,128)(2,1)S(1)} %get-tuple-element.76), channel_id=1, source_target_pairs={{0,2},{1,3},{2,0},{3,1},{4,6},{5,7},{6,4},{7,5},{8,10},{9,11},{10,... | collective-permute-start | bytes 983048 | tf_op jit(solution)/shard_map/ppermute | solution.py:51
  288.6 30.9 %collective-permute-start.53 = (bf16[128,1280]{1,0:T(8,128)(2,1)S(1)}, bf16[128,1280]{1,0:T(8,128)(2,1)S(1)}, u32[]{:S(2)}, u32[]{:S(2)}) collective-permute-start(bf16[128,1280]{1,0:T(8,128)(2,1)S(1)} %get-tuple-element.77), channel_id=1, source_target_pairs={{0,1},{1,0},{2,3},{3,2},{4,5},{5,4},{6,7},{7,6},{8,9},{9,8},{10,11... | collective-permute-start | bytes 983048 | tf_op jit(solution)/shard_map/ppermute | solution.py:51
  (81 other events, 883.5 us)

commit v5 on v4

--- a/solution.py
+++ b/solution.py
@@ -182,7 +182,7 @@
         return lambda k: lax.dynamic_slice_in_dim(array, (task_id ^ k) * block, block, 1)
 
     own_inputs = [states[0]]
-    early = []
+    packed = []
     rows_all = gather_rows(states[0], 0, 0)
     for layer in range(sections):
         normed = normalize(rows_all.astype(jnp.float32))
@@ -190,20 +190,18 @@
         preact = dot(normed_b, w_in)
         acted, slope = jax.jvp(gelu_tanh, (preact,), (jnp.ones_like(preact),))
         acted_b = acted.astype(jnp.bfloat16)
+        packed.append(
+            task_partners(
+                lambda k: jnp.concatenate([features_for(normed_b)(k), acted_b], axis=1), layer
+            )
+        )
         if layer + 1 < sections:
-            early.append(
-                task_partners(
-                    lambda k: jnp.concatenate([features_for(normed_b)(k), acted_b], axis=1), layer
-                )
-            )
             mixed = across_hidden(acted_b, w_out)
-            if layer == 0:
-                mixed, pieces[1] = tie(mixed, pieces[1])
             mixed = scatter_sum(mixed, layer, 0)
             own_rows = (own_inputs[layer].astype(jnp.float32) + mixed).astype(jnp.bfloat16)
             if layer == 0:
-                own_rows, (pieces[2], resid_apart) = tie(own_rows, (pieces[2], resid_apart))
-            own_rows, early[layer] = tie(own_rows, early[layer])
+                own_rows, pieces[1:3] = tie(own_rows, pieces[1:3])
+            own_rows, packed[layer] = tie(own_rows, packed[layer])
             own_inputs.append(own_rows)
             arrived = gather_rows(own_rows, 0, layer + 1)
             if layer == 0:
@@ -213,24 +211,27 @@
     steering = in_order(pieces, shard_id, 1)
     steer_in, steer_out = steering[0], steering[1]
 
-    normed_parts = task_partners(features_for(normed_b), sections - 1)
-    acted_b, normed_parts = tie(acted_b, normed_parts)
-    acted_parts = task_partners(lambda k: acted_b, sections - 1)
+    parts = packed[-1]
     for layer in range(sections - 1):
+        here = section_id == layer
         for k in range(1, tasks):
-            here = section_id == layer
-            normed_parts[k] = jnp.where(here, early[layer][k][:, :block], normed_parts[k])
-            acted_parts[k] = jnp.where(here, early[layer][k][:, block:], acted_parts[k])
-    normed_tasks = jnp.concatenate(normed_parts, axis=0)
-    acted_tasks = jnp.concatenate(acted_parts, axis=0)
+            parts[k] = jnp.where(here, packed[layer][k], parts[k])
+    normed_tasks = jnp.concatenate([part[:, :block] for part in parts], axis=0)
+    acted_tasks = jnp.concatenate([part[:, block:] for part in parts], axis=0)
     steered_parts = dot(normed_tasks, steer_in).reshape(tasks, joined, hidden)
-    steered = task_partners(
-        lambda k: steered_parts[k] if k == 0 else steered_parts[k].astype(jnp.bfloat16)
-    )
-    steered = sum(part.astype(jnp.float32) for part in steered)
-    turned_parts = across_hidden(acted_tasks, steer_out).astype(jnp.bfloat16)
-    turned_parts = turned_parts.reshape(tasks, joined, block)
-    turned = in_order(task_partners(lambda k: turned_parts[k]), task_id, 1).astype(jnp.float32)
+    turned_parts = across_hidden(acted_tasks, steer_out).reshape(tasks, joined, block)
+    parts = task_partners(
+        lambda k: jnp.concatenate(
+            [
+                steered_parts[k].astype(jnp.bfloat16),
+                turned_parts[k].astype(jnp.bfloat16),
+            ],
+            axis=1,
+        )
+    )
+    parts, resid_apart = tie(parts, resid_apart)
+    steered = sum((part[:, :hidden].astype(jnp.float32) for part in parts[1:]), steered_parts[0])
+    turned = in_order([part[:, hidden:] for part in parts], task_id, 1).astype(jnp.float32)
 
     own_dot = jnp.zeros((row_count, width), jnp.bfloat16)
     for layer in range(sections):

time: 360 us -> 352 us (0.978)
  starting transfers between devices: 147 us -> 132 us
  local copies, waits for them, and re-layouts: 24 us -> 27.6 us
    ppermute x62 -> x56, starting transfers between devices: 140 us -> 125 us  [send(): return lax.ppermute(value, ALL, pairs)]
    ppermute x62 -> x56, waiting for transfers between devices: 105 us -> 106 us  [send(): return lax.ppermute(value, ALL, pairs)]
    unnamed x72 -> x56, local copies, waits for them, and re-layouts: 8.58 us -> 9.41 us
  transfers between devices with their start and end apart: 69 -> 63, of which waited for: 30 -> 32; matrix products, arithmetic and copies ran while one was open for 11% -> 11% of each run, Pallas kernels for 0% -> 0%
where the time goes in v5:
time: 352 us; the launch traced here: 351 us
  starting transfers between devices  132 us (38%)
  waiting for transfers between devices  111 us (32%)
  matrix products  45 us (13%)
  local copies, waits for them, and re-layouts  27.6 us (8%)
  other arithmetic  16.3 us (5%)
  between operations  10.7 us (3%)
  Pallas kernels  7.69 us (2%)
    ppermute x56, starting transfers between devices, send(): return lax.ppermute(value, ALL, pairs)  125 us
    ppermute x56, waiting for transfers between devices, send(): return lax.ppermute(value, ALL, pairs)  106 us
    dot_general x5, matrix products, across_hidden(): lax.dot_general(left_side, right_side, (((1,), (1,)), ((), ())), preferre...  27.1 us
    dot_general x4, matrix products, dot(): return jnp.dot(left_side, right_side, preferred_element_type=jnp.float32)  15.4 us
    transpose x2, local copies, waits for them, and re-layouts, apart(): jnp.transpose(array, (1, 0, 2))  10.7 us
    unnamed x56, local copies, waits for them, and re-layouts  9.41 us
    pallas_call x1, Pallas kernels, update(): pl.pallas_call(update_kernel, grid=(total // columns,), in_specs=[pl.Bloc...  7.69 us
  transfers between devices with their start and end apart: 63, of which 32 were waited for; matrix products, arithmetic and copies ran while one was open for 11% of the time, Pallas kernels for 0%

profile of v5, /device:TPU:0, one launch (start us, length us, event | category | flops | bytes accessed | tf_op | source)
XLA Modules:
  0.0 350.6 jit_solution(3005618114005468732)
XLA Ops:
  0.6 7.0 %collective-permute-start.2 = (bf16[48,2048]{1,0:T(8,128)(2,1)}, bf16[48,2048]{1,0:T(8,128)(2,1)S(1)}, u32[]{:S(2)}, u32[]{:S(2)}) collective-permute-start(bf16[48,2048]{1,0:T(8,128)(2,1)} %bitcast.195), channel_id=1, source_target_pairs={{0,3},{1,2},{2,1},{3,0},{4,7},{5,6},{6,5},{7,4},{8,11},{9,10},{10,... | collective-permute-start | bytes 589832 | tf_op jit(solution)/shard_map/ppermute | solution.py:51
  12.0 4.2 %copy.8 = f32[2,128,5120]{2,1,0:T(8,128)S(1)} copy(f32[2,128,5120]{2,0,1:T(2,128)} %bitcast.189) | data formatting | bytes 10485760 | tf_op jit(solution)/shard_map/transpose | solution.py:150
  32.6 4.3 %fusion.156 = (bf16[192,2048]{1,0:T(8,128)(2,1)S(1)}, f32[192,2048]{1,0:T(8,128)S(1)}) fusion(bf16[192,1280]{1,0:T(8,128)(2,1)S(1)} %fusion.106, bf16[1,1,2,2048,1280]{4,3,2,1,0:T(8,128)(2,1)} %param.6), kind=kOutput, calls=%fused_computation.243 | convolution fusion | flops 1007026176 | bytes 8093696 | tf_op jit(solution)/shard_map/dot_general | solution.py:24
  42.9 4.2 %collective-permute-start.3 = (bf16[48,2048]{1,0:T(8,128)(2,1)S(1)}, bf16[48,2048]{1,0:T(8,128)(2,1)S(1)}, u32[]{:S(2)}, u32[]{:S(2)}) collective-permute-start(bf16[48,2048]{1,0:T(8,128)(2,1)S(1)} %get-tuple-element.112), channel_id=1, source_target_pairs={{0,1},{1,0},{2,3},{3,2},{4,5},{5,4},{6,7},{7,6},{8,9},{9,8},{10,11... | collective-permute-start | bytes 589832 | tf_op jit(solution)/shard_map/ppermute | solution.py:51
  53.7 14.9 %collective-permute-done.4 = bf16[48,2048]{1,0:T(8,128)(2,1)S(1)} collective-permute-done((bf16[48,2048]{1,0:T(8,128)(2,1)S(1)}, bf16[48,2048]{1,0:T(8,128)(2,1)S(1)}, u32[]{:S(2)}, u32[]{:S(2)}) %collective-permute-start.4) | collective-permute-done | bytes 196640 | tf_op jit(solution)/shard_map/ppermute | solution.py:51
  77.5 11.4 %collective-permute-done.9 = bf16[192,1792]{1,0:T(8,128)(2,1)S(1)} collective-permute-done((bf16[192,1792]{1,0:T(8,128)(2,1)S(1)}, bf16[192,1792]{1,0:T(8,128)(2,1)S(1)}, u32[]{:S(2)}, u32[]{:S(2)}) %collective-permute-start.9) | collective-permute-done | bytes 688160 | tf_op jit(solution)/shard_map/ppermute | solution.py:51
  98.3 4.7 %multiply_convert_fusion.1 = (bf16[192,1280]{1,0:T(8,128)(2,1)S(1)}, f32[192,1280]{1,0:T(8,128)}) fusion(bf16[192,2048]{1,0:T(8,128)(2,1)S(1)} %fusion.84, bf16[1,1,2,2048,1280]{4,3,2,1,0:T(8,128)(2,1)} %param.6), kind=kOutput, calls=%fused_computation.113 | convolution fusion | flops 1008844800 | bytes 7503872 | tf_op jit(solution)/shard_map/dot_general | solution.py:36
  117.7 6.5 %copy.9 = f32[2,128,5120]{2,1,0:T(8,128)} copy(f32[2,128,5120]{2,0,1:T(2,128)} %bitcast.187) | data formatting | bytes 10485760 | tf_op jit(solution)/shard_map/transpose | solution.py:150
  125.5 6.1 %collective-permute-done.19 = bf16[192,1792]{1,0:T(8,128)(2,1)} collective-permute-done((bf16[192,1792]{1,0:T(8,128)(2,1)S(1)}, bf16[192,1792]{1,0:T(8,128)(2,1)}, u32[]{:S(2)}, u32[]{:S(2)}) %collective-permute-start.19) | collective-permute-done | bytes 688160 | tf_op jit(solution)/shard_map/ppermute | solution.py:51
  133.9 6.8 %collective-permute-done.21 = bf16[192,1792]{1,0:T(8,128)(2,1)} collective-permute-done((bf16[192,1792]{1,0:T(8,128)(2,1)}, bf16[192,1792]{1,0:T(8,128)(2,1)}, u32[]{:S(2)}, u32[]{:S(2)}) %collective-permute-start.21) | collective-permute-done | bytes 688160 | tf_op jit(solution)/shard_map/ppermute | solution.py:51
  144.7 5.5 %fusion.158 = (bf16[192,2048]{1,0:T(8,128)(2,1)S(1)}, f32[192,2048]{1,0:T(8,128)S(1)}) fusion(bf16[192,512]{1,0:T(8,128)(2,1)S(1)} %get-tuple-element.98, bf16[192,512]{1,0:T(8,128)(2,1)S(1)} %get-tuple-element.99, bf16[192,512]{1,0:T(8,128)(2,1)S(1)} %get-tuple-element.100, bf16[192,512]{1,0:T(8,128)(2,1)S(1)} %get-tuple-element.97, ...), kind=kOutput, calls=%fused_computation.245 | convolution fusion | flops 1016463360 | bytes 11829248 | tf_op jit(solution)/shard_map/dot_general | solution.py:24
  156.2 4.2 %collective-permute-start.22 = (bf16[48,2048]{1,0:T(8,128)(2,1)S(1)}, bf16[48,2048]{1,0:T(8,128)(2,1)S(1)}, u32[]{:S(2)}, u32[]{:S(2)}) collective-permute-start(bf16[48,2048]{1,0:T(8,128)(2,1)S(1)} %get-tuple-element.94), channel_id=1, source_target_pairs={{0,1},{1,0},{2,3},{3,2},{4,5},{5,4},{6,7},{7,6},{8,9},{9,8},{10,11... | collective-permute-start | bytes 589832 | tf_op jit(solution)/shard_map/ppermute | solution.py:51
  166.0 7.4 %collective-permute-start.28 = (bf16[48,2048]{1,0:T(8,128)(2,1)S(1)}, bf16[48,2048]{1,0:T(8,128)(2,1)S(1)}, u32[]{:S(2)}, u32[]{:S(2)}) collective-permute-start(bf16[48,2048]{1,0:T(8,128)(2,1)S(1)} %fusion.128), channel_id=1, source_target_pairs={{0,19},{1,18},{2,17},{3,16},{4,23},{5,22},{6,21},{7,20},{8,27},{9,... | collective-permute-start | bytes 589832 | tf_op jit(solution)/shard_map/ppermute | solution.py:51
  181.6 8.8 %fusion.57 = bf16[192,2048]{1,0:T(8,128)(2,1)S(1)} fusion(bf16[1,1,2,2048,1280]{4,3,2,1,0:T(8,128)(2,1)} %param.6, bf16[192,2048]{1,0:T(8,128)(2,1)S(1)} %get-tuple-element.48, f32[192]{0:T(256)S(1)} %multiply_multiply_fusion.3, f32[192]{0:T(256)S(1)} %fusion.134, bf16[48,2048]{1,0:T(8,128)(2,1)} %copy-done.17, bf16[48,2048]{1,0:T(8,128)(2,1)} %copy-done.18, ...), kind=kOutput, calls=%fused_computation.58 | convolution fusion | flops 2028453888 | bytes 17073664 | tf_op jit(solution)/shard_map/dot_general | solution.py:24
  199.4 5.3 %collective-permute-done.31 = bf16[48,2048]{1,0:T(8,128)(2,1)S(1)} collective-permute-done((bf16[48,2048]{1,0:T(8,128)(2,1)S(1)}, bf16[48,2048]{1,0:T(8,128)(2,1)S(1)}, u32[]{:S(2)}, u32[]{:S(2)}) %collective-permute-start.31) | collective-permute-done | bytes 196640 | tf_op jit(solution)/shard_map/ppermute | solution.py:51
  213.5 7.4 %fusion.54 = bf16[192,2048]{1,0:T(8,128)(2,1)S(1)} fusion(bf16[1,1,2,2048,1280]{4,3,2,1,0:T(8,128)(2,1)} %param.6, bf16[48,2048]{1,0:T(8,128)(2,1)S(1)} %collective-permute-done.36, bf16[48,2048]{1,0:T(8,128)(2,1)S(1)} %collective-permute-done.35, bf16[48,2048]{1,0:T(8,128)(2,1)S(1)} %collective-permute-done.34, ...), kind=kOutput, calls=%fused_computation.57 | convolution fusion | flops 2021621760 | bytes 13041665 | tf_op jit(solution)/shard_map/dot_general | solution.py:24
  226.2 4.3 %collective-permute-done.40 = bf16[48,2048]{1,0:T(8,128)(2,1)S(1)} collective-permute-done((bf16[48,2048]{1,0:T(8,128)(2,1)S(1)}, bf16[48,2048]{1,0:T(8,128)(2,1)S(1)}, u32[]{:S(2)}, u32[]{:S(2)}) %collective-permute-start.40) | collective-permute-done | bytes 196640 | tf_op jit(solution)/shard_map/ppermute | solution.py:51
  230.5 5.7 %collective-permute-done.39 = bf16[48,2048]{1,0:T(8,128)(2,1)S(1)} collective-permute-done((bf16[48,2048]{1,0:T(8,128)(2,1)S(1)}, bf16[48,2048]{1,0:T(8,128)(2,1)S(1)}, u32[]{:S(2)}, u32[]{:S(2)}) %collective-permute-start.39) | collective-permute-done | bytes 196640 | tf_op jit(solution)/shard_map/ppermute | solution.py:51
  242.6 4.3 %collective-permute-start.41 = (bf16[48,2048]{1,0:T(8,128)(2,1)S(1)}, bf16[48,2048]{1,0:T(8,128)(2,1)S(1)}, u32[]{:S(2)}, u32[]{:S(2)}) collective-permute-start(bf16[48,2048]{1,0:T(8,128)(2,1)S(1)} %fusion.125), channel_id=1, source_target_pairs={{0,1},{1,0},{2,3},{3,2},{4,5},{5,4},{6,7},{7,6},{8,9},{9,8},{10,11... | collective-permute-start | bytes 589832 | tf_op jit(solution)/shard_map/ppermute | solution.py:51
  246.9 4.5 %multiply_reduce_fusion = f32[]{:T(128)} fusion(f32[2,128,5120]{2,1,0:T(8,128)} %copy.9), kind=kLoop, calls=%fused_computation.18 | loop fusion | flops 2621439 | bytes 5242884 | tf_op jit(solution)/shard_map/reduce_sum | solution.py:278
  281.4 11.7 %collective-permute-start.47 = (bf16[128,1280]{1,0:T(8,128)(2,1)S(1)}, bf16[128,1280]{1,0:T(8,128)(2,1)S(1)}, u32[]{:S(2)}, u32[]{:S(2)}) collective-permute-start(bf16[128,1280]{1,0:T(8,128)(2,1)S(1)} %get-tuple-element.73), channel_id=1, source_target_pairs={{0,1},{1,0},{2,3},{3,2},{4,5},{5,4},{6,7},{7,6},{8,9},{9,8},{10,11... | collective-permute-start | bytes 983048 | tf_op jit(solution)/shard_map/ppermute | solution.py:51
  293.1 11.4 %collective-permute-done.54 = bf16[128,1280]{1,0:T(8,128)(2,1)S(1)} collective-permute-done((bf16[128,1280]{1,0:T(8,128)(2,1)S(1)}, bf16[128,1280]{1,0:T(8,128)(2,1)S(1)}, u32[]{:S(2)}, u32[]{:S(2)}) %collective-permute-start.54) | collective-permute-done | bytes 327712 | tf_op jit(solution)/shard_map/ppermute | solution.py:51
  304.7 7.5 %collective-permute-done.48 = bf16[128,1280]{1,0:T(8,128)(2,1)S(1)} collective-permute-done((bf16[128,1280]{1,0:T(8,128)(2,1)S(1)}, bf16[128,1280]{1,0:T(8,128)(2,1)S(1)}, u32[]{:S(2)}, u32[]{:S(2)}) %collective-permute-start.48) | collective-permute-done | bytes 327712 | tf_op jit(solution)/shard_map/ppermute | solution.py:51
  341.8 7.7 %shard_map.76 = (f32[128,2,5120]{2,1,0:T(2,128)}, f32[128,2,5120]{2,1,0:T(2,128)}) custom-call(f32[2]{0:T(128)S(1)} %pad_maximum_fusion.33.scalars, bf16[128,5120]{1,0:T(8,128)(2,1)S(1)} %get-tuple-element.45.in_ref, bf16[128,5120]{1,0:T(8,128)(2,1)S(1)} %get-tuple-element.46.out_ref, f32[128,2,5120]{2,1,0:T(2,128)S(1)} %bitcast.188, ...), custom_call_target="tpu_custom_call" | custom-call | flops 5242880 | bytes 26214400 | tf_op jit(solution)/shard_map/pallas_call | solution.py:136
  (245 shorter events, 174.3 us)
Async XLA Ops:
  0.6 25.6 %collective-permute-start.2 = (bf16[48,2048]{1,0:T(8,128)(2,1)}, bf16[48,2048]{1,0:T(8,128)(2,1)S(1)}, u32[]{:S(2)}, u32[]{:S(2)}) collective-permute-start(bf16[48,2048]{1,0:T(8,128)(2,1)} %bitcast.195), channel_id=1, source_target_pairs={{0,3},{1,2},{2,1},{3,0},{4,7},{5,6},{6,5},{7,4},{8,11},{9,10},{10,... | collective-permute-start | bytes 589832 | tf_op jit(solution)/shard_map/ppermute | solution.py:51
  7.6 18.6 %collective-permute-start.1 = (bf16[48,2048]{1,0:T(8,128)(2,1)}, bf16[48,2048]{1,0:T(8,128)(2,1)S(1)}, u32[]{:S(2)}, u32[]{:S(2)}) collective-permute-start(bf16[48,2048]{1,0:T(8,128)(2,1)} %bitcast.196), channel_id=1, source_target_pairs={{0,2},{1,3},{2,0},{3,1},{4,6},{5,7},{6,4},{7,5},{8,10},{9,11},{10,... | collective-permute-start | bytes 589832 | tf_op jit(solution)/shard_map/ppermute | solution.py:51
  9.5 18.9 %collective-permute-start = (bf16[48,2048]{1,0:T(8,128)(2,1)}, bf16[48,2048]{1,0:T(8,128)(2,1)S(1)}, u32[]{:S(2)}, u32[]{:S(2)}) collective-permute-start(bf16[48,2048]{1,0:T(8,128)(2,1)} %bitcast.197), channel_id=1, source_target_pairs={{0,1},{1,0},{2,3},{3,2},{4,5},{5,4},{6,7},{7,6},{8,9},{9,8},{10,11... | collective-permute-start | bytes 589832 | tf_op jit(solution)/shard_map/ppermute | solution.py:51
  20.9 54.6 %collective-permute-start.6 = (bf16[2,128,1280]{2,1,0:T(8,128)(2,1)}, bf16[2,128,1280]{2,1,0:T(8,128)(2,1)S(1)}, u32[]{:S(2)}, u32[]{:S(2)}) collective-permute-start(bf16[2,128,1280]{2,1,0:T(8,128)(2,1)} %pad_maximum_fusion.23), channel_id=1, source_target_pairs={{0,1},{1,0},{2,3},{3,2},{4,5},{5,4},{6,7},{7,6},{8,9},{9,8},{10,11... | collective-permute-start | bytes 1966088 | tf_op jit(solution)/shard_map/ppermute | solution.py:51
  23.3 54.2 %collective-permute-start.7 = (bf16[2,128,1280]{2,1,0:T(8,128)(2,1)}, bf16[2,128,1280]{2,1,0:T(8,128)(2,1)}, u32[]{:S(2)}, u32[]{:S(2)}) collective-permute-start(bf16[2,128,1280]{2,1,0:T(8,128)(2,1)} %pad_maximum_fusion.24), channel_id=1, source_target_pairs={{0,2},{1,3},{2,0},{3,1},{4,6},{5,7},{6,4},{7,5},{8,10},{9,11},{10,... | collective-permute-start | bytes 1966088 | tf_op jit(solution)/shard_map/ppermute | solution.py:51
  37.0 13.3 %collective-permute-start.5 = (bf16[48,2048]{1,0:T(8,128)(2,1)S(1)}, bf16[48,2048]{1,0:T(8,128)(2,1)S(1)}, u32[]{:S(2)}, u32[]{:S(2)}) collective-permute-start(bf16[48,2048]{1,0:T(8,128)(2,1)S(1)} %get-tuple-element.113), channel_id=1, source_target_pairs={{0,3},{1,2},{2,1},{3,0},{4,7},{5,6},{6,5},{7,4},{8,11},{9,10},{10,... | collective-permute-start | bytes 589832 | tf_op jit(solution)/shard_map/ppermute | solution.py:51
  41.0 27.7 %collective-permute-start.4 = (bf16[48,2048]{1,0:T(8,128)(2,1)S(1)}, bf16[48,2048]{1,0:T(8,128)(2,1)S(1)}, u32[]{:S(2)}, u32[]{:S(2)}) collective-permute-start(bf16[48,2048]{1,0:T(8,128)(2,1)S(1)} %get-tuple-element.114), channel_id=1, source_target_pairs={{0,2},{1,3},{2,0},{3,1},{4,6},{5,7},{6,4},{7,5},{8,10},{9,11},{10,... | collective-permute-start | bytes 589832 | tf_op jit(solution)/shard_map/ppermute | solution.py:51
  42.9 29.2 %collective-permute-start.3 = (bf16[48,2048]{1,0:T(8,128)(2,1)S(1)}, bf16[48,2048]{1,0:T(8,128)(2,1)S(1)}, u32[]{:S(2)}, u32[]{:S(2)}) collective-permute-start(bf16[48,2048]{1,0:T(8,128)(2,1)S(1)} %get-tuple-element.112), channel_id=1, source_target_pairs={{0,1},{1,0},{2,3},{3,2},{4,5},{5,4},{6,7},{7,6},{8,9},{9,8},{10,11... | collective-permute-start | bytes 589832 | tf_op jit(solution)/shard_map/ppermute | solution.py:51
  50.3 27.2 %collective-permute-start.8 = (bf16[192,1792]{1,0:T(8,128)(2,1)S(1)}, bf16[192,1792]{1,0:T(8,128)(2,1)S(1)}, u32[]{:S(2)}, u32[]{:S(2)}) collective-permute-start(bf16[192,1792]{1,0:T(8,128)(2,1)S(1)} %get-tuple-element.120), channel_id=1, source_target_pairs={{0,4},{1,5},{2,6},{3,7},{4,0},{5,1},{6,2},{7,3},{8,12},{9,13},{10,... | collective-permute-start | bytes 2064392 | tf_op jit(solution)/shard_map/ppermute | solution.py:51
  68.6 20.2 %collective-permute-start.9 = (bf16[192,1792]{1,0:T(8,128)(2,1)S(1)}, bf16[192,1792]{1,0:T(8,128)(2,1)S(1)}, u32[]{:S(2)}, u32[]{:S(2)}) collective-permute-start(bf16[192,1792]{1,0:T(8,128)(2,1)S(1)} %get-tuple-element.119), channel_id=1, source_target_pairs={{0,8},{1,9},{2,10},{3,11},{4,12},{5,13},{6,14},{7,15},{8,0},{9,1},... | collective-permute-start | bytes 2064392 | tf_op jit(solution)/shard_map/ppermute | solution.py:51
  72.1 16.8 %collective-permute-start.10 = (bf16[192,1792]{1,0:T(8,128)(2,1)S(1)}, bf16[192,1792]{1,0:T(8,128)(2,1)S(1)}, u32[]{:S(2)}, u32[]{:S(2)}) collective-permute-start(bf16[192,1792]{1,0:T(8,128)(2,1)S(1)} %get-tuple-element.118), channel_id=1, source_target_pairs={{0,12},{1,13},{2,14},{3,15},{4,8},{5,9},{6,10},{7,11},{8,4},{9,5},... | collective-permute-start | bytes 2064392 | tf_op jit(solution)/shard_map/ppermute | solution.py:51
  75.5 22.2 %collective-permute-start.15 = (bf16[2,128,1280]{2,1,0:T(8,128)(2,1)S(1)}, bf16[2,128,1280]{2,1,0:T(8,128)(2,1)S(1)}, u32[]{:S(2)}, u32[]{:S(2)}) collective-permute-start(bf16[2,128,1280]{2,1,0:T(8,128)(2,1)S(1)} %pad_maximum_fusion.25), channel_id=1, source_target_pairs={{0,3},{1,2},{2,1},{3,0},{4,7},{5,6},{6,5},{7,4},{8,11},{9,10},{10,... | collective-permute-start | bytes 1966088 | tf_op jit(solution)/shard_map/ppermute | solution.py:51
  113.1 18.5 %collective-permute-start.19 = (bf16[192,1792]{1,0:T(8,128)(2,1)S(1)}, bf16[192,1792]{1,0:T(8,128)(2,1)}, u32[]{:S(2)}, u32[]{:S(2)}) collective-permute-start(bf16[192,1792]{1,0:T(8,128)(2,1)S(1)} %pad_maximum_fusion.20), channel_id=1, source_target_pairs={{0,4},{1,5},{2,6},{3,7},{4,0},{5,1},{6,2},{7,3},{8,12},{9,13},{10,... | collective-permute-start | bytes 2064392 | tf_op jit(solution)/shard_map/ppermute | solution.py:51
  114.7 19.2 %collective-permute-start.20 = (bf16[192,1792]{1,0:T(8,128)(2,1)S(1)}, bf16[192,1792]{1,0:T(8,128)(2,1)}, u32[]{:S(2)}, u32[]{:S(2)}) collective-permute-start(bf16[192,1792]{1,0:T(8,128)(2,1)S(1)} %pad_maximum_fusion.21), channel_id=1, source_target_pairs={{0,8},{1,9},{2,10},{3,11},{4,12},{5,13},{6,14},{7,15},{8,0},{9,1},... | collective-permute-start | bytes 2064392 | tf_op jit(solution)/shard_map/ppermute | solution.py:51
  117.2 23.5 %collective-permute-start.21 = (bf16[192,1792]{1,0:T(8,128)(2,1)}, bf16[192,1792]{1,0:T(8,128)(2,1)}, u32[]{:S(2)}, u32[]{:S(2)}) collective-permute-start(bf16[192,1792]{1,0:T(8,128)(2,1)} %pad_maximum_fusion.22), channel_id=1, source_target_pairs={{0,12},{1,13},{2,14},{3,15},{4,8},{5,9},{6,10},{7,11},{8,4},{9,5},... | collective-permute-start | bytes 2064392 | tf_op jit(solution)/shard_map/ppermute | solution.py:51
  222.3 13.9 %collective-permute-start.39 = (bf16[48,2048]{1,0:T(8,128)(2,1)S(1)}, bf16[48,2048]{1,0:T(8,128)(2,1)S(1)}, u32[]{:S(2)}, u32[]{:S(2)}) collective-permute-start(bf16[48,2048]{1,0:T(8,128)(2,1)S(1)} %get-tuple-element.88), channel_id=1, source_target_pairs={{16,2},{17,3},{18,0},{19,1},{20,6},{21,7},{22,4},{23,5},{24,10},{2... | collective-permute-start | bytes 589832 | tf_op jit(solution)/shard_map/ppermute | solution.py:51
  236.7 14.7 %collective-permute-start.43 = (bf16[48,2048]{1,0:T(8,128)(2,1)S(1)}, bf16[48,2048]{1,0:T(8,128)(2,1)S(1)}, u32[]{:S(2)}, u32[]{:S(2)}) collective-permute-start(bf16[48,2048]{1,0:T(8,128)(2,1)S(1)} %fusion.125), channel_id=1, source_target_pairs={{0,3},{1,2},{2,1},{3,0},{4,7},{5,6},{6,5},{7,4},{8,11},{9,10},{10,... | collective-permute-start | bytes 589832 | tf_op jit(solution)/shard_map/ppermute | solution.py:51
  261.7 13.9 %collective-permute-start.45 = (bf16[192,1280]{1,0:T(8,128)(2,1)S(1)}, bf16[192,1280]{1,0:T(8,128)(2,1)S(1)}, u32[]{:S(2)}, u32[]{:S(2)}) collective-permute-start(bf16[192,1280]{1,0:T(8,128)(2,1)S(1)} %fusion.60), channel_id=1, source_target_pairs={{0,8},{1,9},{2,10},{3,11},{4,12},{5,13},{6,14},{7,15},{8,0},{9,1},... | collective-permute-start | bytes 1474568 | tf_op jit(solution)/shard_map/ppermute | solution.py:51
  266.2 15.2 %collective-permute-start.55 = (bf16[128,1280]{1,0:T(8,128)(2,1)S(1)}, bf16[128,1280]{1,0:T(8,128)(2,1)S(1)}, u32[]{:S(2)}, u32[]{:S(2)}) collective-permute-start(bf16[128,1280]{1,0:T(8,128)(2,1)S(1)} %get-tuple-element.63), channel_id=1, source_target_pairs={{0,3},{1,2},{2,1},{3,0},{4,7},{5,6},{6,5},{7,4},{8,11},{9,10},{10,... | collective-permute-start | bytes 983048 | tf_op jit(solution)/shard_map/ppermute | solution.py:51
  268.0 36.4 %collective-permute-start.54 = (bf16[128,1280]{1,0:T(8,128)(2,1)S(1)}, bf16[128,1280]{1,0:T(8,128)(2,1)S(1)}, u32[]{:S(2)}, u32[]{:S(2)}) collective-permute-start(bf16[128,1280]{1,0:T(8,128)(2,1)S(1)} %get-tuple-element.64), channel_id=1, source_target_pairs={{0,2},{1,3},{2,0},{3,1},{4,6},{5,7},{6,4},{7,5},{8,10},{9,11},{10,... | collective-permute-start | bytes 983048 | tf_op jit(solution)/shard_map/ppermute | solution.py:51
  270.4 34.1 %collective-permute-start.53 = (bf16[128,1280]{1,0:T(8,128)(2,1)S(1)}, bf16[128,1280]{1,0:T(8,128)(2,1)S(1)}, u32[]{:S(2)}, u32[]{:S(2)}) collective-permute-start(bf16[128,1280]{1,0:T(8,128)(2,1)S(1)} %get-tuple-element.65), channel_id=1, source_target_pairs={{0,1},{1,0},{2,3},{3,2},{4,5},{5,4},{6,7},{7,6},{8,9},{9,8},{10,11... | collective-permute-start | bytes 983048 | tf_op jit(solution)/shard_map/ppermute | solution.py:51
  276.9 27.8 %collective-permute-start.49 = (bf16[128,1280]{1,0:T(8,128)(2,1)S(1)}, bf16[128,1280]{1,0:T(8,128)(2,1)S(1)}, u32[]{:S(2)}, u32[]{:S(2)}) collective-permute-start(bf16[128,1280]{1,0:T(8,128)(2,1)S(1)} %get-tuple-element.71), channel_id=1, source_target_pairs={{0,3},{1,2},{2,1},{3,0},{4,7},{5,6},{6,5},{7,4},{8,11},{9,10},{10,... | collective-permute-start | bytes 983048 | tf_op jit(solution)/shard_map/ppermute | solution.py:51
  279.0 33.3 %collective-permute-start.48 = (bf16[128,1280]{1,0:T(8,128)(2,1)S(1)}, bf16[128,1280]{1,0:T(8,128)(2,1)S(1)}, u32[]{:S(2)}, u32[]{:S(2)}) collective-permute-start(bf16[128,1280]{1,0:T(8,128)(2,1)S(1)} %get-tuple-element.72), channel_id=1, source_target_pairs={{0,2},{1,3},{2,0},{3,1},{4,6},{5,7},{6,4},{7,5},{8,10},{9,11},{10,... | collective-permute-start | bytes 983048 | tf_op jit(solution)/shard_map/ppermute | solution.py:51
  281.4 30.9 %collective-permute-start.47 = (bf16[128,1280]{1,0:T(8,128)(2,1)S(1)}, bf16[128,1280]{1,0:T(8,128)(2,1)S(1)}, u32[]{:S(2)}, u32[]{:S(2)}) collective-permute-start(bf16[128,1280]{1,0:T(8,128)(2,1)S(1)} %get-tuple-element.73), channel_id=1, source_target_pairs={{0,1},{1,0},{2,3},{3,2},{4,5},{5,4},{6,7},{7,6},{8,9},{9,8},{10,11... | collective-permute-start | bytes 983048 | tf_op jit(solution)/shard_map/ppermute | solution.py:51
  (67 other events, 611.3 us)

commit v6 on v5

--- a/solution.py
+++ b/solution.py
@@ -122,28 +122,36 @@
     return value
 
 
-def update_kernel(scalars, in_ref, out_ref, resid_ref, direc_ref, resid_next, direc_next):
+def update_kernel(sums_ref, in_ref, out_ref, resid_ref, direc_ref, resid_next, direc_next, step_ref):
+    start_norm, curvature, crossed, squared = (
+        jnp.sum(sums_ref[i : i + 1, :], axis=1, keepdims=True) for i in range(4)
+    )
+    step_size = start_norm / curvature
+    next_norm = start_norm - 2.0 * step_size * crossed + step_size * step_size * squared
+    ratio = next_norm / start_norm
+    step_ref[...] = step_size
     for i, product in ((0, in_ref), (1, out_ref)):
-        fresh = resid_ref[:, i, :] - scalars[0] * product[...].astype(jnp.float32)
+        fresh = resid_ref[:, i, :] - step_size * product[...].astype(jnp.float32)
         resid_next[:, i, :] = fresh
-        direc_next[:, i, :] = fresh + scalars[1] * direc_ref[:, i, :]
-
-
-def update(scalars, curved_in, curved_out, resid, direc, columns):
+        direc_next[:, i, :] = fresh + ratio * direc_ref[:, i, :]
+
+
+def update(sums, curved_in, curved_out, resid, direc, columns):
     rows, pair, total = resid.shape
     native = pl.BlockSpec((rows, pair, columns), lambda i: (0, 0, i))
     flat = pl.BlockSpec((rows, columns), lambda i: (0, i))
     return pl.pallas_call(
         update_kernel,
         grid=(total // columns,),
-        in_specs=[pl.BlockSpec(memory_space=pltpu.SMEM), flat, flat, native, native],
-        out_specs=[native, native],
-        out_shape=[jax.ShapeDtypeStruct(resid.shape, jnp.float32)] * 2,
-        compiler_params=pltpu.CompilerParams(vmem_limit_bytes=32 * 1024 * 1024),
+        in_specs=[pl.BlockSpec(sums.shape, lambda i: (0, 0)), flat, flat, native, native],
+        out_specs=[native, native, pl.BlockSpec((1, 1), lambda i: (0, 0))],
+        out_shape=[jax.ShapeDtypeStruct(resid.shape, jnp.float32)] * 2
+        + [jax.ShapeDtypeStruct((1, 1), jnp.float32)],
+        compiler_params=pltpu.CompilerParams(vmem_limit_bytes=58 * 1024 * 1024),
         cost_estimate=pl.CostEstimate(
             flops=4 * resid.size, bytes_accessed=20 * resid.size, transcendentals=0
         ),
-    )(scalars, curved_in, curved_out, resid, direc)
+    )(sums, curved_in, curved_out, resid, direc)
 
 
 def apart(array):
@@ -272,28 +280,26 @@
     curved_in = to_owners(across_tokens(normed_tasks, preact_bars_tasks))
     products = [curved.astype(jnp.float32) for curved in (curved_in, curved_out)]
 
+    def folded(values):
+        blocks = [
+            value[:, i * hidden : (i + 1) * hidden] for value in values for i in range(shards)
+        ]
+        return jnp.sum(sum(blocks), axis=0)
+
     sums = sum_everywhere(
         jnp.stack(
             [
-                jnp.sum(resid_apart * resid_apart),
-                sum(jnp.sum(direc_apart[i] * products[i]) for i in range(2)),
-                sum(jnp.sum(resid_apart[i] * products[i]) for i in range(2)),
-                sum(jnp.sum(products[i] * products[i]) for i in range(2)),
+                folded([resid_apart[i] * resid_apart[i] for i in range(2)]),
+                folded([direc_apart[i] * products[i] for i in range(2)]),
+                folded([resid_apart[i] * products[i] for i in range(2)]),
+                folded([products[i] * products[i] for i in range(2)]),
             ]
         )
     )
-    start_norm, curvature, crossed, squared = sums[0], sums[1], sums[2], sums[3]
-    step_size = start_norm / curvature
-    next_norm = start_norm - 2.0 * step_size * crossed + step_size * step_size * squared
-    resid_next, direc_next = update(
-        jnp.stack([step_size, next_norm / start_norm]),
-        curved_in,
-        curved_out,
-        resid_local,
-        direc_local,
-        hidden,
-    )
-    return (resid_next[None], direc_next[None], step_size)
+    resid_next, direc_next, step_size = update(
+        sums, curved_in, curved_out, resid_local, direc_local, hidden
+    )
+    return (resid_next[None], direc_next[None], step_size[0, 0])
 
 
 def solution(mesh):

time: 352 us -> 347 us (0.986)
  waiting for transfers between devices: 111 us -> 124 us
  between operations: 10.7 us -> 1.87 us
  starting transfers between devices: 132 us -> 125 us
  local copies, waits for them, and re-layouts: 27.6 us -> 23.3 us
    ppermute x56, waiting for transfers between devices: 106 us -> 121 us  [send(): return lax.ppermute(value, ALL, pairs)]
    ppermute x56, starting transfers between devices: 125 us -> 117 us  [send(): return lax.ppermute(value, ALL, pairs)]
    reduce_sum x2 -> x4, other arithmetic: 6.52 us -> 1.28 us  [folded(): return jnp.sum(sum(blocks), axis=0)]
    unnamed x56 -> x52, local copies, waits for them, and re-layouts: 9.41 us -> 5.71 us
    pallas_call x1, Pallas kernels: 7.69 us -> 11.2 us  [update(): pl.pallas_call(update_kernel, grid=(total // columns,), in_specs=[pl.Bloc...]
  transfers between devices with their start and end apart: 63 -> 63, of which waited for: 32 -> 31; matrix products, arithmetic and copies ran while one was open for 11% -> 11% of each run, Pallas kernels for 0% -> 0%
where the time goes in v6:
time: 347 us; the launch traced here: 346 us
  starting transfers between devices  125 us (36%)
  waiting for transfers between devices  124 us (36%)
  matrix products  44.9 us (13%)
  local copies, waits for them, and re-layouts  23.3 us (7%)
  other arithmetic  14.8 us (4%)
  Pallas kernels  11.2 us (3%)
    ppermute x56, waiting for transfers between devices, send(): return lax.ppermute(value, ALL, pairs)  121 us
    ppermute x56, starting transfers between devices, send(): return lax.ppermute(value, ALL, pairs)  117 us
    dot_general x5, matrix products, across_hidden(): lax.dot_general(left_side, right_side, (((1,), (1,)), ((), ())), preferre...  27.1 us
    dot_general x4, matrix products, dot(): return jnp.dot(left_side, right_side, preferred_element_type=jnp.float32)  15.4 us
    pallas_call x1, Pallas kernels, update(): pl.pallas_call(update_kernel, grid=(total // columns,), in_specs=[pl.Bloc...  11.2 us
    transpose x2, local copies, waits for them, and re-layouts, apart(): jnp.transpose(array, (1, 0, 2))  10.7 us
    ppermute x7, starting transfers between devices, sum_everywhere(): parts.append(lax.ppermute(value, axis, [(i, i ^ k) for i in range(count)]))  8.08 us
  transfers between devices with their start and end apart: 63, of which 31 were waited for; matrix products, arithmetic and copies ran while one was open for 11% of the time, Pallas kernels for 0%

profile of v6, /device:TPU:0, one launch (start us, length us, event | category | flops | bytes accessed | tf_op | source)
XLA Modules:
  0.0 345.6 jit_solution(15753095299542017399)
XLA Ops:
  0.6 7.0 %collective-permute-start.2 = (bf16[48,2048]{1,0:T(8,128)(2,1)}, bf16[48,2048]{1,0:T(8,128)(2,1)S(1)}, u32[]{:S(2)}, u32[]{:S(2)}) collective-permute-start(bf16[48,2048]{1,0:T(8,128)(2,1)} %bitcast.188), channel_id=1, source_target_pairs={{0,3},{1,2},{2,1},{3,0},{4,7},{5,6},{6,5},{7,4},{8,11},{9,10},{10,... | collective-permute-start | bytes 589832 | tf_op jit(solution)/shard_map/ppermute | solution.py:51
  12.0 4.2 %copy.8 = f32[2,128,5120]{2,1,0:T(8,128)S(1)} copy(f32[2,128,5120]{2,0,1:T(2,128)} %bitcast.184) | data formatting | bytes 10485760 | tf_op jit(solution)/shard_map/transpose | solution.py:158
  32.6 4.3 %fusion.154 = (bf16[192,2048]{1,0:T(8,128)(2,1)S(1)}, f32[192,2048]{1,0:T(8,128)S(1)}) fusion(bf16[192,1280]{1,0:T(8,128)(2,1)S(1)} %fusion.100, bf16[1,1,2,2048,1280]{4,3,2,1,0:T(8,128)(2,1)} %param.6), kind=kOutput, calls=%fused_computation.269 | convolution fusion | flops 1007026176 | bytes 8093696 | tf_op jit(solution)/shard_map/dot_general | solution.py:24
  49.5 4.3 %collective-permute-start.10 = (bf16[192,1792]{1,0:T(8,128)(2,1)S(1)}, bf16[192,1792]{1,0:T(8,128)(2,1)S(1)}, u32[]{:S(2)}, u32[]{:S(2)}) collective-permute-start(bf16[192,1792]{1,0:T(8,128)(2,1)S(1)} %get-tuple-element.118), channel_id=1, source_target_pairs={{0,12},{1,13},{2,14},{3,15},{4,8},{5,9},{6,10},{7,11},{8,4},{9,5},... | collective-permute-start | bytes 2064392 | tf_op jit(solution)/shard_map/ppermute | solution.py:51
  57.9 10.7 %collective-permute-done.4 = bf16[48,2048]{1,0:T(8,128)(2,1)S(1)} collective-permute-done((bf16[48,2048]{1,0:T(8,128)(2,1)S(1)}, bf16[48,2048]{1,0:T(8,128)(2,1)S(1)}, u32[]{:S(2)}, u32[]{:S(2)}) %collective-permute-start.4) | collective-permute-done | bytes 196640 | tf_op jit(solution)/shard_map/ppermute | solution.py:51
  73.8 7.7 %collective-permute-done.8 = bf16[192,1792]{1,0:T(8,128)(2,1)S(1)} collective-permute-done((bf16[192,1792]{1,0:T(8,128)(2,1)S(1)}, bf16[192,1792]{1,0:T(8,128)(2,1)S(1)}, u32[]{:S(2)}, u32[]{:S(2)}) %collective-permute-start.8) | collective-permute-done | bytes 688160 | tf_op jit(solution)/shard_map/ppermute | solution.py:51
  90.9 4.6 %multiply_convert_fusion.1 = (bf16[192,1280]{1,0:T(8,128)(2,1)S(1)}, f32[192,1280]{1,0:T(8,128)}) fusion(bf16[192,2048]{1,0:T(8,128)(2,1)S(1)} %fusion.78, bf16[1,1,2,2048,1280]{4,3,2,1,0:T(8,128)(2,1)} %param.6), kind=kOutput, calls=%fused_computation.108 | convolution fusion | flops 1008844800 | bytes 7503872 | tf_op jit(solution)/shard_map/dot_general | solution.py:36
  110.2 6.5 %copy.9 = f32[2,128,5120]{2,1,0:T(8,128)} copy(f32[2,128,5120]{2,0,1:T(2,128)} %bitcast.186) | data formatting | bytes 10485760 | tf_op jit(solution)/shard_map/transpose | solution.py:158
  118.1 6.1 %collective-permute-done.19 = bf16[192,1792]{1,0:T(8,128)(2,1)} collective-permute-done((bf16[192,1792]{1,0:T(8,128)(2,1)S(1)}, bf16[192,1792]{1,0:T(8,128)(2,1)}, u32[]{:S(2)}, u32[]{:S(2)}) %collective-permute-start.19) | collective-permute-done | bytes 688160 | tf_op jit(solution)/shard_map/ppermute | solution.py:51
  124.2 15.0 %collective-permute-done.20 = bf16[192,1792]{1,0:T(8,128)(2,1)} collective-permute-done((bf16[192,1792]{1,0:T(8,128)(2,1)S(1)}, bf16[192,1792]{1,0:T(8,128)(2,1)}, u32[]{:S(2)}, u32[]{:S(2)}) %collective-permute-start.20) | collective-permute-done | bytes 688160 | tf_op jit(solution)/shard_map/ppermute | solution.py:51
  143.3 5.5 %fusion.156 = (bf16[192,2048]{1,0:T(8,128)(2,1)S(1)}, f32[192,2048]{1,0:T(8,128)S(1)}) fusion(bf16[192,512]{1,0:T(8,128)(2,1)S(1)} %get-tuple-element.98, bf16[192,512]{1,0:T(8,128)(2,1)S(1)} %get-tuple-element.99, bf16[192,512]{1,0:T(8,128)(2,1)S(1)} %get-tuple-element.100, bf16[192,512]{1,0:T(8,128)(2,1)S(1)} %get-tuple-element.97, ...), kind=kOutput, calls=%fused_computation.271 | convolution fusion | flops 1016463360 | bytes 11829248 | tf_op jit(solution)/shard_map/dot_general | solution.py:24
  160.3 5.8 %collective-permute-done.23 = bf16[48,2048]{1,0:T(8,128)(2,1)S(1)} collective-permute-done((bf16[48,2048]{1,0:T(8,128)(2,1)S(1)}, bf16[48,2048]{1,0:T(8,128)(2,1)S(1)}, u32[]{:S(2)}, u32[]{:S(2)}) %collective-permute-start.23) | collective-permute-done | bytes 196640 | tf_op jit(solution)/shard_map/ppermute | solution.py:51
  166.2 11.7 %collective-permute-start.28 = (bf16[48,2048]{1,0:T(8,128)(2,1)S(1)}, bf16[48,2048]{1,0:T(8,128)(2,1)S(1)}, u32[]{:S(2)}, u32[]{:S(2)}) collective-permute-start(bf16[48,2048]{1,0:T(8,128)(2,1)S(1)} %fusion.126), channel_id=1, source_target_pairs={{0,19},{1,18},{2,17},{3,16},{4,23},{5,22},{6,21},{7,20},{8,27},{9,... | collective-permute-start | bytes 589832 | tf_op jit(solution)/shard_map/ppermute | solution.py:51
  186.0 8.7 %fusion.51 = bf16[192,2048]{1,0:T(8,128)(2,1)S(1)} fusion(bf16[1,1,2,2048,1280]{4,3,2,1,0:T(8,128)(2,1)} %param.6, bf16[192,2048]{1,0:T(8,128)(2,1)S(1)} %get-tuple-element.40, f32[192]{0:T(256)S(1)} %multiply_multiply_fusion.3, f32[192]{0:T(256)S(1)} %fusion.132, bf16[48,2048]{1,0:T(8,128)(2,1)} %copy-done.15, bf16[48,2048]{1,0:T(8,128)(2,1)} %copy-done.16, ...), kind=kOutput, calls=%fused_computation.53 | convolution fusion | flops 2028453888 | bytes 17073664 | tf_op jit(solution)/shard_map/dot_general | solution.py:24
  200.1 5.0 %collective-permute-done.32 = bf16[48,2048]{1,0:T(8,128)(2,1)S(1)} collective-permute-done((bf16[48,2048]{1,0:T(8,128)(2,1)S(1)}, bf16[48,2048]{1,0:T(8,128)(2,1)S(1)}, u32[]{:S(2)}, u32[]{:S(2)}) %collective-permute-start.32) | collective-permute-done | bytes 196640 | tf_op jit(solution)/shard_map/ppermute | solution.py:51
  205.1 5.3 %collective-permute-done.31 = bf16[48,2048]{1,0:T(8,128)(2,1)S(1)} collective-permute-done((bf16[48,2048]{1,0:T(8,128)(2,1)S(1)}, bf16[48,2048]{1,0:T(8,128)(2,1)S(1)}, u32[]{:S(2)}, u32[]{:S(2)}) %collective-permute-start.31) | collective-permute-done | bytes 196640 | tf_op jit(solution)/shard_map/ppermute | solution.py:51
  219.3 7.4 %fusion.48 = bf16[192,2048]{1,0:T(8,128)(2,1)S(1)} fusion(bf16[1,1,2,2048,1280]{4,3,2,1,0:T(8,128)(2,1)} %param.6, bf16[48,2048]{1,0:T(8,128)(2,1)S(1)} %collective-permute-done.36, bf16[48,2048]{1,0:T(8,128)(2,1)S(1)} %collective-permute-done.35, bf16[48,2048]{1,0:T(8,128)(2,1)S(1)} %collective-permute-done.34, ...), kind=kOutput, calls=%fused_computation.52 | convolution fusion | flops 2021621760 | bytes 13041665 | tf_op jit(solution)/shard_map/dot_general | solution.py:24
  232.6 4.9 %collective-permute-done.40 = bf16[48,2048]{1,0:T(8,128)(2,1)S(1)} collective-permute-done((bf16[48,2048]{1,0:T(8,128)(2,1)S(1)}, bf16[48,2048]{1,0:T(8,128)(2,1)S(1)}, u32[]{:S(2)}, u32[]{:S(2)}) %collective-permute-start.40) | collective-permute-done | bytes 196640 | tf_op jit(solution)/shard_map/ppermute | solution.py:51
  237.5 5.8 %collective-permute-done.39 = bf16[48,2048]{1,0:T(8,128)(2,1)S(1)} collective-permute-done((bf16[48,2048]{1,0:T(8,128)(2,1)S(1)}, bf16[48,2048]{1,0:T(8,128)(2,1)S(1)}, u32[]{:S(2)}, u32[]{:S(2)}) %collective-permute-start.39) | collective-permute-done | bytes 196640 | tf_op jit(solution)/shard_map/ppermute | solution.py:51
  243.8 4.4 %collective-permute-start.43 = (bf16[48,2048]{1,0:T(8,128)(2,1)S(1)}, bf16[48,2048]{1,0:T(8,128)(2,1)S(1)}, u32[]{:S(2)}, u32[]{:S(2)}) collective-permute-start(bf16[48,2048]{1,0:T(8,128)(2,1)S(1)} %fusion.123), channel_id=1, source_target_pairs={{0,3},{1,2},{2,1},{3,0},{4,7},{5,6},{6,5},{7,4},{8,11},{9,10},{10,... | collective-permute-start | bytes 589832 | tf_op jit(solution)/shard_map/ppermute | solution.py:51
  280.2 5.2 %collective-permute-done.45 = bf16[192,1280]{1,0:T(8,128)(2,1)S(1)} collective-permute-done((bf16[192,1280]{1,0:T(8,128)(2,1)S(1)}, bf16[192,1280]{1,0:T(8,128)(2,1)S(1)}, u32[]{:S(2)}, u32[]{:S(2)}) %collective-permute-start.45) | collective-permute-done | bytes 491552 | tf_op jit(solution)/shard_map/ppermute | solution.py:51
  292.9 13.5 %collective-permute-done.54 = bf16[128,1280]{1,0:T(8,128)(2,1)S(1)} collective-permute-done((bf16[128,1280]{1,0:T(8,128)(2,1)S(1)}, bf16[128,1280]{1,0:T(8,128)(2,1)S(1)}, u32[]{:S(2)}, u32[]{:S(2)}) %collective-permute-start.54) | collective-permute-done | bytes 327712 | tf_op jit(solution)/shard_map/ppermute | solution.py:51
  306.7 8.1 %collective-permute-done.48 = bf16[128,1280]{1,0:T(8,128)(2,1)S(1)} collective-permute-done((bf16[128,1280]{1,0:T(8,128)(2,1)S(1)}, bf16[128,1280]{1,0:T(8,128)(2,1)S(1)}, u32[]{:S(2)}, u32[]{:S(2)}) %collective-permute-start.48) | collective-permute-done | bytes 327712 | tf_op jit(solution)/shard_map/ppermute | solution.py:51
  334.4 11.2 %shard_map.76 = (f32[128,2,5120]{2,1,0:T(2,128)}, f32[128,2,5120]{2,1,0:T(2,128)}, f32[1,1]{1,0:T(1,128)}) custom-call(f32[4,1280]{1,0:T(4,128)} %add_add_fusion.1.sums_ref, bf16[128,5120]{1,0:T(8,128)(2,1)} %pad_maximum_fusion.4.in_ref, bf16[128,5120]{1,0:T(8,128)(2,1)} %pad_maximum_fusion.6.out_ref, f32[128,2,5120]{2,1,0:T(2,128)} %bitcast.187, ...), custom_call_target="tpu_custom_call" | custom-call | flops 5242880 | bytes 26214400 | tf_op jit(solution)/shard_map/pallas_call | solution.py:143
  (249 shorter events, 170.8 us)
Async XLA Ops:
  0.6 25.6 %collective-permute-start.2 = (bf16[48,2048]{1,0:T(8,128)(2,1)}, bf16[48,2048]{1,0:T(8,128)(2,1)S(1)}, u32[]{:S(2)}, u32[]{:S(2)}) collective-permute-start(bf16[48,2048]{1,0:T(8,128)(2,1)} %bitcast.188), channel_id=1, source_target_pairs={{0,3},{1,2},{2,1},{3,0},{4,7},{5,6},{6,5},{7,4},{8,11},{9,10},{10,... | collective-permute-start | bytes 589832 | tf_op jit(solution)/shard_map/ppermute | solution.py:51
  7.6 18.6 %collective-permute-start.1 = (bf16[48,2048]{1,0:T(8,128)(2,1)}, bf16[48,2048]{1,0:T(8,128)(2,1)S(1)}, u32[]{:S(2)}, u32[]{:S(2)}) collective-permute-start(bf16[48,2048]{1,0:T(8,128)(2,1)} %bitcast.189), channel_id=1, source_target_pairs={{0,2},{1,3},{2,0},{3,1},{4,6},{5,7},{6,4},{7,5},{8,10},{9,11},{10,... | collective-permute-start | bytes 589832 | tf_op jit(solution)/shard_map/ppermute | solution.py:51
  9.5 18.9 %collective-permute-start = (bf16[48,2048]{1,0:T(8,128)(2,1)}, bf16[48,2048]{1,0:T(8,128)(2,1)S(1)}, u32[]{:S(2)}, u32[]{:S(2)}) collective-permute-start(bf16[48,2048]{1,0:T(8,128)(2,1)} %bitcast.190), channel_id=1, source_target_pairs={{0,1},{1,0},{2,3},{3,2},{4,5},{5,4},{6,7},{7,6},{8,9},{9,8},{10,11... | collective-permute-start | bytes 589832 | tf_op jit(solution)/shard_map/ppermute | solution.py:51
  20.9 51.2 %collective-permute-start.6 = (bf16[2,128,1280]{2,1,0:T(8,128)(2,1)}, bf16[2,128,1280]{2,1,0:T(8,128)(2,1)S(1)}, u32[]{:S(2)}, u32[]{:S(2)}) collective-permute-start(bf16[2,128,1280]{2,1,0:T(8,128)(2,1)} %pad_maximum_fusion.23), channel_id=1, source_target_pairs={{0,1},{1,0},{2,3},{3,2},{4,5},{5,4},{6,7},{7,6},{8,9},{9,8},{10,11... | collective-permute-start | bytes 1966088 | tf_op jit(solution)/shard_map/ppermute | solution.py:51
  23.3 50.5 %collective-permute-start.7 = (bf16[2,128,1280]{2,1,0:T(8,128)(2,1)}, bf16[2,128,1280]{2,1,0:T(8,128)(2,1)}, u32[]{:S(2)}, u32[]{:S(2)}) collective-permute-start(bf16[2,128,1280]{2,1,0:T(8,128)(2,1)} %pad_maximum_fusion.24), channel_id=1, source_target_pairs={{0,2},{1,3},{2,0},{3,1},{4,6},{5,7},{6,4},{7,5},{8,10},{9,11},{10,... | collective-permute-start | bytes 1966088 | tf_op jit(solution)/shard_map/ppermute | solution.py:51
  39.0 15.5 %collective-permute-start.5 = (bf16[48,2048]{1,0:T(8,128)(2,1)S(1)}, bf16[48,2048]{1,0:T(8,128)(2,1)S(1)}, u32[]{:S(2)}, u32[]{:S(2)}) collective-permute-start(bf16[48,2048]{1,0:T(8,128)(2,1)S(1)} %get-tuple-element.113), channel_id=1, source_target_pairs={{0,3},{1,2},{2,1},{3,0},{4,7},{5,6},{6,5},{7,4},{8,11},{9,10},{10,... | collective-permute-start | bytes 589832 | tf_op jit(solution)/shard_map/ppermute | solution.py:51
  42.9 25.7 %collective-permute-start.4 = (bf16[48,2048]{1,0:T(8,128)(2,1)S(1)}, bf16[48,2048]{1,0:T(8,128)(2,1)S(1)}, u32[]{:S(2)}, u32[]{:S(2)}) collective-permute-start(bf16[48,2048]{1,0:T(8,128)(2,1)S(1)} %get-tuple-element.114), channel_id=1, source_target_pairs={{0,2},{1,3},{2,0},{3,1},{4,6},{5,7},{6,4},{7,5},{8,10},{9,11},{10,... | collective-permute-start | bytes 589832 | tf_op jit(solution)/shard_map/ppermute | solution.py:51
  49.5 24.2 %collective-permute-start.10 = (bf16[192,1792]{1,0:T(8,128)(2,1)S(1)}, bf16[192,1792]{1,0:T(8,128)(2,1)S(1)}, u32[]{:S(2)}, u32[]{:S(2)}) collective-permute-start(bf16[192,1792]{1,0:T(8,128)(2,1)S(1)} %get-tuple-element.118), channel_id=1, source_target_pairs={{0,12},{1,13},{2,14},{3,15},{4,8},{5,9},{6,10},{7,11},{8,4},{9,5},... | collective-permute-start | bytes 2064392 | tf_op jit(solution)/shard_map/ppermute | solution.py:51
  54.5 19.3 %collective-permute-start.9 = (bf16[192,1792]{1,0:T(8,128)(2,1)S(1)}, bf16[192,1792]{1,0:T(8,128)(2,1)S(1)}, u32[]{:S(2)}, u32[]{:S(2)}) collective-permute-start(bf16[192,1792]{1,0:T(8,128)(2,1)S(1)} %get-tuple-element.119), channel_id=1, source_target_pairs={{0,8},{1,9},{2,10},{3,11},{4,12},{5,13},{6,14},{7,15},{8,0},{9,1},... | collective-permute-start | bytes 2064392 | tf_op jit(solution)/shard_map/ppermute | solution.py:51
  72.1 18.2 %collective-permute-start.15 = (bf16[2,128,1280]{2,1,0:T(8,128)(2,1)S(1)}, bf16[2,128,1280]{2,1,0:T(8,128)(2,1)S(1)}, u32[]{:S(2)}, u32[]{:S(2)}) collective-permute-start(bf16[2,128,1280]{2,1,0:T(8,128)(2,1)S(1)} %pad_maximum_fusion.25), channel_id=1, source_target_pairs={{0,3},{1,2},{2,1},{3,0},{4,7},{5,6},{6,5},{7,4},{8,11},{9,10},{10,... | collective-permute-start | bytes 1966088 | tf_op jit(solution)/shard_map/ppermute | solution.py:51
  105.7 18.5 %collective-permute-start.19 = (bf16[192,1792]{1,0:T(8,128)(2,1)S(1)}, bf16[192,1792]{1,0:T(8,128)(2,1)}, u32[]{:S(2)}, u32[]{:S(2)}) collective-permute-start(bf16[192,1792]{1,0:T(8,128)(2,1)S(1)} %pad_maximum_fusion.20), channel_id=1, source_target_pairs={{0,4},{1,5},{2,6},{3,7},{4,0},{5,1},{6,2},{7,3},{8,12},{9,13},{10,... | collective-permute-start | bytes 2064392 | tf_op jit(solution)/shard_map/ppermute | solution.py:51
  107.2 32.0 %collective-permute-start.20 = (bf16[192,1792]{1,0:T(8,128)(2,1)S(1)}, bf16[192,1792]{1,0:T(8,128)(2,1)}, u32[]{:S(2)}, u32[]{:S(2)}) collective-permute-start(bf16[192,1792]{1,0:T(8,128)(2,1)S(1)} %pad_maximum_fusion.21), channel_id=1, source_target_pairs={{0,8},{1,9},{2,10},{3,11},{4,12},{5,13},{6,14},{7,15},{8,0},{9,1},... | collective-permute-start | bytes 2064392 | tf_op jit(solution)/shard_map/ppermute | solution.py:51
  109.7 29.5 %collective-permute-start.21 = (bf16[192,1792]{1,0:T(8,128)(2,1)}, bf16[192,1792]{1,0:T(8,128)(2,1)}, u32[]{:S(2)}, u32[]{:S(2)}) collective-permute-start(bf16[192,1792]{1,0:T(8,128)(2,1)} %pad_maximum_fusion.22), channel_id=1, source_target_pairs={{0,12},{1,13},{2,14},{3,15},{4,8},{5,9},{6,10},{7,11},{8,4},{9,5},... | collective-permute-start | bytes 2064392 | tf_op jit(solution)/shard_map/ppermute | solution.py:51
  166.2 15.6 %collective-permute-start.28 = (bf16[48,2048]{1,0:T(8,128)(2,1)S(1)}, bf16[48,2048]{1,0:T(8,128)(2,1)S(1)}, u32[]{:S(2)}, u32[]{:S(2)}) collective-permute-start(bf16[48,2048]{1,0:T(8,128)(2,1)S(1)} %fusion.126), channel_id=1, source_target_pairs={{0,19},{1,18},{2,17},{3,16},{4,23},{5,22},{6,21},{7,20},{8,27},{9,... | collective-permute-start | bytes 589832 | tf_op jit(solution)/shard_map/ppermute | solution.py:51
  197.5 12.9 %collective-permute-start.31 = (bf16[48,2048]{1,0:T(8,128)(2,1)S(1)}, bf16[48,2048]{1,0:T(8,128)(2,1)S(1)}, u32[]{:S(2)}, u32[]{:S(2)}) collective-permute-start(bf16[48,2048]{1,0:T(8,128)(2,1)S(1)} %get-tuple-element.92), channel_id=1, source_target_pairs={{16,2},{17,3},{18,0},{19,1},{20,6},{21,7},{22,4},{23,5},{24,10},{2... | collective-permute-start | bytes 589832 | tf_op jit(solution)/shard_map/ppermute | solution.py:51
  229.3 14.0 %collective-permute-start.39 = (bf16[48,2048]{1,0:T(8,128)(2,1)S(1)}, bf16[48,2048]{1,0:T(8,128)(2,1)S(1)}, u32[]{:S(2)}, u32[]{:S(2)}) collective-permute-start(bf16[48,2048]{1,0:T(8,128)(2,1)S(1)} %get-tuple-element.88), channel_id=1, source_target_pairs={{16,2},{17,3},{18,0},{19,1},{20,6},{21,7},{22,4},{23,5},{24,10},{2... | collective-permute-start | bytes 589832 | tf_op jit(solution)/shard_map/ppermute | solution.py:51
  271.9 13.4 %collective-permute-start.45 = (bf16[192,1280]{1,0:T(8,128)(2,1)S(1)}, bf16[192,1280]{1,0:T(8,128)(2,1)S(1)}, u32[]{:S(2)}, u32[]{:S(2)}) collective-permute-start(bf16[192,1280]{1,0:T(8,128)(2,1)S(1)} %fusion.54), channel_id=1, source_target_pairs={{0,8},{1,9},{2,10},{3,11},{4,12},{5,13},{6,14},{7,15},{8,0},{9,1},... | collective-permute-start | bytes 1474568 | tf_op jit(solution)/shard_map/ppermute | solution.py:51
  272.4 13.5 %collective-permute-start.44 = (bf16[192,1280]{1,0:T(8,128)(2,1)S(1)}, bf16[192,1280]{1,0:T(8,128)(2,1)S(1)}, u32[]{:S(2)}, u32[]{:S(2)}) collective-permute-start(bf16[192,1280]{1,0:T(8,128)(2,1)S(1)} %fusion.54), channel_id=1, source_target_pairs={{0,4},{1,5},{2,6},{3,7},{4,0},{5,1},{6,2},{7,3},{8,12},{9,13},{10,... | collective-permute-start | bytes 1474568 | tf_op jit(solution)/shard_map/ppermute | solution.py:51
  275.2 15.0 %collective-permute-start.55 = (bf16[128,1280]{1,0:T(8,128)(2,1)S(1)}, bf16[128,1280]{1,0:T(8,128)(2,1)S(1)}, u32[]{:S(2)}, u32[]{:S(2)}) collective-permute-start(bf16[128,1280]{1,0:T(8,128)(2,1)S(1)} %get-tuple-element.71), channel_id=1, source_target_pairs={{0,3},{1,2},{2,1},{3,0},{4,7},{5,6},{6,5},{7,4},{8,11},{9,10},{10,... | collective-permute-start | bytes 983048 | tf_op jit(solution)/shard_map/ppermute | solution.py:51
  278.7 27.7 %collective-permute-start.54 = (bf16[128,1280]{1,0:T(8,128)(2,1)S(1)}, bf16[128,1280]{1,0:T(8,128)(2,1)S(1)}, u32[]{:S(2)}, u32[]{:S(2)}) collective-permute-start(bf16[128,1280]{1,0:T(8,128)(2,1)S(1)} %get-tuple-element.72), channel_id=1, source_target_pairs={{0,2},{1,3},{2,0},{3,1},{4,6},{5,7},{6,4},{7,5},{8,10},{9,11},{10,... | collective-permute-start | bytes 983048 | tf_op jit(solution)/shard_map/ppermute | solution.py:51
  280.2 26.2 %collective-permute-start.53 = (bf16[128,1280]{1,0:T(8,128)(2,1)S(1)}, bf16[128,1280]{1,0:T(8,128)(2,1)S(1)}, u32[]{:S(2)}, u32[]{:S(2)}) collective-permute-start(bf16[128,1280]{1,0:T(8,128)(2,1)S(1)} %get-tuple-element.73), channel_id=1, source_target_pairs={{0,1},{1,0},{2,3},{3,2},{4,5},{5,4},{6,7},{7,6},{8,9},{9,8},{10,11... | collective-permute-start | bytes 983048 | tf_op jit(solution)/shard_map/ppermute | solution.py:51
  287.3 19.4 %collective-permute-start.49 = (bf16[128,1280]{1,0:T(8,128)(2,1)S(1)}, bf16[128,1280]{1,0:T(8,128)(2,1)S(1)}, u32[]{:S(2)}, u32[]{:S(2)}) collective-permute-start(bf16[128,1280]{1,0:T(8,128)(2,1)S(1)} %get-tuple-element.63), channel_id=1, source_target_pairs={{0,3},{1,2},{2,1},{3,0},{4,7},{5,6},{6,5},{7,4},{8,11},{9,10},{10,... | collective-permute-start | bytes 983048 | tf_op jit(solution)/shard_map/ppermute | solution.py:51
  290.2 24.6 %collective-permute-start.48 = (bf16[128,1280]{1,0:T(8,128)(2,1)S(1)}, bf16[128,1280]{1,0:T(8,128)(2,1)S(1)}, u32[]{:S(2)}, u32[]{:S(2)}) collective-permute-start(bf16[128,1280]{1,0:T(8,128)(2,1)S(1)} %get-tuple-element.64), channel_id=1, source_target_pairs={{0,2},{1,3},{2,0},{3,1},{4,6},{5,7},{6,4},{7,5},{8,10},{9,11},{10,... | collective-permute-start | bytes 983048 | tf_op jit(solution)/shard_map/ppermute | solution.py:51
  290.2 24.6 %collective-permute-start.47 = (bf16[128,1280]{1,0:T(8,128)(2,1)S(1)}, bf16[128,1280]{1,0:T(8,128)(2,1)S(1)}, u32[]{:S(2)}, u32[]{:S(2)}) collective-permute-start(bf16[128,1280]{1,0:T(8,128)(2,1)S(1)} %get-tuple-element.65), channel_id=1, source_target_pairs={{0,1},{1,0},{2,3},{3,2},{4,5},{5,4},{6,7},{7,6},{8,9},{9,8},{10,11... | collective-permute-start | bytes 983048 | tf_op jit(solution)/shard_map/ppermute | solution.py:51
  (65 other events, 526.7 us)

commit v7 on v6

--- a/solution.py
+++ b/solution.py
@@ -86,6 +86,10 @@
     for k in range(1, lax.axis_size("task")):
         parts.append(send(value_of(k), route(k)))
     return parts
+
+
+def across(k, held_by):
+    return lambda s, t, f: (s, t, f ^ k) if s in held_by else None
 
 
 def fsdp_partners(value_of):
@@ -184,7 +188,9 @@
         at = (shard_id ^ k) * hidden
         return jnp.stack([lax.dynamic_slice_in_dim(part, at, hidden, 1) for part in narrow])
 
-    pieces = fsdp_partners(direction_for)
+    chunks = [direction_for(k) for k in range(shards)]
+    pieces = [chunks[0]] + [send(chunks[k], across(k, range(sections))) for k in range(1, shards - 1)]
+    pieces.append(send(chunks[-1], across(shards - 1, range(sections - 1))))
 
     def features_for(array):
         return lambda k: lax.dynamic_slice_in_dim(array, (task_id ^ k) * block, block, 1)
@@ -213,7 +219,9 @@
             own_inputs.append(own_rows)
             arrived = gather_rows(own_rows, 0, layer + 1)
             if layer == 0:
-                arrived, pieces[3] = tie(arrived, pieces[3])
+                arrived, (chunks[-1], pieces[-1]) = tie(arrived, (chunks[-1], pieces[-1]))
+                late = send(chunks[-1], across(shards - 1, [sections - 1]))
+                pieces[-1] = jnp.where(section_id == sections - 1, late, pieces[-1])
             rows_all = jnp.where(section_id == layer + 1, arrived, rows_all)
 
     steering = in_order(pieces, shard_id, 1)

time: 347 us -> 341 us (0.983)
  waiting for transfers between devices: 124 us -> 108 us
  starting transfers between devices: 125 us -> 135 us
    ppermute x56 -> x57, waiting for transfers between devices: 121 us -> 104 us  [send(): return lax.ppermute(value, ALL, pairs)]
    ppermute x56 -> x57, starting transfers between devices: 117 us -> 127 us  [send(): return lax.ppermute(value, ALL, pairs)]
  transfers between devices with their start and end apart: 63 -> 64, of which waited for: 31 -> 31; matrix products, arithmetic and copies ran while one was open for 11% -> 12% of each run, Pallas kernels for 0% -> 0%
where the time goes in v7:
time: 341 us; the launch traced here: 340 us
  starting transfers between devices  135 us (40%)
  waiting for transfers between devices  108 us (32%)
  matrix products  45 us (13%)
  local copies, waits for them, and re-layouts  23.3 us (7%)
  other arithmetic  14.9 us (4%)
  Pallas kernels  11.3 us (3%)
    ppermute x57, starting transfers between devices, send(): return lax.ppermute(value, ALL, pairs)  127 us
    ppermute x57, waiting for transfers between devices, send(): return lax.ppermute(value, ALL, pairs)  104 us
    dot_general x5, matrix products, across_hidden(): lax.dot_general(left_side, right_side, (((1,), (1,)), ((), ())), preferre...  27.1 us
    dot_general x4, matrix products, dot(): return jnp.dot(left_side, right_side, preferred_element_type=jnp.float32)  15.4 us
    pallas_call x1, Pallas kernels, update(): pl.pallas_call(update_kernel, grid=(total // columns,), in_specs=[pl.Bloc...  11.3 us
    transpose x2, local copies, waits for them, and re-layouts, apart(): jnp.transpose(array, (1, 0, 2))  10.7 us
    ppermute x7, starting transfers between devices, sum_everywhere(): parts.append(lax.ppermute(value, axis, [(i, i ^ k) for i in range(count)]))  8.08 us
  transfers between devices with their start and end apart: 64, of which 31 were waited for; matrix products, arithmetic and copies ran while one was open for 12% of the time, Pallas kernels for 0%

profile of v7, /device:TPU:0, one launch (start us, length us, event | category | flops | bytes accessed | tf_op | source)
XLA Modules:
  0.0 340.0 jit_solution(16210049504202522848)
XLA Ops:
  0.6 7.0 %collective-permute-start.2 = (bf16[48,2048]{1,0:T(8,128)(2,1)}, bf16[48,2048]{1,0:T(8,128)(2,1)S(1)}, u32[]{:S(2)}, u32[]{:S(2)}) collective-permute-start(bf16[48,2048]{1,0:T(8,128)(2,1)} %bitcast.189), channel_id=1, source_target_pairs={{0,3},{1,2},{2,1},{3,0},{4,7},{5,6},{6,5},{7,4},{8,11},{9,10},{10,... | collective-permute-start | bytes 589832 | tf_op jit(solution)/shard_map/ppermute | solution.py:51
  49.5 4.3 %collective-permute-start.10 = (bf16[192,1792]{1,0:T(8,128)(2,1)S(1)}, bf16[192,1792]{1,0:T(8,128)(2,1)S(1)}, u32[]{:S(2)}, u32[]{:S(2)}) collective-permute-start(bf16[192,1792]{1,0:T(8,128)(2,1)S(1)} %get-tuple-element.120), channel_id=1, source_target_pairs={{0,12},{1,13},{2,14},{3,15},{4,8},{5,9},{6,10},{7,11},{8,4},{9,5},... | collective-permute-start | bytes 2064392 | tf_op jit(solution)/shard_map/ppermute | solution.py:51
  60.4 5.0 %collective-permute-start.15 = (bf16[2,128,1280]{2,1,0:T(8,128)(2,1)S(1)}, bf16[2,128,1280]{2,1,0:T(8,128)(2,1)S(1)}, u32[]{:S(2)}, u32[]{:S(2)}) collective-permute-start(bf16[2,128,1280]{2,1,0:T(8,128)(2,1)S(1)} %pad_maximum_fusion.25), channel_id=1, source_target_pairs={{0,3},{1,2},{2,1},{3,0},{4,7},{5,6},{6,5},{7,4},{8,11},{9,10},{10,... | collective-permute-start | bytes 1966088 | tf_op jit(solution)/shard_map/ppermute | solution.py:51
  65.5 5.1 %collective-permute-done.9 = bf16[192,1792]{1,0:T(8,128)(2,1)S(1)} collective-permute-done((bf16[192,1792]{1,0:T(8,128)(2,1)S(1)}, bf16[192,1792]{1,0:T(8,128)(2,1)S(1)}, u32[]{:S(2)}, u32[]{:S(2)}) %collective-permute-start.9) | collective-permute-done | bytes 688160 | tf_op jit(solution)/shard_map/ppermute | solution.py:51
  81.3 4.6 %multiply_convert_fusion.1 = (bf16[192,1280]{1,0:T(8,128)(2,1)S(1)}, f32[192,1280]{1,0:T(8,128)}) fusion(bf16[192,2048]{1,0:T(8,128)(2,1)S(1)} %fusion.78, bf16[1,1,2,2048,1280]{4,3,2,1,0:T(8,128)(2,1)} %param.6), kind=kOutput, calls=%fused_computation.108 | convolution fusion | flops 1008844800 | bytes 7503872 | tf_op jit(solution)/shard_map/dot_general | solution.py:36
  100.7 6.5 %copy.9 = f32[2,128,5120]{2,1,0:T(8,128)} copy(f32[2,128,5120]{2,0,1:T(2,128)} %bitcast.187) | data formatting | bytes 10485760 | tf_op jit(solution)/shard_map/transpose | solution.py:162
  112.3 15.7 %collective-permute-done.22 = bf16[192,1792]{1,0:T(8,128)(2,1)} collective-permute-done((bf16[192,1792]{1,0:T(8,128)(2,1)}, bf16[192,1792]{1,0:T(8,128)(2,1)}, u32[]{:S(2)}, u32[]{:S(2)}) %collective-permute-start.22) | collective-permute-done | bytes 688160 | tf_op jit(solution)/shard_map/ppermute | solution.py:51
  132.1 5.5 %fusion.156 = (bf16[192,2048]{1,0:T(8,128)(2,1)S(1)}, f32[192,2048]{1,0:T(8,128)S(1)}) fusion(bf16[192,512]{1,0:T(8,128)(2,1)S(1)} %get-tuple-element.100, bf16[192,512]{1,0:T(8,128)(2,1)S(1)} %get-tuple-element.101, bf16[192,512]{1,0:T(8,128)(2,1)S(1)} %get-tuple-element.102, bf16[192,512]{1,0:T(8,128)(2,1)S(1)} %get-tuple-element.99, ...), kind=kOutput, calls=%fused_computation.272 | convolution fusion | flops 1016463360 | bytes 11829248 | tf_op jit(solution)/shard_map/dot_general | solution.py:24
  137.6 7.7 %collective-permute-start.23 = (bf16[48,2048]{1,0:T(8,128)(2,1)S(1)}, bf16[48,2048]{1,0:T(8,128)(2,1)S(1)}, u32[]{:S(2)}, u32[]{:S(2)}) collective-permute-start(bf16[48,2048]{1,0:T(8,128)(2,1)S(1)} %get-tuple-element.96), channel_id=1, source_target_pairs={{0,1},{1,0},{2,3},{3,2},{4,5},{5,4},{6,7},{7,6},{8,9},{9,8},{10,11... | collective-permute-start | bytes 589832 | tf_op jit(solution)/shard_map/ppermute | solution.py:51
  145.3 4.6 %collective-permute-start.25 = (bf16[48,2048]{1,0:T(8,128)(2,1)S(1)}, bf16[48,2048]{1,0:T(8,128)(2,1)S(1)}, u32[]{:S(2)}, u32[]{:S(2)}) collective-permute-start(bf16[48,2048]{1,0:T(8,128)(2,1)S(1)} %get-tuple-element.97), channel_id=1, source_target_pairs={{0,3},{1,2},{2,1},{3,0},{4,7},{5,6},{6,5},{7,4},{8,11},{9,10},{10,... | collective-permute-start | bytes 589832 | tf_op jit(solution)/shard_map/ppermute | solution.py:51
  159.1 12.8 %collective-permute-start.29 = (bf16[48,2048]{1,0:T(8,128)(2,1)S(1)}, bf16[48,2048]{1,0:T(8,128)(2,1)S(1)}, u32[]{:S(2)}, u32[]{:S(2)}) collective-permute-start(bf16[48,2048]{1,0:T(8,128)(2,1)S(1)} %fusion.126), channel_id=1, source_target_pairs={{0,19},{1,18},{2,17},{3,16},{4,23},{5,22},{6,21},{7,20},{8,27},{9,... | collective-permute-start | bytes 589832 | tf_op jit(solution)/shard_map/ppermute | solution.py:51
  180.1 8.8 %fusion.51 = bf16[192,2048]{1,0:T(8,128)(2,1)S(1)} fusion(bf16[1,1,2,2048,1280]{4,3,2,1,0:T(8,128)(2,1)} %param.6, bf16[192,2048]{1,0:T(8,128)(2,1)S(1)} %get-tuple-element.42, f32[192]{0:T(256)S(1)} %multiply_multiply_fusion.3, f32[192]{0:T(256)S(1)} %fusion.132, bf16[48,2048]{1,0:T(8,128)(2,1)} %copy-done.15, bf16[48,2048]{1,0:T(8,128)(2,1)} %copy-done.16, ...), kind=kOutput, calls=%fused_computation.53 | convolution fusion | flops 2028453888 | bytes 17073664 | tf_op jit(solution)/shard_map/dot_general | solution.py:24
  194.2 5.1 %collective-permute-done.33 = bf16[48,2048]{1,0:T(8,128)(2,1)S(1)} collective-permute-done((bf16[48,2048]{1,0:T(8,128)(2,1)S(1)}, bf16[48,2048]{1,0:T(8,128)(2,1)S(1)}, u32[]{:S(2)}, u32[]{:S(2)}) %collective-permute-start.33) | collective-permute-done | bytes 196640 | tf_op jit(solution)/shard_map/ppermute | solution.py:51
  199.2 5.2 %collective-permute-done.32 = bf16[48,2048]{1,0:T(8,128)(2,1)S(1)} collective-permute-done((bf16[48,2048]{1,0:T(8,128)(2,1)S(1)}, bf16[48,2048]{1,0:T(8,128)(2,1)S(1)}, u32[]{:S(2)}, u32[]{:S(2)}) %collective-permute-start.32) | collective-permute-done | bytes 196640 | tf_op jit(solution)/shard_map/ppermute | solution.py:51
  213.4 7.4 %fusion.48 = bf16[192,2048]{1,0:T(8,128)(2,1)S(1)} fusion(bf16[1,1,2,2048,1280]{4,3,2,1,0:T(8,128)(2,1)} %param.6, bf16[48,2048]{1,0:T(8,128)(2,1)S(1)} %collective-permute-done.37, bf16[48,2048]{1,0:T(8,128)(2,1)S(1)} %collective-permute-done.36, bf16[48,2048]{1,0:T(8,128)(2,1)S(1)} %collective-permute-done.35, ...), kind=kOutput, calls=%fused_computation.52 | convolution fusion | flops 2021621760 | bytes 13041665 | tf_op jit(solution)/shard_map/dot_general | solution.py:24
  226.0 5.7 %collective-permute-done.41 = bf16[48,2048]{1,0:T(8,128)(2,1)S(1)} collective-permute-done((bf16[48,2048]{1,0:T(8,128)(2,1)S(1)}, bf16[48,2048]{1,0:T(8,128)(2,1)S(1)}, u32[]{:S(2)}, u32[]{:S(2)}) %collective-permute-start.41) | collective-permute-done | bytes 196640 | tf_op jit(solution)/shard_map/ppermute | solution.py:51
  231.7 5.7 %collective-permute-done.40 = bf16[48,2048]{1,0:T(8,128)(2,1)S(1)} collective-permute-done((bf16[48,2048]{1,0:T(8,128)(2,1)S(1)}, bf16[48,2048]{1,0:T(8,128)(2,1)S(1)}, u32[]{:S(2)}, u32[]{:S(2)}) %collective-permute-start.40) | collective-permute-done | bytes 196640 | tf_op jit(solution)/shard_map/ppermute | solution.py:51
  243.1 5.0 %collective-permute-start.42 = (bf16[48,2048]{1,0:T(8,128)(2,1)S(1)}, bf16[48,2048]{1,0:T(8,128)(2,1)S(1)}, u32[]{:S(2)}, u32[]{:S(2)}) collective-permute-start(bf16[48,2048]{1,0:T(8,128)(2,1)S(1)} %fusion.123), channel_id=1, source_target_pairs={{0,1},{1,0},{2,3},{3,2},{4,5},{5,4},{6,7},{7,6},{8,9},{9,8},{10,11... | collective-permute-start | bytes 589832 | tf_op jit(solution)/shard_map/ppermute | solution.py:51
  252.0 5.7 %collective-permute-done.42 = bf16[48,2048]{1,0:T(8,128)(2,1)S(1)} collective-permute-done((bf16[48,2048]{1,0:T(8,128)(2,1)S(1)}, bf16[48,2048]{1,0:T(8,128)(2,1)S(1)}, u32[]{:S(2)}, u32[]{:S(2)}) %collective-permute-start.42) | collective-permute-done | bytes 196640 | tf_op jit(solution)/shard_map/ppermute | solution.py:51
  275.5 5.2 %collective-permute-done.46 = bf16[192,1280]{1,0:T(8,128)(2,1)S(1)} collective-permute-done((bf16[192,1280]{1,0:T(8,128)(2,1)S(1)}, bf16[192,1280]{1,0:T(8,128)(2,1)S(1)}, u32[]{:S(2)}, u32[]{:S(2)}) %collective-permute-start.46) | collective-permute-done | bytes 491552 | tf_op jit(solution)/shard_map/ppermute | solution.py:51
  283.1 9.1 %collective-permute-start.48 = (bf16[128,1280]{1,0:T(8,128)(2,1)S(1)}, bf16[128,1280]{1,0:T(8,128)(2,1)S(1)}, u32[]{:S(2)}, u32[]{:S(2)}) collective-permute-start(bf16[128,1280]{1,0:T(8,128)(2,1)S(1)} %get-tuple-element.67), channel_id=1, source_target_pairs={{0,1},{1,0},{2,3},{3,2},{4,5},{5,4},{6,7},{7,6},{8,9},{9,8},{10,11... | collective-permute-start | bytes 983048 | tf_op jit(solution)/shard_map/ppermute | solution.py:51
  292.3 8.6 %collective-permute-done.55 = bf16[128,1280]{1,0:T(8,128)(2,1)S(1)} collective-permute-done((bf16[128,1280]{1,0:T(8,128)(2,1)S(1)}, bf16[128,1280]{1,0:T(8,128)(2,1)S(1)}, u32[]{:S(2)}, u32[]{:S(2)}) %collective-permute-start.55) | collective-permute-done | bytes 327712 | tf_op jit(solution)/shard_map/ppermute | solution.py:51
  301.2 6.7 %collective-permute-done.49 = bf16[128,1280]{1,0:T(8,128)(2,1)S(1)} collective-permute-done((bf16[128,1280]{1,0:T(8,128)(2,1)S(1)}, bf16[128,1280]{1,0:T(8,128)(2,1)S(1)}, u32[]{:S(2)}, u32[]{:S(2)}) %collective-permute-start.49) | collective-permute-done | bytes 327712 | tf_op jit(solution)/shard_map/ppermute | solution.py:51
  328.7 11.3 %shard_map.76 = (f32[128,2,5120]{2,1,0:T(2,128)}, f32[128,2,5120]{2,1,0:T(2,128)}, f32[1,1]{1,0:T(1,128)}) custom-call(f32[4,1280]{1,0:T(4,128)} %add_add_fusion.1.sums_ref, bf16[128,5120]{1,0:T(8,128)(2,1)} %pad_maximum_fusion.4.in_ref, bf16[128,5120]{1,0:T(8,128)(2,1)} %pad_maximum_fusion.6.out_ref, f32[128,2,5120]{2,1,0:T(2,128)} %bitcast.188, ...), custom_call_target="tpu_custom_call" | custom-call | flops 5242880 | bytes 26214400 | tf_op jit(solution)/shard_map/pallas_call | solution.py:147
  (252 shorter events, 169.9 us)
Async XLA Ops:
  0.6 25.5 %collective-permute-start.2 = (bf16[48,2048]{1,0:T(8,128)(2,1)}, bf16[48,2048]{1,0:T(8,128)(2,1)S(1)}, u32[]{:S(2)}, u32[]{:S(2)}) collective-permute-start(bf16[48,2048]{1,0:T(8,128)(2,1)} %bitcast.189), channel_id=1, source_target_pairs={{0,3},{1,2},{2,1},{3,0},{4,7},{5,6},{6,5},{7,4},{8,11},{9,10},{10,... | collective-permute-start | bytes 589832 | tf_op jit(solution)/shard_map/ppermute | solution.py:51
  7.6 18.6 %collective-permute-start.1 = (bf16[48,2048]{1,0:T(8,128)(2,1)}, bf16[48,2048]{1,0:T(8,128)(2,1)S(1)}, u32[]{:S(2)}, u32[]{:S(2)}) collective-permute-start(bf16[48,2048]{1,0:T(8,128)(2,1)} %bitcast.190), channel_id=1, source_target_pairs={{0,2},{1,3},{2,0},{3,1},{4,6},{5,7},{6,4},{7,5},{8,10},{9,11},{10,... | collective-permute-start | bytes 589832 | tf_op jit(solution)/shard_map/ppermute | solution.py:51
  9.5 18.9 %collective-permute-start = (bf16[48,2048]{1,0:T(8,128)(2,1)}, bf16[48,2048]{1,0:T(8,128)(2,1)S(1)}, u32[]{:S(2)}, u32[]{:S(2)}) collective-permute-start(bf16[48,2048]{1,0:T(8,128)(2,1)} %bitcast.191), channel_id=1, source_target_pairs={{0,1},{1,0},{2,3},{3,2},{4,5},{5,4},{6,7},{7,6},{8,9},{9,8},{10,11... | collective-permute-start | bytes 589832 | tf_op jit(solution)/shard_map/ppermute | solution.py:51
  20.9 39.5 %collective-permute-start.6 = (bf16[2,128,1280]{2,1,0:T(8,128)(2,1)}, bf16[2,128,1280]{2,1,0:T(8,128)(2,1)S(1)}, u32[]{:S(2)}, u32[]{:S(2)}) collective-permute-start(bf16[2,128,1280]{2,1,0:T(8,128)(2,1)} %pad_maximum_fusion.23), channel_id=1, source_target_pairs={{0,1},{1,0},{2,3},{3,2},{4,5},{5,4},{6,7},{7,6},{8,9},{9,8},{10,11... | collective-permute-start | bytes 1966088 | tf_op jit(solution)/shard_map/ppermute | solution.py:51
  23.3 42.2 %collective-permute-start.7 = (bf16[2,128,1280]{2,1,0:T(8,128)(2,1)}, bf16[2,128,1280]{2,1,0:T(8,128)(2,1)}, u32[]{:S(2)}, u32[]{:S(2)}) collective-permute-start(bf16[2,128,1280]{2,1,0:T(8,128)(2,1)} %pad_maximum_fusion.24), channel_id=1, source_target_pairs={{0,2},{1,3},{2,0},{3,1},{4,6},{5,7},{6,4},{7,5},{8,10},{9,11},{10,... | collective-permute-start | bytes 1966088 | tf_op jit(solution)/shard_map/ppermute | solution.py:51
  39.0 14.9 %collective-permute-start.5 = (bf16[48,2048]{1,0:T(8,128)(2,1)S(1)}, bf16[48,2048]{1,0:T(8,128)(2,1)S(1)}, u32[]{:S(2)}, u32[]{:S(2)}) collective-permute-start(bf16[48,2048]{1,0:T(8,128)(2,1)S(1)} %get-tuple-element.115), channel_id=1, source_target_pairs={{0,3},{1,2},{2,1},{3,0},{4,7},{5,6},{6,5},{7,4},{8,11},{9,10},{10,... | collective-permute-start | bytes 589832 | tf_op jit(solution)/shard_map/ppermute | solution.py:51
  43.0 13.9 %collective-permute-start.4 = (bf16[48,2048]{1,0:T(8,128)(2,1)S(1)}, bf16[48,2048]{1,0:T(8,128)(2,1)S(1)}, u32[]{:S(2)}, u32[]{:S(2)}) collective-permute-start(bf16[48,2048]{1,0:T(8,128)(2,1)S(1)} %get-tuple-element.116), channel_id=1, source_target_pairs={{0,2},{1,3},{2,0},{3,1},{4,6},{5,7},{6,4},{7,5},{8,10},{9,11},{10,... | collective-permute-start | bytes 589832 | tf_op jit(solution)/shard_map/ppermute | solution.py:51
  49.5 16.0 %collective-permute-start.10 = (bf16[192,1792]{1,0:T(8,128)(2,1)S(1)}, bf16[192,1792]{1,0:T(8,128)(2,1)S(1)}, u32[]{:S(2)}, u32[]{:S(2)}) collective-permute-start(bf16[192,1792]{1,0:T(8,128)(2,1)S(1)} %get-tuple-element.120), channel_id=1, source_target_pairs={{0,12},{1,13},{2,14},{3,15},{4,8},{5,9},{6,10},{7,11},{8,4},{9,5},... | collective-permute-start | bytes 2064392 | tf_op jit(solution)/shard_map/ppermute | solution.py:51
  53.9 16.7 %collective-permute-start.9 = (bf16[192,1792]{1,0:T(8,128)(2,1)S(1)}, bf16[192,1792]{1,0:T(8,128)(2,1)S(1)}, u32[]{:S(2)}, u32[]{:S(2)}) collective-permute-start(bf16[192,1792]{1,0:T(8,128)(2,1)S(1)} %get-tuple-element.121), channel_id=1, source_target_pairs={{0,8},{1,9},{2,10},{3,11},{4,12},{5,13},{6,14},{7,15},{8,0},{9,1},... | collective-permute-start | bytes 2064392 | tf_op jit(solution)/shard_map/ppermute | solution.py:51
  56.9 13.8 %collective-permute-start.8 = (bf16[192,1792]{1,0:T(8,128)(2,1)S(1)}, bf16[192,1792]{1,0:T(8,128)(2,1)S(1)}, u32[]{:S(2)}, u32[]{:S(2)}) collective-permute-start(bf16[192,1792]{1,0:T(8,128)(2,1)S(1)} %get-tuple-element.122), channel_id=1, source_target_pairs={{0,4},{1,5},{2,6},{3,7},{4,0},{5,1},{6,2},{7,3},{8,12},{9,13},{10,... | collective-permute-start | bytes 2064392 | tf_op jit(solution)/shard_map/ppermute | solution.py:51
  60.4 19.5 %collective-permute-start.15 = (bf16[2,128,1280]{2,1,0:T(8,128)(2,1)S(1)}, bf16[2,128,1280]{2,1,0:T(8,128)(2,1)S(1)}, u32[]{:S(2)}, u32[]{:S(2)}) collective-permute-start(bf16[2,128,1280]{2,1,0:T(8,128)(2,1)S(1)} %pad_maximum_fusion.25), channel_id=1, source_target_pairs={{0,3},{1,2},{2,1},{3,0},{4,7},{5,6},{6,5},{7,4},{8,11},{9,10},{10,... | collective-permute-start | bytes 1966088 | tf_op jit(solution)/shard_map/ppermute | solution.py:51
  96.1 15.8 %collective-permute-start.20 = (bf16[192,1792]{1,0:T(8,128)(2,1)S(1)}, bf16[192,1792]{1,0:T(8,128)(2,1)}, u32[]{:S(2)}, u32[]{:S(2)}) collective-permute-start(bf16[192,1792]{1,0:T(8,128)(2,1)S(1)} %pad_maximum_fusion.20), channel_id=1, source_target_pairs={{0,4},{1,5},{2,6},{3,7},{4,0},{5,1},{6,2},{7,3},{8,12},{9,13},{10,... | collective-permute-start | bytes 2064392 | tf_op jit(solution)/shard_map/ppermute | solution.py:51
  97.7 14.6 %collective-permute-start.21 = (bf16[192,1792]{1,0:T(8,128)(2,1)S(1)}, bf16[192,1792]{1,0:T(8,128)(2,1)}, u32[]{:S(2)}, u32[]{:S(2)}) collective-permute-start(bf16[192,1792]{1,0:T(8,128)(2,1)S(1)} %pad_maximum_fusion.21), channel_id=1, source_target_pairs={{0,8},{1,9},{2,10},{3,11},{4,12},{5,13},{6,14},{7,15},{8,0},{9,1},... | collective-permute-start | bytes 2064392 | tf_op jit(solution)/shard_map/ppermute | solution.py:51
  100.2 27.8 %collective-permute-start.22 = (bf16[192,1792]{1,0:T(8,128)(2,1)}, bf16[192,1792]{1,0:T(8,128)(2,1)}, u32[]{:S(2)}, u32[]{:S(2)}) collective-permute-start(bf16[192,1792]{1,0:T(8,128)(2,1)} %pad_maximum_fusion.22), channel_id=1, source_target_pairs={{0,12},{1,13},{2,14},{3,15},{4,8},{5,9},{6,10},{7,11},{8,4},{9,5},... | collective-permute-start | bytes 2064392 | tf_op jit(solution)/shard_map/ppermute | solution.py:51
  137.6 14.2 %collective-permute-start.23 = (bf16[48,2048]{1,0:T(8,128)(2,1)S(1)}, bf16[48,2048]{1,0:T(8,128)(2,1)S(1)}, u32[]{:S(2)}, u32[]{:S(2)}) collective-permute-start(bf16[48,2048]{1,0:T(8,128)(2,1)S(1)} %get-tuple-element.96), channel_id=1, source_target_pairs={{0,1},{1,0},{2,3},{3,2},{4,5},{5,4},{6,7},{7,6},{8,9},{9,8},{10,11... | collective-permute-start | bytes 589832 | tf_op jit(solution)/shard_map/ppermute | solution.py:51
  159.1 16.7 %collective-permute-start.29 = (bf16[48,2048]{1,0:T(8,128)(2,1)S(1)}, bf16[48,2048]{1,0:T(8,128)(2,1)S(1)}, u32[]{:S(2)}, u32[]{:S(2)}) collective-permute-start(bf16[48,2048]{1,0:T(8,128)(2,1)S(1)} %fusion.126), channel_id=1, source_target_pairs={{0,19},{1,18},{2,17},{3,16},{4,23},{5,22},{6,21},{7,20},{8,27},{9,... | collective-permute-start | bytes 589832 | tf_op jit(solution)/shard_map/ppermute | solution.py:51
  223.4 13.9 %collective-permute-start.40 = (bf16[48,2048]{1,0:T(8,128)(2,1)S(1)}, bf16[48,2048]{1,0:T(8,128)(2,1)S(1)}, u32[]{:S(2)}, u32[]{:S(2)}) collective-permute-start(bf16[48,2048]{1,0:T(8,128)(2,1)S(1)} %get-tuple-element.90), channel_id=1, source_target_pairs={{16,2},{17,3},{18,0},{19,1},{20,6},{21,7},{22,4},{23,5},{24,10},{2... | collective-permute-start | bytes 589832 | tf_op jit(solution)/shard_map/ppermute | solution.py:51
  243.1 14.5 %collective-permute-start.42 = (bf16[48,2048]{1,0:T(8,128)(2,1)S(1)}, bf16[48,2048]{1,0:T(8,128)(2,1)S(1)}, u32[]{:S(2)}, u32[]{:S(2)}) collective-permute-start(bf16[48,2048]{1,0:T(8,128)(2,1)S(1)} %fusion.123), channel_id=1, source_target_pairs={{0,1},{1,0},{2,3},{3,2},{4,5},{5,4},{6,7},{7,6},{8,9},{9,8},{10,11... | collective-permute-start | bytes 589832 | tf_op jit(solution)/shard_map/ppermute | solution.py:51
  267.6 13.1 %collective-permute-start.46 = (bf16[192,1280]{1,0:T(8,128)(2,1)S(1)}, bf16[192,1280]{1,0:T(8,128)(2,1)S(1)}, u32[]{:S(2)}, u32[]{:S(2)}) collective-permute-start(bf16[192,1280]{1,0:T(8,128)(2,1)S(1)} %fusion.54), channel_id=1, source_target_pairs={{0,8},{1,9},{2,10},{3,11},{4,12},{5,13},{6,14},{7,15},{8,0},{9,1},... | collective-permute-start | bytes 1474568 | tf_op jit(solution)/shard_map/ppermute | solution.py:51
  270.7 30.3 %collective-permute-start.55 = (bf16[128,1280]{1,0:T(8,128)(2,1)S(1)}, bf16[128,1280]{1,0:T(8,128)(2,1)S(1)}, u32[]{:S(2)}, u32[]{:S(2)}) collective-permute-start(bf16[128,1280]{1,0:T(8,128)(2,1)S(1)} %get-tuple-element.74), channel_id=1, source_target_pairs={{0,2},{1,3},{2,0},{3,1},{4,6},{5,7},{6,4},{7,5},{8,10},{9,11},{10,... | collective-permute-start | bytes 983048 | tf_op jit(solution)/shard_map/ppermute | solution.py:51
  275.5 25.4 %collective-permute-start.54 = (bf16[128,1280]{1,0:T(8,128)(2,1)S(1)}, bf16[128,1280]{1,0:T(8,128)(2,1)S(1)}, u32[]{:S(2)}, u32[]{:S(2)}) collective-permute-start(bf16[128,1280]{1,0:T(8,128)(2,1)S(1)} %get-tuple-element.75), channel_id=1, source_target_pairs={{0,1},{1,0},{2,3},{3,2},{4,5},{5,4},{6,7},{7,6},{8,9},{9,8},{10,11... | collective-permute-start | bytes 983048 | tf_op jit(solution)/shard_map/ppermute | solution.py:51
  282.0 19.2 %collective-permute-start.50 = (bf16[128,1280]{1,0:T(8,128)(2,1)S(1)}, bf16[128,1280]{1,0:T(8,128)(2,1)S(1)}, u32[]{:S(2)}, u32[]{:S(2)}) collective-permute-start(bf16[128,1280]{1,0:T(8,128)(2,1)S(1)} %get-tuple-element.65), channel_id=1, source_target_pairs={{0,3},{1,2},{2,1},{3,0},{4,7},{5,6},{6,5},{7,4},{8,11},{9,10},{10,... | collective-permute-start | bytes 983048 | tf_op jit(solution)/shard_map/ppermute | solution.py:51
  282.1 25.7 %collective-permute-start.49 = (bf16[128,1280]{1,0:T(8,128)(2,1)S(1)}, bf16[128,1280]{1,0:T(8,128)(2,1)S(1)}, u32[]{:S(2)}, u32[]{:S(2)}) collective-permute-start(bf16[128,1280]{1,0:T(8,128)(2,1)S(1)} %get-tuple-element.66), channel_id=1, source_target_pairs={{0,2},{1,3},{2,0},{3,1},{4,6},{5,7},{6,4},{7,5},{8,10},{9,11},{10,... | collective-permute-start | bytes 983048 | tf_op jit(solution)/shard_map/ppermute | solution.py:51
  283.1 24.7 %collective-permute-start.48 = (bf16[128,1280]{1,0:T(8,128)(2,1)S(1)}, bf16[128,1280]{1,0:T(8,128)(2,1)S(1)}, u32[]{:S(2)}, u32[]{:S(2)}) collective-permute-start(bf16[128,1280]{1,0:T(8,128)(2,1)S(1)} %get-tuple-element.67), channel_id=1, source_target_pairs={{0,1},{1,0},{2,3},{3,2},{4,5},{5,4},{6,7},{7,6},{8,9},{9,8},{10,11... | collective-permute-start | bytes 983048 | tf_op jit(solution)/shard_map/ppermute | solution.py:51
  (66 other events, 499.4 us)

commit v8 on v7

--- a/solution.py
+++ b/solution.py
@@ -151,7 +151,7 @@
         out_specs=[native, native, pl.BlockSpec((1, 1), lambda i: (0, 0))],
         out_shape=[jax.ShapeDtypeStruct(resid.shape, jnp.float32)] * 2
         + [jax.ShapeDtypeStruct((1, 1), jnp.float32)],
-        compiler_params=pltpu.CompilerParams(vmem_limit_bytes=58 * 1024 * 1024),
+        compiler_params=pltpu.CompilerParams(vmem_limit_bytes=40 * 1024 * 1024),
         cost_estimate=pl.CostEstimate(
             flops=4 * resid.size, bytes_accessed=20 * resid.size, transcendentals=0
         ),

time: 341 us -> 338 us (level)
  transfers between devices with their start and end apart: 64 -> 64, of which waited for: 31 -> 32; matrix products, arithmetic and copies ran while one was open for 12% -> 12% of each run, Pallas kernels for 0% -> 0%
where the time goes in v8:
time: 338 us; the launch traced here: 337 us
  starting transfers between devices  135 us (40%)
  waiting for transfers between devices  110 us (33%)
  matrix products  45 us (13%)
  local copies, waits for them, and re-layouts  23.3 us (7%)
  other arithmetic  11.8 us (3%)
  Pallas kernels  8.92 us (3%)
    ppermute x57, starting transfers between devices, send(): return lax.ppermute(value, ALL, pairs)  127 us
    ppermute x57, waiting for transfers between devices, send(): return lax.ppermute(value, ALL, pairs)  104 us
    dot_general x5, matrix products, across_hidden(): lax.dot_general(left_side, right_side, (((1,), (1,)), ((), ())), preferre...  27.1 us
    dot_general x4, matrix products, dot(): return jnp.dot(left_side, right_side, preferred_element_type=jnp.float32)  15.4 us
    transpose x2, local copies, waits for them, and re-layouts, apart(): jnp.transpose(array, (1, 0, 2))  10.7 us
    pallas_call x1, Pallas kernels, update(): pl.pallas_call(update_kernel, grid=(total // columns,), in_specs=[pl.Bloc...  8.92 us
    ppermute x7, starting transfers between devices, sum_everywhere(): parts.append(lax.ppermute(value, axis, [(i, i ^ k) for i in range(count)]))  8.08 us
  transfers between devices with their start and end apart: 64, of which 32 were waited for; matrix products, arithmetic and copies ran while one was open for 12% of the time, Pallas kernels for 0%

profile of v8, /device:TPU:0, one launch (start us, length us, event | category | flops | bytes accessed | tf_op | source)
XLA Modules:
  0.0 336.8 jit_solution(373387335768938003)
XLA Ops:
  0.6 7.0 %collective-permute-start.2 = (bf16[48,2048]{1,0:T(8,128)(2,1)}, bf16[48,2048]{1,0:T(8,128)(2,1)S(1)}, u32[]{:S(2)}, u32[]{:S(2)}) collective-permute-start(bf16[48,2048]{1,0:T(8,128)(2,1)} %bitcast.193), channel_id=1, source_target_pairs={{0,3},{1,2},{2,1},{3,0},{4,7},{5,6},{6,5},{7,4},{8,11},{9,10},{10,... | collective-permute-start | bytes 589832 | tf_op jit(solution)/shard_map/ppermute | solution.py:51
  49.5 4.3 %collective-permute-start.10 = (bf16[192,1792]{1,0:T(8,128)(2,1)S(1)}, bf16[192,1792]{1,0:T(8,128)(2,1)S(1)}, u32[]{:S(2)}, u32[]{:S(2)}) collective-permute-start(bf16[192,1792]{1,0:T(8,128)(2,1)S(1)} %get-tuple-element.120), channel_id=1, source_target_pairs={{0,12},{1,13},{2,14},{3,15},{4,8},{5,9},{6,10},{7,11},{8,4},{9,5},... | collective-permute-start | bytes 2064392 | tf_op jit(solution)/shard_map/ppermute | solution.py:51
  60.4 5.0 %collective-permute-start.15 = (bf16[2,128,1280]{2,1,0:T(8,128)(2,1)S(1)}, bf16[2,128,1280]{2,1,0:T(8,128)(2,1)S(1)}, u32[]{:S(2)}, u32[]{:S(2)}) collective-permute-start(bf16[2,128,1280]{2,1,0:T(8,128)(2,1)S(1)} %pad_maximum_fusion.25), channel_id=1, source_target_pairs={{0,3},{1,2},{2,1},{3,0},{4,7},{5,6},{6,5},{7,4},{8,11},{9,10},{10,... | collective-permute-start | bytes 1966088 | tf_op jit(solution)/shard_map/ppermute | solution.py:51
  65.5 5.1 %collective-permute-done.9 = bf16[192,1792]{1,0:T(8,128)(2,1)S(1)} collective-permute-done((bf16[192,1792]{1,0:T(8,128)(2,1)S(1)}, bf16[192,1792]{1,0:T(8,128)(2,1)S(1)}, u32[]{:S(2)}, u32[]{:S(2)}) %collective-permute-start.9) | collective-permute-done | bytes 688160 | tf_op jit(solution)/shard_map/ppermute | solution.py:51
  81.3 4.6 %multiply_convert_fusion.1 = (bf16[192,1280]{1,0:T(8,128)(2,1)S(1)}, f32[192,1280]{1,0:T(8,128)}) fusion(bf16[192,2048]{1,0:T(8,128)(2,1)S(1)} %fusion.78, bf16[1,1,2,2048,1280]{4,3,2,1,0:T(8,128)(2,1)} %param.6), kind=kOutput, calls=%fused_computation.108 | convolution fusion | flops 1008844800 | bytes 7503872 | tf_op jit(solution)/shard_map/dot_general | solution.py:36
  100.6 6.5 %copy.9 = f32[2,128,5120]{2,1,0:T(8,128)} copy(f32[2,128,5120]{2,0,1:T(2,128)} %bitcast.185) | data formatting | bytes 10485760 | tf_op jit(solution)/shard_map/transpose | solution.py:162
  112.3 15.7 %collective-permute-done.22 = bf16[192,1792]{1,0:T(8,128)(2,1)} collective-permute-done((bf16[192,1792]{1,0:T(8,128)(2,1)}, bf16[192,1792]{1,0:T(8,128)(2,1)}, u32[]{:S(2)}, u32[]{:S(2)}) %collective-permute-start.22) | collective-permute-done | bytes 688160 | tf_op jit(solution)/shard_map/ppermute | solution.py:51
  132.1 5.5 %fusion.156 = (bf16[192,2048]{1,0:T(8,128)(2,1)S(1)}, f32[192,2048]{1,0:T(8,128)S(1)}) fusion(bf16[192,512]{1,0:T(8,128)(2,1)S(1)} %get-tuple-element.100, bf16[192,512]{1,0:T(8,128)(2,1)S(1)} %get-tuple-element.101, bf16[192,512]{1,0:T(8,128)(2,1)S(1)} %get-tuple-element.102, bf16[192,512]{1,0:T(8,128)(2,1)S(1)} %get-tuple-element.99, ...), kind=kOutput, calls=%fused_computation.272 | convolution fusion | flops 1016463360 | bytes 11829248 | tf_op jit(solution)/shard_map/dot_general | solution.py:24
  137.6 7.7 %collective-permute-start.23 = (bf16[48,2048]{1,0:T(8,128)(2,1)S(1)}, bf16[48,2048]{1,0:T(8,128)(2,1)S(1)}, u32[]{:S(2)}, u32[]{:S(2)}) collective-permute-start(bf16[48,2048]{1,0:T(8,128)(2,1)S(1)} %get-tuple-element.96), channel_id=1, source_target_pairs={{0,1},{1,0},{2,3},{3,2},{4,5},{5,4},{6,7},{7,6},{8,9},{9,8},{10,11... | collective-permute-start | bytes 589832 | tf_op jit(solution)/shard_map/ppermute | solution.py:51
  145.3 4.6 %collective-permute-start.25 = (bf16[48,2048]{1,0:T(8,128)(2,1)S(1)}, bf16[48,2048]{1,0:T(8,128)(2,1)S(1)}, u32[]{:S(2)}, u32[]{:S(2)}) collective-permute-start(bf16[48,2048]{1,0:T(8,128)(2,1)S(1)} %get-tuple-element.97), channel_id=1, source_target_pairs={{0,3},{1,2},{2,1},{3,0},{4,7},{5,6},{6,5},{7,4},{8,11},{9,10},{10,... | collective-permute-start | bytes 589832 | tf_op jit(solution)/shard_map/ppermute | solution.py:51
  159.1 12.8 %collective-permute-start.29 = (bf16[48,2048]{1,0:T(8,128)(2,1)S(1)}, bf16[48,2048]{1,0:T(8,128)(2,1)S(1)}, u32[]{:S(2)}, u32[]{:S(2)}) collective-permute-start(bf16[48,2048]{1,0:T(8,128)(2,1)S(1)} %fusion.126), channel_id=1, source_target_pairs={{0,19},{1,18},{2,17},{3,16},{4,23},{5,22},{6,21},{7,20},{8,27},{9,... | collective-permute-start | bytes 589832 | tf_op jit(solution)/shard_map/ppermute | solution.py:51
  180.1 8.8 %fusion.51 = bf16[192,2048]{1,0:T(8,128)(2,1)S(1)} fusion(bf16[1,1,2,2048,1280]{4,3,2,1,0:T(8,128)(2,1)} %param.6, bf16[192,2048]{1,0:T(8,128)(2,1)S(1)} %get-tuple-element.42, f32[192]{0:T(256)S(1)} %multiply_multiply_fusion.3, f32[192]{0:T(256)S(1)} %fusion.132, bf16[48,2048]{1,0:T(8,128)(2,1)} %copy-done.15, bf16[48,2048]{1,0:T(8,128)(2,1)} %copy-done.16, ...), kind=kOutput, calls=%fused_computation.53 | convolution fusion | flops 2028453888 | bytes 17073664 | tf_op jit(solution)/shard_map/dot_general | solution.py:24
  194.2 5.1 %collective-permute-done.33 = bf16[48,2048]{1,0:T(8,128)(2,1)S(1)} collective-permute-done((bf16[48,2048]{1,0:T(8,128)(2,1)S(1)}, bf16[48,2048]{1,0:T(8,128)(2,1)S(1)}, u32[]{:S(2)}, u32[]{:S(2)}) %collective-permute-start.33) | collective-permute-done | bytes 196640 | tf_op jit(solution)/shard_map/ppermute | solution.py:51
  199.3 5.2 %collective-permute-done.32 = bf16[48,2048]{1,0:T(8,128)(2,1)S(1)} collective-permute-done((bf16[48,2048]{1,0:T(8,128)(2,1)S(1)}, bf16[48,2048]{1,0:T(8,128)(2,1)S(1)}, u32[]{:S(2)}, u32[]{:S(2)}) %collective-permute-start.32) | collective-permute-done | bytes 196640 | tf_op jit(solution)/shard_map/ppermute | solution.py:51
  213.4 7.4 %fusion.48 = bf16[192,2048]{1,0:T(8,128)(2,1)S(1)} fusion(bf16[1,1,2,2048,1280]{4,3,2,1,0:T(8,128)(2,1)} %param.6, bf16[48,2048]{1,0:T(8,128)(2,1)S(1)} %collective-permute-done.37, bf16[48,2048]{1,0:T(8,128)(2,1)S(1)} %collective-permute-done.36, bf16[48,2048]{1,0:T(8,128)(2,1)S(1)} %collective-permute-done.35, ...), kind=kOutput, calls=%fused_computation.52 | convolution fusion | flops 2021621760 | bytes 13041665 | tf_op jit(solution)/shard_map/dot_general | solution.py:24
  226.1 5.7 %collective-permute-done.41 = bf16[48,2048]{1,0:T(8,128)(2,1)S(1)} collective-permute-done((bf16[48,2048]{1,0:T(8,128)(2,1)S(1)}, bf16[48,2048]{1,0:T(8,128)(2,1)S(1)}, u32[]{:S(2)}, u32[]{:S(2)}) %collective-permute-start.41) | collective-permute-done | bytes 196640 | tf_op jit(solution)/shard_map/ppermute | solution.py:51
  231.7 5.7 %collective-permute-done.40 = bf16[48,2048]{1,0:T(8,128)(2,1)S(1)} collective-permute-done((bf16[48,2048]{1,0:T(8,128)(2,1)S(1)}, bf16[48,2048]{1,0:T(8,128)(2,1)S(1)}, u32[]{:S(2)}, u32[]{:S(2)}) %collective-permute-start.40) | collective-permute-done | bytes 196640 | tf_op jit(solution)/shard_map/ppermute | solution.py:51
  243.2 5.0 %collective-permute-start.42 = (bf16[48,2048]{1,0:T(8,128)(2,1)S(1)}, bf16[48,2048]{1,0:T(8,128)(2,1)S(1)}, u32[]{:S(2)}, u32[]{:S(2)}) collective-permute-start(bf16[48,2048]{1,0:T(8,128)(2,1)S(1)} %fusion.123), channel_id=1, source_target_pairs={{0,1},{1,0},{2,3},{3,2},{4,5},{5,4},{6,7},{7,6},{8,9},{9,8},{10,11... | collective-permute-start | bytes 589832 | tf_op jit(solution)/shard_map/ppermute | solution.py:51
  252.0 5.7 %collective-permute-done.42 = bf16[48,2048]{1,0:T(8,128)(2,1)S(1)} collective-permute-done((bf16[48,2048]{1,0:T(8,128)(2,1)S(1)}, bf16[48,2048]{1,0:T(8,128)(2,1)S(1)}, u32[]{:S(2)}, u32[]{:S(2)}) %collective-permute-start.42) | collective-permute-done | bytes 196640 | tf_op jit(solution)/shard_map/ppermute | solution.py:51
  275.6 5.2 %collective-permute-done.46 = bf16[192,1280]{1,0:T(8,128)(2,1)S(1)} collective-permute-done((bf16[192,1280]{1,0:T(8,128)(2,1)S(1)}, bf16[192,1280]{1,0:T(8,128)(2,1)S(1)}, u32[]{:S(2)}, u32[]{:S(2)}) %collective-permute-start.46) | collective-permute-done | bytes 491552 | tf_op jit(solution)/shard_map/ppermute | solution.py:51
  283.2 9.1 %collective-permute-start.48 = (bf16[128,1280]{1,0:T(8,128)(2,1)S(1)}, bf16[128,1280]{1,0:T(8,128)(2,1)S(1)}, u32[]{:S(2)}, u32[]{:S(2)}) collective-permute-start(bf16[128,1280]{1,0:T(8,128)(2,1)S(1)} %get-tuple-element.67), channel_id=1, source_target_pairs={{0,1},{1,0},{2,3},{3,2},{4,5},{5,4},{6,7},{7,6},{8,9},{9,8},{10,11... | collective-permute-start | bytes 983048 | tf_op jit(solution)/shard_map/ppermute | solution.py:51
  292.3 8.6 %collective-permute-done.55 = bf16[128,1280]{1,0:T(8,128)(2,1)S(1)} collective-permute-done((bf16[128,1280]{1,0:T(8,128)(2,1)S(1)}, bf16[128,1280]{1,0:T(8,128)(2,1)S(1)}, u32[]{:S(2)}, u32[]{:S(2)}) %collective-permute-start.55) | collective-permute-done | bytes 327712 | tf_op jit(solution)/shard_map/ppermute | solution.py:51
  301.2 6.7 %collective-permute-done.49 = bf16[128,1280]{1,0:T(8,128)(2,1)S(1)} collective-permute-done((bf16[128,1280]{1,0:T(8,128)(2,1)S(1)}, bf16[128,1280]{1,0:T(8,128)(2,1)S(1)}, u32[]{:S(2)}, u32[]{:S(2)}) %collective-permute-start.49) | collective-permute-done | bytes 327712 | tf_op jit(solution)/shard_map/ppermute | solution.py:51
  327.9 8.9 %shard_map.76 = (f32[128,2,5120]{2,1,0:T(2,128)}, f32[128,2,5120]{2,1,0:T(2,128)}, f32[1,1]{1,0:T(1,128)}) custom-call(f32[4,1280]{1,0:T(4,128)S(1)} %add_add_fusion.1.sums_ref, bf16[128,5120]{1,0:T(8,128)(2,1)S(1)} %pad_maximum_fusion.4.in_ref, bf16[128,5120]{1,0:T(8,128)(2,1)S(1)} %pad_maximum_fusion.6.out_ref, f32[128,2,5120]{2,1,0:T(2,128)S(1)} %bitcast.188, ...), custom_call_target="tpu_custom_call" | custom-call | flops 5242880 | bytes 26214400 | tf_op jit(solution)/shard_map/pallas_call | solution.py:147
  (262 shorter events, 169.1 us)
Async XLA Ops:
  0.6 25.5 %collective-permute-start.2 = (bf16[48,2048]{1,0:T(8,128)(2,1)}, bf16[48,2048]{1,0:T(8,128)(2,1)S(1)}, u32[]{:S(2)}, u32[]{:S(2)}) collective-permute-start(bf16[48,2048]{1,0:T(8,128)(2,1)} %bitcast.193), channel_id=1, source_target_pairs={{0,3},{1,2},{2,1},{3,0},{4,7},{5,6},{6,5},{7,4},{8,11},{9,10},{10,... | collective-permute-start | bytes 589832 | tf_op jit(solution)/shard_map/ppermute | solution.py:51
  7.6 18.6 %collective-permute-start.1 = (bf16[48,2048]{1,0:T(8,128)(2,1)}, bf16[48,2048]{1,0:T(8,128)(2,1)S(1)}, u32[]{:S(2)}, u32[]{:S(2)}) collective-permute-start(bf16[48,2048]{1,0:T(8,128)(2,1)} %bitcast.194), channel_id=1, source_target_pairs={{0,2},{1,3},{2,0},{3,1},{4,6},{5,7},{6,4},{7,5},{8,10},{9,11},{10,... | collective-permute-start | bytes 589832 | tf_op jit(solution)/shard_map/ppermute | solution.py:51
  9.5 18.9 %collective-permute-start = (bf16[48,2048]{1,0:T(8,128)(2,1)}, bf16[48,2048]{1,0:T(8,128)(2,1)S(1)}, u32[]{:S(2)}, u32[]{:S(2)}) collective-permute-start(bf16[48,2048]{1,0:T(8,128)(2,1)} %bitcast.195), channel_id=1, source_target_pairs={{0,1},{1,0},{2,3},{3,2},{4,5},{5,4},{6,7},{7,6},{8,9},{9,8},{10,11... | collective-permute-start | bytes 589832 | tf_op jit(solution)/shard_map/ppermute | solution.py:51
  20.9 39.5 %collective-permute-start.6 = (bf16[2,128,1280]{2,1,0:T(8,128)(2,1)}, bf16[2,128,1280]{2,1,0:T(8,128)(2,1)S(1)}, u32[]{:S(2)}, u32[]{:S(2)}) collective-permute-start(bf16[2,128,1280]{2,1,0:T(8,128)(2,1)} %pad_maximum_fusion.23), channel_id=1, source_target_pairs={{0,1},{1,0},{2,3},{3,2},{4,5},{5,4},{6,7},{7,6},{8,9},{9,8},{10,11... | collective-permute-start | bytes 1966088 | tf_op jit(solution)/shard_map/ppermute | solution.py:51
  23.3 42.2 %collective-permute-start.7 = (bf16[2,128,1280]{2,1,0:T(8,128)(2,1)}, bf16[2,128,1280]{2,1,0:T(8,128)(2,1)}, u32[]{:S(2)}, u32[]{:S(2)}) collective-permute-start(bf16[2,128,1280]{2,1,0:T(8,128)(2,1)} %pad_maximum_fusion.24), channel_id=1, source_target_pairs={{0,2},{1,3},{2,0},{3,1},{4,6},{5,7},{6,4},{7,5},{8,10},{9,11},{10,... | collective-permute-start | bytes 1966088 | tf_op jit(solution)/shard_map/ppermute | solution.py:51
  39.0 14.9 %collective-permute-start.5 = (bf16[48,2048]{1,0:T(8,128)(2,1)S(1)}, bf16[48,2048]{1,0:T(8,128)(2,1)S(1)}, u32[]{:S(2)}, u32[]{:S(2)}) collective-permute-start(bf16[48,2048]{1,0:T(8,128)(2,1)S(1)} %get-tuple-element.115), channel_id=1, source_target_pairs={{0,3},{1,2},{2,1},{3,0},{4,7},{5,6},{6,5},{7,4},{8,11},{9,10},{10,... | collective-permute-start | bytes 589832 | tf_op jit(solution)/shard_map/ppermute | solution.py:51
  43.0 13.9 %collective-permute-start.4 = (bf16[48,2048]{1,0:T(8,128)(2,1)S(1)}, bf16[48,2048]{1,0:T(8,128)(2,1)S(1)}, u32[]{:S(2)}, u32[]{:S(2)}) collective-permute-start(bf16[48,2048]{1,0:T(8,128)(2,1)S(1)} %get-tuple-element.116), channel_id=1, source_target_pairs={{0,2},{1,3},{2,0},{3,1},{4,6},{5,7},{6,4},{7,5},{8,10},{9,11},{10,... | collective-permute-start | bytes 589832 | tf_op jit(solution)/shard_map/ppermute | solution.py:51
  49.5 16.0 %collective-permute-start.10 = (bf16[192,1792]{1,0:T(8,128)(2,1)S(1)}, bf16[192,1792]{1,0:T(8,128)(2,1)S(1)}, u32[]{:S(2)}, u32[]{:S(2)}) collective-permute-start(bf16[192,1792]{1,0:T(8,128)(2,1)S(1)} %get-tuple-element.120), channel_id=1, source_target_pairs={{0,12},{1,13},{2,14},{3,15},{4,8},{5,9},{6,10},{7,11},{8,4},{9,5},... | collective-permute-start | bytes 2064392 | tf_op jit(solution)/shard_map/ppermute | solution.py:51
  53.9 16.7 %collective-permute-start.9 = (bf16[192,1792]{1,0:T(8,128)(2,1)S(1)}, bf16[192,1792]{1,0:T(8,128)(2,1)S(1)}, u32[]{:S(2)}, u32[]{:S(2)}) collective-permute-start(bf16[192,1792]{1,0:T(8,128)(2,1)S(1)} %get-tuple-element.121), channel_id=1, source_target_pairs={{0,8},{1,9},{2,10},{3,11},{4,12},{5,13},{6,14},{7,15},{8,0},{9,1},... | collective-permute-start | bytes 2064392 | tf_op jit(solution)/shard_map/ppermute | solution.py:51
  56.9 13.8 %collective-permute-start.8 = (bf16[192,1792]{1,0:T(8,128)(2,1)S(1)}, bf16[192,1792]{1,0:T(8,128)(2,1)S(1)}, u32[]{:S(2)}, u32[]{:S(2)}) collective-permute-start(bf16[192,1792]{1,0:T(8,128)(2,1)S(1)} %get-tuple-element.122), channel_id=1, source_target_pairs={{0,4},{1,5},{2,6},{3,7},{4,0},{5,1},{6,2},{7,3},{8,12},{9,13},{10,... | collective-permute-start | bytes 2064392 | tf_op jit(solution)/shard_map/ppermute | solution.py:51
  60.4 19.5 %collective-permute-start.15 = (bf16[2,128,1280]{2,1,0:T(8,128)(2,1)S(1)}, bf16[2,128,1280]{2,1,0:T(8,128)(2,1)S(1)}, u32[]{:S(2)}, u32[]{:S(2)}) collective-permute-start(bf16[2,128,1280]{2,1,0:T(8,128)(2,1)S(1)} %pad_maximum_fusion.25), channel_id=1, source_target_pairs={{0,3},{1,2},{2,1},{3,0},{4,7},{5,6},{6,5},{7,4},{8,11},{9,10},{10,... | collective-permute-start | bytes 1966088 | tf_op jit(solution)/shard_map/ppermute | solution.py:51
  96.1 15.9 %collective-permute-start.20 = (bf16[192,1792]{1,0:T(8,128)(2,1)S(1)}, bf16[192,1792]{1,0:T(8,128)(2,1)}, u32[]{:S(2)}, u32[]{:S(2)}) collective-permute-start(bf16[192,1792]{1,0:T(8,128)(2,1)S(1)} %pad_maximum_fusion.20), channel_id=1, source_target_pairs={{0,4},{1,5},{2,6},{3,7},{4,0},{5,1},{6,2},{7,3},{8,12},{9,13},{10,... | collective-permute-start | bytes 2064392 | tf_op jit(solution)/shard_map/ppermute | solution.py:51
  97.7 14.6 %collective-permute-start.21 = (bf16[192,1792]{1,0:T(8,128)(2,1)S(1)}, bf16[192,1792]{1,0:T(8,128)(2,1)}, u32[]{:S(2)}, u32[]{:S(2)}) collective-permute-start(bf16[192,1792]{1,0:T(8,128)(2,1)S(1)} %pad_maximum_fusion.21), channel_id=1, source_target_pairs={{0,8},{1,9},{2,10},{3,11},{4,12},{5,13},{6,14},{7,15},{8,0},{9,1},... | collective-permute-start | bytes 2064392 | tf_op jit(solution)/shard_map/ppermute | solution.py:51
  100.2 27.9 %collective-permute-start.22 = (bf16[192,1792]{1,0:T(8,128)(2,1)}, bf16[192,1792]{1,0:T(8,128)(2,1)}, u32[]{:S(2)}, u32[]{:S(2)}) collective-permute-start(bf16[192,1792]{1,0:T(8,128)(2,1)} %pad_maximum_fusion.22), channel_id=1, source_target_pairs={{0,12},{1,13},{2,14},{3,15},{4,8},{5,9},{6,10},{7,11},{8,4},{9,5},... | collective-permute-start | bytes 2064392 | tf_op jit(solution)/shard_map/ppermute | solution.py:51
  137.6 14.2 %collective-permute-start.23 = (bf16[48,2048]{1,0:T(8,128)(2,1)S(1)}, bf16[48,2048]{1,0:T(8,128)(2,1)S(1)}, u32[]{:S(2)}, u32[]{:S(2)}) collective-permute-start(bf16[48,2048]{1,0:T(8,128)(2,1)S(1)} %get-tuple-element.96), channel_id=1, source_target_pairs={{0,1},{1,0},{2,3},{3,2},{4,5},{5,4},{6,7},{7,6},{8,9},{9,8},{10,11... | collective-permute-start | bytes 589832 | tf_op jit(solution)/shard_map/ppermute | solution.py:51
  159.1 16.8 %collective-permute-start.29 = (bf16[48,2048]{1,0:T(8,128)(2,1)S(1)}, bf16[48,2048]{1,0:T(8,128)(2,1)S(1)}, u32[]{:S(2)}, u32[]{:S(2)}) collective-permute-start(bf16[48,2048]{1,0:T(8,128)(2,1)S(1)} %fusion.126), channel_id=1, source_target_pairs={{0,19},{1,18},{2,17},{3,16},{4,23},{5,22},{6,21},{7,20},{8,27},{9,... | collective-permute-start | bytes 589832 | tf_op jit(solution)/shard_map/ppermute | solution.py:51
  223.5 13.9 %collective-permute-start.40 = (bf16[48,2048]{1,0:T(8,128)(2,1)S(1)}, bf16[48,2048]{1,0:T(8,128)(2,1)S(1)}, u32[]{:S(2)}, u32[]{:S(2)}) collective-permute-start(bf16[48,2048]{1,0:T(8,128)(2,1)S(1)} %get-tuple-element.90), channel_id=1, source_target_pairs={{16,2},{17,3},{18,0},{19,1},{20,6},{21,7},{22,4},{23,5},{24,10},{2... | collective-permute-start | bytes 589832 | tf_op jit(solution)/shard_map/ppermute | solution.py:51
  243.2 14.5 %collective-permute-start.42 = (bf16[48,2048]{1,0:T(8,128)(2,1)S(1)}, bf16[48,2048]{1,0:T(8,128)(2,1)S(1)}, u32[]{:S(2)}, u32[]{:S(2)}) collective-permute-start(bf16[48,2048]{1,0:T(8,128)(2,1)S(1)} %fusion.123), channel_id=1, source_target_pairs={{0,1},{1,0},{2,3},{3,2},{4,5},{5,4},{6,7},{7,6},{8,9},{9,8},{10,11... | collective-permute-start | bytes 589832 | tf_op jit(solution)/shard_map/ppermute | solution.py:51
  267.4 13.3 %collective-permute-start.46 = (bf16[192,1280]{1,0:T(8,128)(2,1)S(1)}, bf16[192,1280]{1,0:T(8,128)(2,1)S(1)}, u32[]{:S(2)}, u32[]{:S(2)}) collective-permute-start(bf16[192,1280]{1,0:T(8,128)(2,1)S(1)} %fusion.54), channel_id=1, source_target_pairs={{0,8},{1,9},{2,10},{3,11},{4,12},{5,13},{6,14},{7,15},{8,0},{9,1},... | collective-permute-start | bytes 1474568 | tf_op jit(solution)/shard_map/ppermute | solution.py:51
  270.7 30.2 %collective-permute-start.55 = (bf16[128,1280]{1,0:T(8,128)(2,1)S(1)}, bf16[128,1280]{1,0:T(8,128)(2,1)S(1)}, u32[]{:S(2)}, u32[]{:S(2)}) collective-permute-start(bf16[128,1280]{1,0:T(8,128)(2,1)S(1)} %get-tuple-element.74), channel_id=1, source_target_pairs={{0,2},{1,3},{2,0},{3,1},{4,6},{5,7},{6,4},{7,5},{8,10},{9,11},{10,... | collective-permute-start | bytes 983048 | tf_op jit(solution)/shard_map/ppermute | solution.py:51
  275.6 25.3 %collective-permute-start.54 = (bf16[128,1280]{1,0:T(8,128)(2,1)S(1)}, bf16[128,1280]{1,0:T(8,128)(2,1)S(1)}, u32[]{:S(2)}, u32[]{:S(2)}) collective-permute-start(bf16[128,1280]{1,0:T(8,128)(2,1)S(1)} %get-tuple-element.75), channel_id=1, source_target_pairs={{0,1},{1,0},{2,3},{3,2},{4,5},{5,4},{6,7},{7,6},{8,9},{9,8},{10,11... | collective-permute-start | bytes 983048 | tf_op jit(solution)/shard_map/ppermute | solution.py:51
  282.1 19.1 %collective-permute-start.50 = (bf16[128,1280]{1,0:T(8,128)(2,1)S(1)}, bf16[128,1280]{1,0:T(8,128)(2,1)S(1)}, u32[]{:S(2)}, u32[]{:S(2)}) collective-permute-start(bf16[128,1280]{1,0:T(8,128)(2,1)S(1)} %get-tuple-element.65), channel_id=1, source_target_pairs={{0,3},{1,2},{2,1},{3,0},{4,7},{5,6},{6,5},{7,4},{8,11},{9,10},{10,... | collective-permute-start | bytes 983048 | tf_op jit(solution)/shard_map/ppermute | solution.py:51
  282.2 25.7 %collective-permute-start.49 = (bf16[128,1280]{1,0:T(8,128)(2,1)S(1)}, bf16[128,1280]{1,0:T(8,128)(2,1)S(1)}, u32[]{:S(2)}, u32[]{:S(2)}) collective-permute-start(bf16[128,1280]{1,0:T(8,128)(2,1)S(1)} %get-tuple-element.66), channel_id=1, source_target_pairs={{0,2},{1,3},{2,0},{3,1},{4,6},{5,7},{6,4},{7,5},{8,10},{9,11},{10,... | collective-permute-start | bytes 983048 | tf_op jit(solution)/shard_map/ppermute | solution.py:51
  283.2 24.7 %collective-permute-start.48 = (bf16[128,1280]{1,0:T(8,128)(2,1)S(1)}, bf16[128,1280]{1,0:T(8,128)(2,1)S(1)}, u32[]{:S(2)}, u32[]{:S(2)}) collective-permute-start(bf16[128,1280]{1,0:T(8,128)(2,1)S(1)} %get-tuple-element.67), channel_id=1, source_target_pairs={{0,1},{1,0},{2,3},{3,2},{4,5},{5,4},{6,7},{7,6},{8,9},{9,8},{10,11... | collective-permute-start | bytes 983048 | tf_op jit(solution)/shard_map/ppermute | solution.py:51
  (70 other events, 561.4 us)
